TPU v7x, 256 devices: a whole 4x4x8 slice. The times are simulated.
256 devices in a mesh: section: 4 (over x), seq: 64 (over z, y, core).
Axes of the slice: x: 4, y: 4, z: 8, core: 2. Of those that a mesh axis runs over, the one named last changes fastest.
Arguments:
- patches: bfloat16 [2, 4096, 2048], P(None, 'seq'), may hold values from -6 to 6
- stale_cache: bfloat16 [4, 2, 4096, 4096], P('section', None, 'seq'), may hold values from -200 to 200
- block_lists: int32 [4, 16, 512, 16], P('section'), may hold values from 0 to 255, as said below
- block_counts: int32 [4, 16], P('section'), may hold values from 8 to 16, as said below
- query_gain: float32 [4, 2048], P('section'), may hold values from 1 to 3
- branch_gate: float32 [4, 2048], P('section'), may hold values from 1 to 4
Outputs:
- section_outputs: bfloat16 [4, 2, 4096, 2048], P('section', None, 'seq')
Inputs may be any that keep to these rules, and one draw needn't show every extreme that they name: `block_lists`: for each section, head and query block the 16 entries are distinct key block numbers; the first is the key block that holds the query block's own tokens. `block_counts`: all query blocks of one head in one section use the same number of list entries; in every section some head uses 16.
All inputs are finite; a program needn't handle non-finite values.
Results may differ from a plain program's by a relative error of at most 0.02.
The roundings to bfloat16 on the way count: a program that leaves them out, or rounds other values in their place, can miss the bound.
Values may be sent and summed in bfloat16 or wider, within the bound.
No kernel may reach another device: no remote copies, remote signals or barrier semaphores. Data moves between devices by JAX's collectives and lax.ppermute only.
A program may use at most 128 MiB of HBM per device.

v0:
```python
import math

import jax
import jax.numpy as jnp
from jax import lax
from jax.sharding import PartitionSpec as P

HEADS = 16
HEAD_DIM = 128
QUERY_BLOCK = 16
KEY_BLOCK = 32
SLOTS = 16


SCORE_FLOOR = -1e30


def shortened(array):
    return jax.tree.map(lambda a: a.astype(jnp.bfloat16) if a.dtype == jnp.float32 else a, array)


def passed_along(value, axis, steps):
    count = lax.axis_size(axis)
    leading, last = (max(0, -steps), min(count, count - steps))
    return lax.ppermute(value, axis, [(source, source + steps) for source in range(leading, last)])


def attend(queries, blocks, positions, count):
    n_query, q_rows, head_width = queries.shape
    slot_total = positions.shape[1]
    block_rows = blocks.shape[1]
    group_size = math.gcd(n_query, 16)
    query_groups = queries.reshape(n_query // group_size, group_size, q_rows, head_width)
    position_groups = positions.reshape(n_query // group_size, group_size, slot_total)
    slot_live = jnp.arange(slot_total * block_rows) // block_rows < count
    scale_factor = head_width ** (-0.5)
    key_table = blocks[..., :head_width]
    value_table = blocks[..., head_width:]

    def one_group(group_pair):
        query_part, position_part = group_pair
        keys_part = jnp.take(key_table, position_part, axis=0).reshape(
            group_size, slot_total * block_rows, head_width
        )
        value_part = jnp.take(value_table, position_part, axis=0).reshape(
            group_size, slot_total * block_rows, head_width
        )
        scores = (
            jnp.einsum("gqd,gkd->gqk", query_part, keys_part, preferred_element_type=jnp.float32)
            * scale_factor
        )
        scores = jnp.where(slot_live, scores, SCORE_FLOOR)
        highest = jnp.max(scores, axis=-1, keepdims=True)
        exponent = jnp.exp(scores - highest)
        weights = (exponent / jnp.sum(exponent, axis=-1, keepdims=True)).astype(jnp.bfloat16)
        summed = jnp.einsum("gqk,gkd->gqd", weights, value_part, preferred_element_type=jnp.float32)
        return summed.astype(jnp.bfloat16)

    result = lax.map(one_group, (query_groups, position_groups))
    return result.reshape(n_query, q_rows, head_width)


def block_places(listed, shard_count, patch_rows, micro_count, layout_parts):
    per_shard = patch_rows // KEY_BLOCK
    per_micro = shard_count * per_shard
    per_piece = micro_count * patch_rows // (layout_parts * KEY_BLOCK)
    micro_index = listed // per_micro
    remain = listed % per_micro
    source_shard = remain // per_shard
    local_block = micro_index * per_shard + remain % per_shard
    return (
        local_block // per_piece * shard_count + source_shard
    ) * per_piece + local_block % per_piece


def local(patches, stale_cache, block_lists, block_counts, query_gain, branch_gate):
    shard_count = lax.axis_size("seq")
    section_count = lax.axis_size("section")
    section_index = lax.axis_index("section")
    shard_index = lax.axis_index("seq")
    micro_count, patch_rows, channels = patches.shape
    query_parts = max(1, shard_count // 16)
    unit_total = HEADS * query_parts
    unit_local = unit_total // shard_count
    part_rows = patch_rows // query_parts
    local_rows = micro_count * patch_rows
    pair_width = 2 * HEAD_DIM
    by_head = (
        stale_cache[0]
        .reshape(local_rows, 2, HEADS, HEAD_DIM)
        .transpose(2, 0, 1, 3)
        .reshape(HEADS, local_rows, pair_width)
    )
    outgoing = jnp.broadcast_to(
        by_head[:, None], (HEADS, query_parts, local_rows, pair_width)
    ).reshape(unit_total, local_rows, pair_width)
    assembled = lax.all_to_all(outgoing, "seq", split_axis=0, concat_axis=1, tiled=True)
    layout_parts = 1
    key_blocks = assembled.reshape(unit_local, -1, KEY_BLOCK, pair_width)
    lists_local = block_lists[0]
    counts_local = block_counts[0]
    head_gain = query_gain[0].reshape(HEADS, HEAD_DIM)
    gate_row = branch_gate[0]
    blocks_per_part = part_rows // QUERY_BLOCK
    zero_index = jnp.zeros((), jnp.int32)
    finished = jnp.zeros_like(patches)
    received = jnp.zeros((patch_rows, channels), jnp.bfloat16)
    last_step = micro_count + section_count - 2
    for step_index in range(micro_count + section_count - 1):
        micro_now = step_index - section_index
        active = (micro_now >= 0) & (micro_now < micro_count)
        micro_safe = jnp.clip(micro_now, 0, micro_count - 1)
        fresh_rows = lax.dynamic_index_in_dim(patches, micro_safe, 0, keepdims=False)
        current = jnp.where(section_index == 0, fresh_rows, received)
        widened = current.astype(jnp.float32)
        per_head = widened.reshape(patch_rows, HEADS, HEAD_DIM)
        normed = (
            per_head
            * lax.rsqrt(jnp.mean(per_head * per_head, axis=-1, keepdims=True) + 1e-06)
            * head_gain
        )
        queries = normed.astype(jnp.bfloat16)
        outgoing_query = (
            queries.reshape(query_parts, part_rows, HEADS, HEAD_DIM)
            .transpose(2, 0, 1, 3)
            .reshape(unit_total, part_rows, HEAD_DIM)
        )
        gathered_query = lax.all_to_all(
            outgoing_query, "seq", split_axis=0, concat_axis=1, tiled=True
        )

        def run_units():
            unit_id = shard_index * unit_local + 0
            head_id = unit_id // query_parts
            part_id = unit_id % query_parts
            head_lists = lax.dynamic_index_in_dim(lists_local, head_id, 0, keepdims=False)
            shaped = head_lists.reshape(
                micro_count, shard_count, query_parts, blocks_per_part, SLOTS
            )
            chosen = lax.dynamic_slice(
                shaped,
                (micro_safe, zero_index, part_id, zero_index, zero_index),
                (1, shard_count, 1, blocks_per_part, SLOTS),
            )
            chosen = chosen.reshape(shard_count * blocks_per_part, SLOTS)
            places = block_places(chosen, shard_count, patch_rows, micro_count, layout_parts)
            head_count = lax.dynamic_index_in_dim(counts_local, head_id, 0, keepdims=False)
            unit_queries = gathered_query[0].reshape(-1, QUERY_BLOCK, HEAD_DIM)
            attended = attend(unit_queries, key_blocks[0], places, head_count)
            results = [attended.reshape(shard_count * part_rows, HEAD_DIM)]
            return jnp.stack(results)

        def skip_units():
            return jnp.zeros((unit_local, shard_count * part_rows, HEAD_DIM), jnp.bfloat16)

        unit_outputs = lax.cond(active, run_units, skip_units)
        returned = lax.all_to_all(
            shortened(unit_outputs), "seq", split_axis=1, concat_axis=0, tiled=True
        ).astype(unit_outputs.dtype)
        merged = (
            returned.reshape(HEADS, query_parts, part_rows, HEAD_DIM)
            .transpose(1, 2, 0, 3)
            .reshape(patch_rows, channels)
        )
        updated = (widened + gate_row * merged.astype(jnp.float32)).astype(jnp.bfloat16)
        stored = lax.dynamic_update_index_in_dim(finished, updated, micro_safe, 0)
        finished = jnp.where(active, stored, finished)
        if step_index < last_step:
            received = passed_along(updated, "section", 1)
    return finished[None]


def solution(mesh):
    return jax.shard_map(
        local,
        mesh=mesh,
        in_specs=(
            P(None, "seq", None),
            P("section", None, "seq", None),
            P("section", None, None, None),
            P("section", None),
            P("section", None),
            P("section", None),
        ),
        out_specs=P("section", None, "seq", None),
        check_vma=False,
    )
```

profile of v0, /device:TPU:6, one launch (start us, length us, event | category | flops | bytes accessed | tf_op | source)
XLA Modules:
  0.0 656.5 jit_solution(11344562939826951824)
XLA Ops:
  3.5 12.1 %all-to-all-start = ((bf16[64,16,128]{2,1,0:T(8,128)(2,1)}), bf16[64,16,128]{2,1,0:T(8,128)(2,1)S(1)}, u32[]{:S(2)}, u32[]{:S(2)}) async-start(bf16[64,16,128]{2,1,0:T(8,128)(2,1)} %bitcast.34), calls=%async_computation | async-start | bytes 524288 | tf_op jit(solution)/shard_map/all_to_all | solution.py:128
  17.5 11.1 %all-to-all-done = bf16[64,16,128]{2,1,0:T(8,128)(2,1)S(1)} async-done(((bf16[64,16,128]{2,1,0:T(8,128)(2,1)}), bf16[64,16,128]{2,1,0:T(8,128)(2,1)S(1)}, u32[]{:S(2)}, u32[]{:S(2)}) %all-to-all-start) | async-done | bytes 262176 | tf_op jit(solution)/shard_map/all_to_all | solution.py:128
  31.1 5.8 all-to-all-start.1
  39.5 93.6 %all-to-all-done.1 = bf16[64,128,256]{2,1,0:T(8,128)(2,1)} async-done(((bf16[64,128,256]{2,1,0:T(8,128)(2,1)}), bf16[64,128,256]{2,1,0:T(8,128)(2,1)}, u32[]{:S(2)}, u32[]{:S(2)}) %all-to-all-start.1) | async-done | bytes 4194336 | tf_op jit(solution)/shard_map/all_to_all | solution.py:97
  138.1 18.6 %all_to_all.52 = bf16[64,2,1024]{2,1,0:T(2,128)(2,1)S(1)} all-to-all(bf16[64,2,1024]{2,1,0:T(2,128)(2,1)S(1)} %reshape.538), channel_id=1, replica_groups=mesh['section'=4,'seq'=64] {'seq'}, dimensions={0} | all-to-all | bytes 524288 | tf_op jit(solution)/shard_map/all_to_all | solution.py:157
  160.1 9.1 %collective-permute-done = bf16[64,2048]{1,0:T(8,128)(2,1)S(1)} collective-permute-done((bf16[64,2048]{1,0:T(8,128)(2,1)S(1)}, bf16[64,2048]{1,0:T(8,128)(2,1)S(1)}, u32[]{:S(2)}, u32[]{:S(2)}) %collective-permute-start) | collective-permute-done | bytes 262176 | tf_op jit(solution)/shard_map/ppermute | solution.py:25
  170.7 5.5 all-to-all-start.3
  176.2 12.8 %all-to-all-done.3 = bf16[64,16,128]{2,1,0:T(8,128)(2,1)} async-done(((bf16[64,16,128]{2,1,0:T(8,128)(2,1)}), bf16[64,16,128]{2,1,0:T(8,128)(2,1)}, u32[]{:S(2)}, u32[]{:S(2)}) %all-to-all-start.3) | async-done | bytes 262176 | tf_op jit(solution)/shard_map/all_to_all | solution.py:128
  194.2 4.9 all-to-all-start.4
  199.3 12.7 %all-to-all-done.4 = bf16[64,2,1024]{2,1,0:T(2,128)(2,1)S(1)} async-done(((bf16[64,2,1024]{2,1,0:T(2,128)(2,1)}), bf16[64,2,1024]{2,1,0:T(2,128)(2,1)S(1)}, u32[]{:S(2)}, u32[]{:S(2)}) %all-to-all-start.4) | async-done | bytes 262176 | tf_op jit(solution)/shard_map/all_to_all | solution.py:157
  214.7 9.1 %collective-permute-done.1 = bf16[64,2048]{1,0:T(8,128)(2,1)S(1)} collective-permute-done((bf16[64,2048]{1,0:T(8,128)(2,1)S(1)}, bf16[64,2048]{1,0:T(8,128)(2,1)S(1)}, u32[]{:S(2)}, u32[]{:S(2)}) %collective-permute-start.1) | collective-permute-done | bytes 262176 | tf_op jit(solution)/shard_map/ppermute | solution.py:25
  225.4 5.6 all-to-all-start.5
  231.0 12.8 %all-to-all-done.5 = bf16[64,16,128]{2,1,0:T(8,128)(2,1)} async-done(((bf16[64,16,128]{2,1,0:T(8,128)(2,1)}), bf16[64,16,128]{2,1,0:T(8,128)(2,1)}, u32[]{:S(2)}, u32[]{:S(2)}) %all-to-all-start.5) | async-done | bytes 262176 | tf_op jit(solution)/shard_map/all_to_all | solution.py:128
  248.2 17.8 %all_to_all.53 = bf16[64,2,1024]{2,1,0:T(2,128)(2,1)S(1)} all-to-all(bf16[64,2,1024]{2,1,0:T(2,128)(2,1)S(1)} %reshape.542), channel_id=1, replica_groups=mesh['section'=4,'seq'=64] {'seq'}, dimensions={0} | all-to-all | bytes 524288 | tf_op jit(solution)/shard_map/all_to_all | solution.py:157
  268.7 176.3 %collective-permute-done.2 = bf16[64,2048]{1,0:T(8,128)(2,1)S(1)} collective-permute-done((bf16[64,2048]{1,0:T(8,128)(2,1)S(1)}, bf16[64,2048]{1,0:T(8,128)(2,1)S(1)}, u32[]{:S(2)}, u32[]{:S(2)}) %collective-permute-start.2) | collective-permute-done | bytes 262176 | tf_op jit(solution)/shard_map/ppermute | solution.py:25
  446.6 5.5 all-to-all-start.7
  452.1 12.8 %all-to-all-done.7 = bf16[64,16,128]{2,1,0:T(8,128)(2,1)} async-done(((bf16[64,16,128]{2,1,0:T(8,128)(2,1)}), bf16[64,16,128]{2,1,0:T(8,128)(2,1)}, u32[]{:S(2)}, u32[]{:S(2)}) %all-to-all-start.7) | async-done | bytes 262176 | tf_op jit(solution)/shard_map/all_to_all | solution.py:128
  464.9 58.9 %conditional.8 = (bf16[1,1024,128]{2,1,0:T(8,128)(2,1)}) conditional(s32[]{:T(128)} %convert_element_type.222, () %tuple.62, (bf16[64,16,128]{2,1,0:T(8,128)(2,1)}, s32[]{:T(128)}, s32[16,512,16]{2,1,0:T(8,128)}, s32[]{:T(128)}, bf16[1,8192,256]{2,1,0:T(8,128)(2,1)}, /*index=5*/s32[16]{0:T(128)S(1)}) %tuple.198), branch_computations={%region_22.24_spmd, %region_23.29_spmd} | conditional | flops 70229280 | bytes 40082432 | solution.py:156
  466.9 4.9 fusion.201
  471.8 52.0 %while.53 = (s32[]{:T(128)}, bf16[4,16,16,128]{3,2,1,0:T(8,128)(2,1)}, bf16[4,16,16,128]{3,2,1,0:T(8,128)(2,1)}, s32[4,16,16]{2,1,0:T(8,128)S(1)}, bf16[256,32,1...) while((s32[]{:T(128)}, bf16[4,16,16,128]{3,2,1,0:T(8,128)(2,1)}, ...), condition=%wide.region_27.28_spmd.clone, body=%wide.region_24.27_spmd.clone.sunk | while | flops 70164736 | bytes 31611512 | solution.py:59
  487.5 3.8 gather_fusion.7
  513.5 3.8 gather_fusion.7
  527.4 17.8 %all_to_all.54 = bf16[64,2,1024]{2,1,0:T(2,128)(2,1)S(1)} all-to-all(bf16[64,2,1024]{2,1,0:T(2,128)(2,1)S(1)} %reshape.544), channel_id=1, replica_groups=mesh['section'=4,'seq'=64] {'seq'}, dimensions={0} | all-to-all | bytes 524288 | tf_op jit(solution)/shard_map/all_to_all | solution.py:157
  548.0 9.1 %collective-permute-done.3 = bf16[64,2048]{1,0:T(8,128)(2,1)S(1)} collective-permute-done((bf16[64,2048]{1,0:T(8,128)(2,1)S(1)}, bf16[64,2048]{1,0:T(8,128)(2,1)S(1)}, u32[]{:S(2)}, u32[]{:S(2)}) %collective-permute-start.3) | collective-permute-done | bytes 262176 | tf_op jit(solution)/shard_map/ppermute | solution.py:25
  558.6 4.6 all-to-all-start.9
  563.2 13.0 %all-to-all-done.9 = bf16[64,16,128]{2,1,0:T(8,128)(2,1)S(1)} async-done(((bf16[64,16,128]{2,1,0:T(8,128)(2,1)}), bf16[64,16,128]{2,1,0:T(8,128)(2,1)S(1)}, u32[]{:S(2)}, u32[]{:S(2)}) %all-to-all-start.9) | async-done | bytes 262176 | tf_op jit(solution)/shard_map/all_to_all | solution.py:128
  576.2 55.6 %conditional.9 = (bf16[1,1024,128]{2,1,0:T(8,128)(2,1)}) conditional(s32[]{:T(128)} %convert_element_type.230, () %tuple.64, (bf16[64,16,128]{2,1,0:T(8,128)(2,1)S(1)}, s32[]{:T(128)}, s32[16,512,16]{2,1,0:T(8,128)}, s32[]{:T(128)}, bf16[1,8192,256]{2,1,0:T(8,128)(2,1)}, /*index=5*/s32[16]{0:T(128)S(1)}) %tuple.199), branch_computations={%region_29.31_spmd, %region_30.36_spmd} | conditional | flops 70229280 | bytes 40081924 | solution.py:156
  578.2 4.9 fusion.203
  583.1 48.7 %while.54 = (s32[]{:T(128)}, bf16[4,16,16,128]{3,2,1,0:T(8,128)(2,1)}, bf16[4,16,16,128]{3,2,1,0:T(8,128)(2,1)S(1)}, s32[4,16,16]{2,1,0:T(8,128)S(1)}, bf16[256,...) while((s32[]{:T(128)}, ...), condition=%wide.region_34.35_spmd.clone, body=%wide.region_31.34_spmd.clone.sunk | while | flops 70164736 | bytes 31611004 | solution.py:59
  597.9 3.8 gather_fusion.9
  636.1 4.9 all-to-all-start.10
  641.8 12.2 %all-to-all-done.10 = bf16[64,2,1024]{2,1,0:T(2,128)(2,1)S(1)} async-done(((bf16[64,2,1024]{2,1,0:T(2,128)(2,1)}), bf16[64,2,1024]{2,1,0:T(2,128)(2,1)S(1)}, u32[]{:S(2)}, u32[]{:S(2)}) %all-to-all-start.10) | async-done | bytes 262176 | tf_op jit(solution)/shard_map/all_to_all | solution.py:157
  (226 shorter events, 148.0 us)
Async XLA Ops:
  0.0 2.5 copy-start.17
  2.0 13.6 %copy-start.14 = (bf16[1,2,64,4096]{3,2,1,0:T(8,128)(2,1)S(1)}, bf16[1,2,64,4096]{3,2,1,0:T(8,128)(2,1)}, u32[]{:S(2)}) copy-start(bf16[1,2,64,4096]{3,2,1,0:T(8,128)(2,1)} %param.29) | copy-start | bytes 3145732
  3.5 25.1 %all-to-all-start = ((bf16[64,16,128]{2,1,0:T(8,128)(2,1)}), bf16[64,16,128]{2,1,0:T(8,128)(2,1)S(1)}, u32[]{:S(2)}, u32[]{:S(2)}) async-start(bf16[64,16,128]{2,1,0:T(8,128)(2,1)} %bitcast.34), calls=%async_computation | async-start | bytes 524288 | tf_op jit(solution)/shard_map/all_to_all | solution.py:128
  31.1 5.8 copy-start.15
  31.1 102.0 %all-to-all-start.1 = ((bf16[64,128,256]{2,1,0:T(8,128)(2,1)}), bf16[64,128,256]{2,1,0:T(8,128)(2,1)}, u32[]{:S(2)}, u32[]{:S(2)}) async-start(bf16[64,128,256]{2,1,0:T(8,128)(2,1)} %bitcast.477), calls=%async_computation.1 | async-start | bytes 8388608 | tf_op jit(solution)/shard_map/all_to_all | solution.py:97
  36.9 96.2 %copy-start.18 = (s32[1,16]{1,0:T(1,128)S(1)}, s32[1,16]{1,0:T(1,128)}, u32[]{:S(2)}) copy-start(s32[1,16]{1,0:T(1,128)} %param.31) | copy-start | bytes 196
  138.0 20.6 %copy-start.5 = (bf16[2,64,2048]{2,1,0:T(8,128)(2,1)S(1)}, bf16[2,64,2048]{2,1,0:T(8,128)(2,1)}, u32[]{:S(2)}) copy-start(bf16[2,64,2048]{2,1,0:T(8,128)(2,1)} %param.28) | copy-start | bytes 1572868
  138.0 20.6 %copy-start.16 = (f32[1,2048]{1,0:T(1,128)S(1)}, f32[1,2048]{1,0:T(1,128)}, u32[]{:S(2)}) copy-start(f32[1,2048]{1,0:T(1,128)} %param.33) | copy-start | bytes 24580
  158.8 10.4 %collective-permute-start = (bf16[64,2048]{1,0:T(8,128)(2,1)S(1)}, bf16[64,2048]{1,0:T(8,128)(2,1)S(1)}, u32[]{:S(2)}, u32[]{:S(2)}) collective-permute-start(bf16[64,2048]{1,0:T(8,128)(2,1)S(1)} %fusion.166), channel_id=1, source_target_pairs={{0,64},{64,128},{128,192},{1,65},{65,129},{129,193},{2,66},{66,130... | collective-permute-start | bytes 786440 | tf_op jit(solution)/shard_map/ppermute | solution.py:25
  170.7 18.3 %all-to-all-start.3 = ((bf16[64,16,128]{2,1,0:T(8,128)(2,1)}), bf16[64,16,128]{2,1,0:T(8,128)(2,1)}, u32[]{:S(2)}, u32[]{:S(2)}) async-start(bf16[64,16,128]{2,1,0:T(8,128)(2,1)} %bitcast.48), calls=%async_computation.3 | async-start | bytes 524288 | tf_op jit(solution)/shard_map/all_to_all | solution.py:128
  189.7 9.3 %copy-start.13 = (f32[4,16,16,128]{3,2,1,0:T(8,128)S(1)}, f32[4,16,16,128]{3,2,1,0:T(8,128)}, u32[]{:S(2)}) copy-start(f32[4,16,16,128]{3,2,1,0:T(8,128)} %copy-done.12) | copy-start | bytes 1572868
  194.2 17.9 %all-to-all-start.4 = ((bf16[64,2,1024]{2,1,0:T(2,128)(2,1)}), bf16[64,2,1024]{2,1,0:T(2,128)(2,1)S(1)}, u32[]{:S(2)}, u32[]{:S(2)}) async-start(bf16[64,2,1024]{2,1,0:T(2,128)(2,1)} %reshape.540), calls=%async_computation.4 | async-start | bytes 524288 | tf_op jit(solution)/shard_map/all_to_all | solution.py:157
  213.4 10.7 %copy-start.6 = (bf16[2,64,2048]{2,1,0:T(8,128)(2,1)}, bf16[2,64,2048]{2,1,0:T(8,128)(2,1)S(1)}, u32[]{:S(2)}) copy-start(bf16[2,64,2048]{2,1,0:T(8,128)(2,1)S(1)} %get-tuple-element.476) | copy-start | bytes 1572868
  213.4 10.4 %collective-permute-start.1 = (bf16[64,2048]{1,0:T(8,128)(2,1)S(1)}, bf16[64,2048]{1,0:T(8,128)(2,1)S(1)}, u32[]{:S(2)}, u32[]{:S(2)}) collective-permute-start(bf16[64,2048]{1,0:T(8,128)(2,1)S(1)} %get-tuple-element.477), channel_id=1, source_target_pairs={{0,64},{64,128},{128,192},{1,65},{65,129},{129,193},{2,66},{66,130... | collective-permute-start | bytes 786440 | tf_op jit(solution)/shard_map/ppermute | solution.py:25
  225.4 18.5 %all-to-all-start.5 = ((bf16[64,16,128]{2,1,0:T(8,128)(2,1)}), bf16[64,16,128]{2,1,0:T(8,128)(2,1)}, u32[]{:S(2)}, u32[]{:S(2)}) async-start(bf16[64,16,128]{2,1,0:T(8,128)(2,1)} %bitcast.55), calls=%async_computation.5 | async-start | bytes 524288 | tf_op jit(solution)/shard_map/all_to_all | solution.py:128
  248.1 19.0 %copy-start.7 = (bf16[2,64,2048]{2,1,0:T(8,128)(2,1)S(1)}, bf16[2,64,2048]{2,1,0:T(8,128)(2,1)}, u32[]{:S(2)}) copy-start(bf16[2,64,2048]{2,1,0:T(8,128)(2,1)} %copy-done.6) | copy-start | bytes 1572868
  267.4 178.0 %copy-start.8 = (bf16[2,64,2048]{2,1,0:T(8,128)(2,1)}, bf16[2,64,2048]{2,1,0:T(8,128)(2,1)S(1)}, u32[]{:S(2)}) copy-start(bf16[2,64,2048]{2,1,0:T(8,128)(2,1)S(1)} %get-tuple-element.472) | copy-start | bytes 1572868
  267.4 177.6 %collective-permute-start.2 = (bf16[64,2048]{1,0:T(8,128)(2,1)S(1)}, bf16[64,2048]{1,0:T(8,128)(2,1)S(1)}, u32[]{:S(2)}, u32[]{:S(2)}) collective-permute-start(bf16[64,2048]{1,0:T(8,128)(2,1)S(1)} %get-tuple-element.473), channel_id=1, source_target_pairs={{0,64},{64,128},{128,192},{1,65},{65,129},{129,193},{2,66},{66,130... | collective-permute-start | bytes 786440 | tf_op jit(solution)/shard_map/ppermute | solution.py:25
  446.6 18.3 %all-to-all-start.7 = ((bf16[64,16,128]{2,1,0:T(8,128)(2,1)}), bf16[64,16,128]{2,1,0:T(8,128)(2,1)}, u32[]{:S(2)}, u32[]{:S(2)}) async-start(bf16[64,16,128]{2,1,0:T(8,128)(2,1)} %bitcast.62), calls=%async_computation.7 | async-start | bytes 524288 | tf_op jit(solution)/shard_map/all_to_all | solution.py:128
  481.1 2.5 copy-start.3
  494.1 2.5 copy-start.3
  507.1 2.5 copy-start.3
  520.1 2.5 copy-start.3
  527.4 19.0 %copy-start.9 = (bf16[2,64,2048]{2,1,0:T(8,128)(2,1)S(1)}, bf16[2,64,2048]{2,1,0:T(8,128)(2,1)}, u32[]{:S(2)}) copy-start(bf16[2,64,2048]{2,1,0:T(8,128)(2,1)} %copy-done.8) | copy-start | bytes 1572868
  546.6 10.7 %copy-start.10 = (bf16[2,64,2048]{2,1,0:T(8,128)(2,1)}, bf16[2,64,2048]{2,1,0:T(8,128)(2,1)S(1)}, u32[]{:S(2)}) copy-start(bf16[2,64,2048]{2,1,0:T(8,128)(2,1)S(1)} %get-tuple-element.468) | copy-start | bytes 1572868
  546.6 10.4 %collective-permute-start.3 = (bf16[64,2048]{1,0:T(8,128)(2,1)S(1)}, bf16[64,2048]{1,0:T(8,128)(2,1)S(1)}, u32[]{:S(2)}, u32[]{:S(2)}) collective-permute-start(bf16[64,2048]{1,0:T(8,128)(2,1)S(1)} %get-tuple-element.469), channel_id=1, source_target_pairs={{0,64},{64,128},{128,192},{1,65},{65,129},{129,193},{2,66},{66,130... | collective-permute-start | bytes 786440 | tf_op jit(solution)/shard_map/ppermute | solution.py:25
  558.6 17.6 %all-to-all-start.9 = ((bf16[64,16,128]{2,1,0:T(8,128)(2,1)}), bf16[64,16,128]{2,1,0:T(8,128)(2,1)S(1)}, u32[]{:S(2)}, u32[]{:S(2)}) async-start(bf16[64,16,128]{2,1,0:T(8,128)(2,1)} %bitcast.70), calls=%async_computation.9 | async-start | bytes 524288 | tf_op jit(solution)/shard_map/all_to_all | solution.py:128
  592.4 1.6 copy-start.4
  604.5 1.6 copy-start.4
  616.7 1.6 copy-start.4
  631.8 9.3 %copy-start.11 = (bf16[2,64,2048]{2,1,0:T(8,128)(2,1)S(1)}, bf16[2,64,2048]{2,1,0:T(8,128)(2,1)}, u32[]{:S(2)}) copy-start(bf16[2,64,2048]{2,1,0:T(8,128)(2,1)} %copy-done.10) | copy-start | bytes 1572868
  636.1 17.9 %all-to-all-start.10 = ((bf16[64,2,1024]{2,1,0:T(2,128)(2,1)}), bf16[64,2,1024]{2,1,0:T(2,128)(2,1)S(1)}, u32[]{:S(2)}, u32[]{:S(2)}) async-start(bf16[64,2,1024]{2,1,0:T(2,128)(2,1)} %reshape.546), calls=%async_computation.10 | async-start | bytes 524288 | tf_op jit(solution)/shard_map/all_to_all | solution.py:157
  (2 other events, 2.4 us)
where the time goes:
time: 666 us; the launch traced here: 656 us
  waiting for transfers between devices  384 us (58%)
  local copies, waits for them, and re-layouts  92.4 us (14%)
  blocking collectives  54.2 us (8%)
  starting transfers between devices  54.1 us (8%)
  other arithmetic  50.9 us (8%)
  matrix products  18.5 us (3%)
    ppermute x4, waiting for transfers between devices, passed_along(): lax.ppermute(value, axis, [(source, source + steps) for source in range(l...  203 us
    all_to_all x1, waiting for transfers between devices, local(): lax.all_to_all(outgoing, 'seq', split_axis=0, concat_axis=1, tiled=True)  93.6 us
    all_to_all x5, waiting for transfers between devices, local(): lax.all_to_all(outgoing_query, 'seq', split_axis=0, concat_axis=1, tiled=...  62.4 us
    all_to_all x3, blocking collectives, local(): lax.all_to_all(shortened(unit_outputs), 'seq', split_axis=1, concat_axis=...  54.2 us
    all_to_all x5, starting transfers between devices, local(): lax.all_to_all(outgoing_query, 'seq', split_axis=0, concat_axis=1, tiled=...  33.3 us
    gather x8, local copies, waits for them, and re-layouts, one_group(): jnp.take(value_table, position_part, axis=0)  30.3 us
    all_to_all x2, waiting for transfers between devices, local(): lax.all_to_all(shortened(unit_outputs), 'seq', split_axis=1, concat_axis=...  24.9 us
    select_n x8, other arithmetic, one_group(): jnp.take(key_table, position_part, axis=0)  22.6 us
  transfers between devices with their start and end apart: 12, of which 12 were waited for; matrix products, arithmetic and copies ran while one was open for 1% of the time, Pallas kernels for 0%

commit v1 on v0

v1 whole, which is shorter than its diff:
```python
import functools

import jax
import jax.numpy as jnp
from jax import lax
from jax.experimental import pallas as pl
from jax.experimental.pallas import tpu as pltpu
from jax.sharding import Mesh, PartitionSpec as P

HEADS = 16
HEAD_DIM = 128
QUERY_BLOCK = 16
KEY_BLOCK = 32
SLOTS = 16
SECTIONS = 4
CHUNKS = 4
GROUP = 8
SPAN = SLOTS * KEY_BLOCK
SCORE_FLOOR = -1e30

OWNERS = ("z", "yh")


def attend_kernel(
    places, meta, x_ref, gain_ref, gate_ref, *rest, pieces, groups
):
    k_parts = rest[:pieces]
    v_parts = rest[pieces : 2 * pieces]
    out_ref, k_tab, v_tab, sems = rest[2 * pieces :]
    rows = k_tab.shape[0] // pieces
    base = meta[1]
    live_keys = meta[2] * KEY_BLOCK

    @pl.when(meta[0] > 0)
    def _():
        copies = []
        for which, (parts, tab) in enumerate(((k_parts, k_tab), (v_parts, v_tab))):
            for p in range(pieces):
                copy = pltpu.make_async_copy(
                    parts[p], tab.at[pl.ds(p * rows, rows), :], sems.at[which, p]
                )
                copy.start()
                copies.append(copy)
        for copy in copies:
            copy.wait()

        def one_group(index, carry):
            row0 = pl.multiple_of(index * (GROUP * QUERY_BLOCK), GROUP * QUERY_BLOCK)
            wide = x_ref[pl.ds(row0, GROUP * QUERY_BLOCK), :].astype(jnp.float32)
            mean = jnp.mean(wide * wide, axis=-1, keepdims=True)
            queries = (wide * lax.rsqrt(mean + 1e-06) * gain_ref[...]).astype(jnp.bfloat16)
            first = base + index * (GROUP * SLOTS)
            scores = []
            starts = []
            for g in range(GROUP):
                at = [
                    pl.multiple_of(places[first + g * SLOTS + j], KEY_BLOCK)
                    for j in range(SLOTS)
                ]
                starts.append(at)
                keys = jnp.concatenate(
                    [k_tab[pl.ds(a, KEY_BLOCK), :] for a in at], axis=0
                )
                scores.append(
                    lax.dot_general(
                        queries[g * QUERY_BLOCK : (g + 1) * QUERY_BLOCK],
                        keys,
                        (((1,), (1,)), ((), ())),
                        preferred_element_type=jnp.float32,
                    )
                )
            scores = jnp.concatenate(scores, axis=0) * (HEAD_DIM**-0.5)
            lane = lax.broadcasted_iota(jnp.int32, scores.shape, 1)
            scores = jnp.where(lane < live_keys, scores, SCORE_FLOOR)
            highest = jnp.max(scores, axis=-1, keepdims=True)
            exponent = jnp.exp(scores - highest)
            total = jnp.sum(exponent, axis=-1, keepdims=True)
            weights = (exponent / total).astype(jnp.bfloat16)
            summed = []
            for g in range(GROUP):
                values = jnp.concatenate(
                    [v_tab[pl.ds(a, KEY_BLOCK), :] for a in starts[g]], axis=0
                )
                summed.append(
                    jnp.dot(
                        weights[g * QUERY_BLOCK : (g + 1) * QUERY_BLOCK],
                        values,
                        preferred_element_type=jnp.float32,
                    )
                )
            heads = jnp.concatenate(summed, axis=0).astype(jnp.bfloat16)
            updated = wide + gate_ref[...] * heads.astype(jnp.float32)
            out_ref[pl.ds(row0, GROUP * QUERY_BLOCK), :] = updated.astype(jnp.bfloat16)
            return carry

        lax.fori_loop(0, groups, one_group, 0)

    @pl.when(meta[0] <= 0)
    def _():
        out_ref[...] = jnp.zeros_like(out_ref)


def attend(places, meta, x, gain, gate, k_parts, v_parts):
    pieces = len(k_parts)
    rows = k_parts[0].shape[0]
    total = pieces * rows
    queries = x.shape[0]
    vmem = pl.BlockSpec(memory_space=pltpu.VMEM)
    smem = pl.BlockSpec(memory_space=pltpu.SMEM)
    hbm = pl.BlockSpec(memory_space=pl.ANY)
    return pl.pallas_call(
        functools.partial(
            attend_kernel, pieces=pieces, groups=queries // (GROUP * QUERY_BLOCK)
        ),
        out_shape=jax.ShapeDtypeStruct(x.shape, jnp.bfloat16),
        in_specs=[smem, smem, vmem, vmem, vmem] + [hbm] * (2 * pieces),
        out_specs=vmem,
        scratch_shapes=[
            pltpu.VMEM((total, HEAD_DIM), jnp.bfloat16),
            pltpu.VMEM((total, HEAD_DIM), jnp.bfloat16),
            pltpu.SemaphoreType.DMA((2, pieces)),
        ],
        compiler_params=pltpu.CompilerParams(vmem_limit_bytes=24 * 1024 * 1024),
        cost_estimate=pl.CostEstimate(
            flops=4 * queries * SPAN * HEAD_DIM,
            bytes_accessed=2 * total * HEAD_DIM * 2,
            transcendentals=queries * SPAN,
        ),
    )(places, meta, x, gain, gate, *k_parts, *v_parts)


def swapped(value, axis):
    return lax.ppermute(value, axis, [(0, 1), (1, 0)])


def spread(value):
    other = swapped(value, "yl")
    return [value, other, swapped(value, "core"), swapped(other, "core")]


def local(patches, stale_cache, block_lists, block_counts, query_gain, branch_gate):
    section = lax.axis_index("section")
    owner = lax.axis_index("z") * lax.axis_size("yh") + lax.axis_index("yh")
    yl, core = lax.axis_index("yl"), lax.axis_index("core")
    micro_count, patch_rows, channels = patches.shape
    sources = lax.axis_size("z") * lax.axis_size("yh")
    tokens = micro_count * patch_rows
    chunk_tokens = tokens // CHUNKS

    by_head = stale_cache[0].reshape(tokens, 2, HEADS, HEAD_DIM).transpose(1, 2, 0, 3)
    mine = lax.dynamic_slice_in_dim(
        patches.reshape(tokens, HEADS, HEAD_DIM), section * chunk_tokens, chunk_tokens, 0
    ).transpose(1, 0, 2)
    mine = lax.all_to_all(mine, OWNERS, 0, 0, tiled=True)
    fresh = [mine.reshape(sources * chunk_tokens, HEAD_DIM)]
    for c in range(1, CHUNKS):
        fresh.append(lax.ppermute(fresh[0], "section", [(c, 0)]))
    tables = []
    for which in range(2):
        moved = lax.all_to_all(by_head[which], OWNERS, 0, 0, tiled=True)
        tables.append(spread(moved.reshape(sources * tokens, HEAD_DIM)))
    k_parts, v_parts = tables

    query_blocks = patch_rows // QUERY_BLOCK
    lists = lax.dynamic_index_in_dim(block_lists[0], owner, 0, keepdims=False)
    lists = lists.reshape(micro_count, sources, 2, 2, query_blocks, SLOTS)
    lists = lax.dynamic_slice(
        lists, (0, 0, yl, core, 0, 0), (micro_count, sources, 1, 1, query_blocks, SLOTS)
    )
    lists = lists.reshape(micro_count, sources, query_blocks, SLOTS).transpose(0, 2, 1, 3)
    lists = lists.reshape(CHUNKS, -1, sources, SLOTS).transpose(0, 2, 1, 3)
    per_shard = patch_rows // KEY_BLOCK
    per_micro = per_shard * sources * 4
    micro, rest = lists // per_micro, lists % per_micro
    shard, half = rest // per_shard, rest % per_shard
    piece = ((shard % 2) ^ core) * 2 + ((shard // 2 % 2) ^ yl)
    places = ((piece * sources + shard // 4) * micro_count + micro) * patch_rows + half * KEY_BLOCK
    places = places.reshape(-1)
    chunk_entries = places.shape[0] // CHUNKS
    count = lax.dynamic_index_in_dim(block_counts[0], owner, 0, keepdims=False)
    gain = lax.dynamic_index_in_dim(query_gain.reshape(HEADS, HEAD_DIM), owner, 0)
    gate = lax.dynamic_index_in_dim(branch_gate.reshape(HEADS, HEAD_DIM), owner, 0)

    steps = CHUNKS + SECTIONS - 1
    results = []
    received = None
    for step in range(steps):
        if step == 0:
            x = fresh[0]
        elif step < CHUNKS:
            x = jnp.where(section == 0, fresh[step], received)
        else:
            x = received
        chunk = step - section
        active = ((chunk >= 0) & (chunk < CHUNKS)).astype(jnp.int32)
        meta = jnp.stack([active, jnp.clip(chunk, 0, CHUNKS - 1) * chunk_entries, count])
        result = attend(places, meta, x, gain, gate, k_parts, v_parts)
        results.append(result)
        if step < steps - 1:
            received = lax.ppermute(
                result, "section", [(s, s + 1) for s in range(SECTIONS - 1)]
            )
    done = lax.dynamic_slice_in_dim(jnp.stack(results), section, CHUNKS, 0)
    done = done.reshape(CHUNKS, sources, chunk_tokens, HEAD_DIM).transpose(1, 0, 2, 3)
    done = lax.all_to_all(done, OWNERS, 0, 0, tiled=True)
    done = done.reshape(HEADS, micro_count, patch_rows, HEAD_DIM).transpose(1, 2, 0, 3)
    return done.reshape(1, micro_count, patch_rows, channels)


def solution(mesh):
    fine = Mesh(
        mesh.devices.reshape(SECTIONS, -1, 2, 2, 2), ("section", "z", "yh", "yl", "core")
    )
    seq = ("z", "yh", "yl", "core")
    return jax.shard_map(
        local,
        mesh=fine,
        in_specs=(
            P(None, seq, None),
            P("section", None, seq, None),
            P("section", None, None, None),
            P("section", None),
            P("section", None),
            P("section", None),
        ),
        out_specs=P("section", None, seq, None),
        check_vma=False,
    )
```

time: 666 us -> 180 us (0.27); the launches traced: 656 us -> 179 us
  waiting for transfers between devices: 384 us -> 67.5 us
  local copies, waits for them, and re-layouts: 92.4 us -> 7.46 us
  other arithmetic: 50.9 us -> 10.3 us
  starting transfers between devices: 54.1 us -> 21.9 us
  matrix products: 18.5 us -> 0 us
  Pallas kernels: 0 us -> 17.9 us
    all_to_all x8 -> x2, waiting for transfers between devices: 181 us -> 15.4 us  [the longest x1 15.4 us: local(): moved = lax.all_to_all(by_head[which], OWNERS, 0, 0, tiled=True)]
    ppermute x4 -> x15, waiting for transfers between devices: 203 us -> 52.1 us  [the longest x6 42.5 us: local(): lax.ppermute(result, 'section', [(s, s + 1) for s in range(SECTIONS - 1)])]
    gather x16 -> x0, local copies, waits for them, and re-layouts: 51 us -> none  [the longest x8 30.3 us: one_group(): jnp.take(value_table, position_part, axis=0)]
    all_to_all x8 -> x2, starting transfers between devices: 48.9 us -> 7.08 us  [the longest x1 3.57 us: local(): moved = lax.all_to_all(by_head[which], OWNERS, 0, 0, tiled=True)]
    select_n x13 -> x3, other arithmetic: 24.5 us -> 0.05 us  [local(): x = jnp.where(section == 0, fresh[step], received)]
    dot_general x16 -> x0, matrix products: 18.5 us -> none  [the longest x8 9.91 us: one_group(): jnp.einsum('gqk,gkd->gqd', weights, value_part, preferred_element_type=jn...]
    pallas_call x0 -> x6, Pallas kernels: none -> 17.9 us  [attend(): pl.pallas_call(functools.partial(attend_kernel, pieces=pieces, groups=que...]
    unnamed x15 -> x0, other arithmetic: 13.5 us -> none
  transfers between devices with their start and end apart: 12 -> 17, of which waited for: 12 -> 8; matrix products, arithmetic and copies ran while one was open for 1% -> 4% of each run, Pallas kernels for 0% -> 1%
where the time goes in v1:
time: 180 us; the launch traced here: 179 us
  waiting for transfers between devices  67.5 us (38%)
  blocking collectives  53.4 us (30%)
  starting transfers between devices  21.9 us (12%)
  Pallas kernels  17.9 us (10%)
  other arithmetic  10.3 us (6%)
  local copies, waits for them, and re-layouts  7.46 us (4%)
    ppermute x6, waiting for transfers between devices, local(): lax.ppermute(result, 'section', [(s, s + 1) for s in range(SECTIONS - 1)])  42.5 us
    all_to_all x1, blocking collectives, local(): moved = lax.all_to_all(by_head[which], OWNERS, 0, 0, tiled=True)  29.6 us
    all_to_all x1, blocking collectives, local(): done = lax.all_to_all(done, OWNERS, 0, 0, tiled=True)  23.8 us
    pallas_call x6, Pallas kernels, attend(): pl.pallas_call(functools.partial(attend_kernel, pieces=pieces, groups=que...  17.9 us
    all_to_all x1, waiting for transfers between devices, local(): moved = lax.all_to_all(by_head[which], OWNERS, 0, 0, tiled=True)  15.4 us
    ppermute x6, waiting for transfers between devices, swapped(): return lax.ppermute(value, axis, [(0, 1), (1, 0)])  9.56 us
    ppermute x6, starting transfers between devices, local(): lax.ppermute(result, 'section', [(s, s + 1) for s in range(SECTIONS - 1)])  7.75 us
    pallas_call x1, other arithmetic, attend(): pl.pallas_call(functools.partial(attend_kernel, pieces=pieces, groups=que...  5.2 us
  transfers between devices with their start and end apart: 17, of which 8 were waited for; matrix products, arithmetic and copies ran while one was open for 4% of the time, Pallas kernels for 1%

profile of v1, /device:TPU:6, one launch (start us, length us, event | category | flops | bytes accessed | tf_op | source)
XLA Modules:
  0.0 178.9 jit_solution(793826006401179395)
XLA Ops:
  0.0 1.5 copy.36
  1.9 0.9 slice_bitcast_fusion
  2.8 29.6 %all_to_all.20 = bf16[16,128,128]{2,1,0:T(8,128)(2,1)S(1)} all-to-all(bf16[16,128,128]{2,1,0:T(8,128)(2,1)S(1)} %get-tuple-element.6), channel_id=1, replica_groups=mesh['section'=4,'z'=8,'yh'=2,'yl'=2,'core'=2] {'z','yh'}, dimensions={0} | all-to-all | bytes 1048576 | tf_op jit(solution)/shard_map/all_to_all | solution.py:160
  32.5 3.6 %all-to-all-start.2 = ((bf16[16,128,128]{2,1,0:T(8,128)(2,1)}), bf16[16,128,128]{2,1,0:T(8,128)(2,1)S(1)}, u32[]{:S(2)}, u32[]{:S(2)}) async-start(bf16[16,128,128]{2,1,0:T(8,128)(2,1)} %get-tuple-element.5), calls=%async_computation.2 | async-start | bytes 1048576 | tf_op jit(solution)/shard_map/all_to_all | solution.py:160
  39.1 15.4 %all-to-all-done.2 = bf16[16,128,128]{2,1,0:T(8,128)(2,1)S(1)} async-done(((bf16[16,128,128]{2,1,0:T(8,128)(2,1)}), bf16[16,128,128]{2,1,0:T(8,128)(2,1)S(1)}, u32[]{:S(2)}, u32[]{:S(2)}) %all-to-all-start.2) | async-done | bytes 524320 | tf_op jit(solution)/shard_map/all_to_all | solution.py:160
  54.4 3.5 %all-to-all-start = ((bf16[16,32,128]{2,1,0:T(8,128)(2,1)}), bf16[16,32,128]{2,1,0:T(8,128)(2,1)S(1)}, u32[]{:S(2)}, u32[]{:S(2)}) async-start(bf16[16,32,128]{2,1,0:T(8,128)(2,1)} %bitcast.67), calls=%async_computation | async-start | bytes 262144 | tf_op jit(solution)/shard_map/all_to_all | solution.py:154
  57.9 0.8 collective-permute-start.3
  62.8 9.5 %collective-permute-done.3.rest_5_ = bf16[2048,128]{1,0:T(8,128)(2,1)S(1)} collective-permute-done((bf16[2048,128]{1,0:T(8,128)(2,1)S(1)}, bf16[2048,128]{1,0:T(8,128)(2,1)S(1)}, u32[]{:S(2)}, u32[]{:S(2)}) %collective-permute-start.3) | collective-permute-done | bytes 524320 | tf_op jit(solution)/shard_map/ppermute | solution.py:133
  73.5 0.7 add_add_fusion.6
  74.2 0.7 constant_dynamic-slice_fusion.1
  76.2 3.6 %collective-permute-start.10 = (bf16[512,128]{1,0:T(8,128)(2,1)S(1)}, bf16[512,128]{1,0:T(8,128)(2,1)S(1)}, u32[]{:S(2)}, u32[]{:S(2)}) collective-permute-start(bf16[512,128]{1,0:T(8,128)(2,1)S(1)} %bitcast.88), channel_id=1, source_target_pairs={{192,0},{193,1},{194,2},{195,3},{196,4},{197,5},{198,6},{199,7},{2... | collective-permute-start | bytes 393224 | tf_op jit(solution)/shard_map/ppermute | solution.py:157
  79.9 0.8 shard_map.64
  80.7 1.3 collective-permute-start.7
  82.0 6.2 %collective-permute-done.7 = bf16[512,128]{1,0:T(8,128)(2,1)S(1)} collective-permute-done((bf16[512,128]{1,0:T(8,128)(2,1)S(1)}, bf16[512,128]{1,0:T(8,128)(2,1)S(1)}, u32[]{:S(2)}, u32[]{:S(2)}) %collective-permute-start.7) | collective-permute-done | bytes 131104 | tf_op jit(solution)/shard_map/ppermute | solution.py:200
  88.2 0.8 shard_map.65
  89.0 1.3 collective-permute-start.9
  90.4 5.5 %collective-permute-done.9 = bf16[512,128]{1,0:T(8,128)(2,1)S(1)} collective-permute-done((bf16[512,128]{1,0:T(8,128)(2,1)S(1)}, bf16[512,128]{1,0:T(8,128)(2,1)S(1)}, u32[]{:S(2)}, u32[]{:S(2)}) %collective-permute-start.9) | collective-permute-done | bytes 131104 | tf_op jit(solution)/shard_map/ppermute | solution.py:200
  95.9 0.8 shard_map.66
  96.7 1.3 collective-permute-start.11
  98.0 14.2 %collective-permute-done.11 = bf16[512,128]{1,0:T(8,128)(2,1)S(1)} collective-permute-done((bf16[512,128]{1,0:T(8,128)(2,1)S(1)}, bf16[512,128]{1,0:T(8,128)(2,1)S(1)}, u32[]{:S(2)}, u32[]{:S(2)}) %collective-permute-start.11) | collective-permute-done | bytes 131104 | tf_op jit(solution)/shard_map/ppermute | solution.py:200
  112.3 5.2 %shard_map.67 = bf16[512,128]{1,0:T(8,128)(2,1)S(1)} custom-call(s32[2048]{0:T(1024)S(1)} %reshape.46.places, s32[3]{0:T(128)S(1)} %add_add_fusion.3.meta, bf16[512,128]{1,0:T(8,128)(2,1)S(1)} %broadcast_select_fusion.x_ref, f32[1,128]{1,0:T(1,128)S(1)} %get-tuple-element.8.gain_ref, f32[1,128]{1,0:T(1,128)S(1)} %get-tuple-element.7.gate_ref, ...), custom_call_target="tpu_custom_call" | custom-call | flops 134217728 | bytes 4194304 | tf_op jit(solution)/shard_map/pallas_call | solution.py:111
  117.5 1.3 collective-permute-start.12
  118.8 5.5 %collective-permute-done.12.x_ref = bf16[512,128]{1,0:T(8,128)(2,1)S(1)} collective-permute-done((bf16[512,128]{1,0:T(8,128)(2,1)S(1)}, bf16[512,128]{1,0:T(8,128)(2,1)S(1)}, u32[]{:S(2)}, u32[]{:S(2)}) %collective-permute-start.12) | collective-permute-done | bytes 131104 | tf_op jit(solution)/shard_map/ppermute | solution.py:200
  124.3 5.2 %shard_map.68 = bf16[512,128]{1,0:T(8,128)(2,1)S(1)} custom-call(s32[2048]{0:T(1024)S(1)} %reshape.46.places, s32[3]{0:T(128)S(1)} %add_add_fusion.4.meta, bf16[512,128]{1,0:T(8,128)(2,1)S(1)} %collective-permute-done.12.x_ref, f32[1,128]{1,0:T(1,128)S(1)} %get-tuple-element.8.gain_ref, f32[1,128]{1,0:T(1,128)S(1)} %get-tuple-element.7.gate_ref, ...), custom_call_target="tpu_custom_call" | custom-call | flops 134217728 | bytes 4194304 | tf_op jit(solution)/shard_map/pallas_call | solution.py:111
  129.5 1.3 collective-permute-start.13
  130.9 5.5 %collective-permute-done.13.x_ref = bf16[512,128]{1,0:T(8,128)(2,1)S(1)} collective-permute-done((bf16[512,128]{1,0:T(8,128)(2,1)S(1)}, bf16[512,128]{1,0:T(8,128)(2,1)S(1)}, u32[]{:S(2)}, u32[]{:S(2)}) %collective-permute-start.13) | collective-permute-done | bytes 131104 | tf_op jit(solution)/shard_map/ppermute | solution.py:200
  136.4 5.2 %shard_map.69 = bf16[512,128]{1,0:T(8,128)(2,1)S(1)} custom-call(s32[2048]{0:T(1024)S(1)} %reshape.46.places, s32[3]{0:T(128)S(1)} %add_add_fusion.5.meta, bf16[512,128]{1,0:T(8,128)(2,1)S(1)} %collective-permute-done.13.x_ref, f32[1,128]{1,0:T(1,128)S(1)} %get-tuple-element.8.gain_ref, f32[1,128]{1,0:T(1,128)S(1)} %get-tuple-element.7.gate_ref, ...), custom_call_target="tpu_custom_call" | custom-call | flops 134217728 | bytes 4194304 | tf_op jit(solution)/shard_map/pallas_call | solution.py:111
  141.6 1.3 collective-permute-start.14
  142.9 5.5 %collective-permute-done.14 = bf16[512,128]{1,0:T(8,128)(2,1)S(1)} collective-permute-done((bf16[512,128]{1,0:T(8,128)(2,1)S(1)}, bf16[512,128]{1,0:T(8,128)(2,1)S(1)}, u32[]{:S(2)}, u32[]{:S(2)}) %collective-permute-start.14) | collective-permute-done | bytes 131104 | tf_op jit(solution)/shard_map/ppermute | solution.py:200
  148.5 5.2 %shard_map.70 = bf16[7,512,128]{2,1,0:T(8,128)(2,1)S(1)} fusion(bf16[7,512,128]{2,1,0:T(8,128)(2,1)S(1)} %bitcast_dynamic-update-slice_fusion.1, s32[2048]{0:T(1024)S(1)} %reshape.46.places, s32[3]{0:T(128)S(1)} %add_add_fusion.6, bf16[512,128]{1,0:T(8,128)(2,1)S(1)} %collective-permute-done.14, f32[1,128]{1,0:T(1,128)S(1)} %get-tuple-element.8.gain_ref, ...), kind=kCustom, calls=%fused_computation.4 | custom fusion | flops 134217728 | bytes 4466176 | tf_op jit(solution)/shard_map/pallas_call | solution.py:111
  153.8 23.8 %all_to_all.21 = bf16[16,4,32,128]{3,2,1,0:T(8,128)(2,1)S(1)} all-to-all(bf16[16,4,32,128]{3,2,1,0:T(8,128)(2,1)S(1)} %copy.31), channel_id=1, replica_groups=mesh['section'=4,'z'=8,'yh'=2,'yl'=2,'core'=2] {'z','yh'}, dimensions={0} | all-to-all | bytes 1048576 | tf_op jit(solution)/shard_map/all_to_all | solution.py:205
  177.9 1.0 reshape.55
  (52 shorter events, 10.4 us)
Async XLA Ops:
  0.0 36.1 %copy-start = (s32[1,16,512,16]{2,3,1,0:T(8,128)S(1)}, s32[1,16,512,16]{2,3,1,0:T(8,128)}, u32[]{:S(2)}) copy-start(s32[1,16,512,16]{2,3,1,0:T(8,128)} %param.8) | copy-start | bytes 1572868
  32.5 22.0 %all-to-all-start.2 = ((bf16[16,128,128]{2,1,0:T(8,128)(2,1)}), bf16[16,128,128]{2,1,0:T(8,128)(2,1)S(1)}, u32[]{:S(2)}, u32[]{:S(2)}) async-start(bf16[16,128,128]{2,1,0:T(8,128)(2,1)} %get-tuple-element.5), calls=%async_computation.2 | async-start | bytes 1048576 | tf_op jit(solution)/shard_map/all_to_all | solution.py:160
  36.0 1.5 copy-start.1
  36.3 0.7 copy-start.2
  38.4 24.3 %collective-permute-start = (bf16[2048,128]{1,0:T(8,128)(2,1)S(1)}, bf16[2048,128]{1,0:T(8,128)(2,1)S(1)}, u32[]{:S(2)}, u32[]{:S(2)}) collective-permute-start(bf16[2048,128]{1,0:T(8,128)(2,1)S(1)} %bitcast.68), channel_id=1, source_target_pairs={{0,2},{2,0},{1,3},{3,1},{4,6},{6,4},{5,7},{7,5},{8,10},{10,8},{9,1... | collective-permute-start | bytes 1572872 | tf_op jit(solution)/shard_map/ppermute | solution.py:133
  54.4 20.5 %all-to-all-start = ((bf16[16,32,128]{2,1,0:T(8,128)(2,1)}), bf16[16,32,128]{2,1,0:T(8,128)(2,1)S(1)}, u32[]{:S(2)}, u32[]{:S(2)}) async-start(bf16[16,32,128]{2,1,0:T(8,128)(2,1)} %bitcast.67), calls=%async_computation | async-start | bytes 262144 | tf_op jit(solution)/shard_map/all_to_all | solution.py:154
  57.9 14.4 %collective-permute-start.3 = (bf16[2048,128]{1,0:T(8,128)(2,1)S(1)}, bf16[2048,128]{1,0:T(8,128)(2,1)S(1)}, u32[]{:S(2)}, u32[]{:S(2)}) collective-permute-start(bf16[2048,128]{1,0:T(8,128)(2,1)S(1)} %bitcast.77), channel_id=1, source_target_pairs={{0,2},{2,0},{1,3},{3,1},{4,6},{6,4},{5,7},{7,5},{8,10},{10,8},{9,1... | collective-permute-start | bytes 1572872 | tf_op jit(solution)/shard_map/ppermute | solution.py:133
  62.2 13.4 %collective-permute-start.1 = (bf16[2048,128]{1,0:T(8,128)(2,1)S(1)}, bf16[2048,128]{1,0:T(8,128)(2,1)S(1)}, u32[]{:S(2)}, u32[]{:S(2)}) collective-permute-start(bf16[2048,128]{1,0:T(8,128)(2,1)S(1)} %bitcast.69), channel_id=1, source_target_pairs={{0,1},{1,0},{2,3},{3,2},{4,5},{5,4},{6,7},{7,6},{8,9},{9,8},{10,11... | collective-permute-start | bytes 1572872 | tf_op jit(solution)/shard_map/ppermute | solution.py:133
  62.2 14.0 %collective-permute-start.4 = (bf16[2048,128]{1,0:T(8,128)(2,1)S(1)}, bf16[2048,128]{1,0:T(8,128)(2,1)}, u32[]{:S(2)}, u32[]{:S(2)}) collective-permute-start(bf16[2048,128]{1,0:T(8,128)(2,1)S(1)} %bitcast.78), channel_id=1, source_target_pairs={{0,1},{1,0},{2,3},{3,2},{4,5},{5,4},{6,7},{7,6},{8,9},{9,8},{10,11... | collective-permute-start | bytes 1572872 | tf_op jit(solution)/shard_map/ppermute | solution.py:133
  62.7 17.2 %collective-permute-start.2 = (bf16[2048,128]{1,0:T(8,128)(2,1)S(1)}, bf16[2048,128]{1,0:T(8,128)(2,1)}, u32[]{:S(2)}, u32[]{:S(2)}) collective-permute-start(bf16[2048,128]{1,0:T(8,128)(2,1)S(1)} %collective-permute-done.rest_1_), channel_id=1, source_target_pairs={{0,1},{1,0},{2,3},{3,2},{4,5},{5,4},{6,7},{7,6},{8,9},{9,8},{10,11... | collective-permute-start | bytes 1572872 | tf_op jit(solution)/shard_map/ppermute | solution.py:133
  72.4 7.5 %collective-permute-start.5 = (bf16[2048,128]{1,0:T(8,128)(2,1)S(1)}, bf16[2048,128]{1,0:T(8,128)(2,1)}, u32[]{:S(2)}, u32[]{:S(2)}) collective-permute-start(bf16[2048,128]{1,0:T(8,128)(2,1)S(1)} %collective-permute-done.3.rest_5_), channel_id=1, source_target_pairs={{0,1},{1,0},{2,3},{3,2},{4,5},{5,4},{6,7},{7,6},{8,9},{9,8},{10,11... | collective-permute-start | bytes 1572872 | tf_op jit(solution)/shard_map/ppermute | solution.py:133
  74.9 7.1 %collective-permute-start.6 = (bf16[512,128]{1,0:T(8,128)(2,1)S(1)}, bf16[512,128]{1,0:T(8,128)(2,1)S(1)}, u32[]{:S(2)}, u32[]{:S(2)}) collective-permute-start(bf16[512,128]{1,0:T(8,128)(2,1)S(1)} %bitcast.86), channel_id=1, source_target_pairs={{64,0},{65,1},{66,2},{67,3},{68,4},{69,5},{70,6},{71,7},{72,8},{73... | collective-permute-start | bytes 393224 | tf_op jit(solution)/shard_map/ppermute | solution.py:157
  75.6 14.8 %collective-permute-start.8 = (bf16[512,128]{1,0:T(8,128)(2,1)S(1)}, bf16[512,128]{1,0:T(8,128)(2,1)S(1)}, u32[]{:S(2)}, u32[]{:S(2)}) collective-permute-start(bf16[512,128]{1,0:T(8,128)(2,1)S(1)} %bitcast.87), channel_id=1, source_target_pairs={{128,0},{129,1},{130,2},{131,3},{132,4},{133,5},{134,6},{135,7},{1... | collective-permute-start | bytes 393224 | tf_op jit(solution)/shard_map/ppermute | solution.py:157
  76.2 21.8 %collective-permute-start.10 = (bf16[512,128]{1,0:T(8,128)(2,1)S(1)}, bf16[512,128]{1,0:T(8,128)(2,1)S(1)}, u32[]{:S(2)}, u32[]{:S(2)}) collective-permute-start(bf16[512,128]{1,0:T(8,128)(2,1)S(1)} %bitcast.88), channel_id=1, source_target_pairs={{192,0},{193,1},{194,2},{195,3},{196,4},{197,5},{198,6},{199,7},{2... | collective-permute-start | bytes 393224 | tf_op jit(solution)/shard_map/ppermute | solution.py:157
  80.7 7.5 %collective-permute-start.7 = (bf16[512,128]{1,0:T(8,128)(2,1)S(1)}, bf16[512,128]{1,0:T(8,128)(2,1)S(1)}, u32[]{:S(2)}, u32[]{:S(2)}) collective-permute-start(bf16[512,128]{1,0:T(8,128)(2,1)S(1)} %shard_map.64), channel_id=1, source_target_pairs={{0,64},{64,128},{128,192},{1,65},{65,129},{129,193},{2,66},{66,130... | collective-permute-start | bytes 393224 | tf_op jit(solution)/shard_map/ppermute | solution.py:200
  89.0 6.9 %collective-permute-start.9 = (bf16[512,128]{1,0:T(8,128)(2,1)S(1)}, bf16[512,128]{1,0:T(8,128)(2,1)S(1)}, u32[]{:S(2)}, u32[]{:S(2)}) collective-permute-start(bf16[512,128]{1,0:T(8,128)(2,1)S(1)} %shard_map.65), channel_id=1, source_target_pairs={{0,64},{64,128},{128,192},{1,65},{65,129},{129,193},{2,66},{66,130... | collective-permute-start | bytes 393224 | tf_op jit(solution)/shard_map/ppermute | solution.py:200
  96.7 15.6 %collective-permute-start.11 = (bf16[512,128]{1,0:T(8,128)(2,1)S(1)}, bf16[512,128]{1,0:T(8,128)(2,1)S(1)}, u32[]{:S(2)}, u32[]{:S(2)}) collective-permute-start(bf16[512,128]{1,0:T(8,128)(2,1)S(1)} %shard_map.66), channel_id=1, source_target_pairs={{0,64},{64,128},{128,192},{1,65},{65,129},{129,193},{2,66},{66,130... | collective-permute-start | bytes 393224 | tf_op jit(solution)/shard_map/ppermute | solution.py:200
  117.5 6.9 %collective-permute-start.12 = (bf16[512,128]{1,0:T(8,128)(2,1)S(1)}, bf16[512,128]{1,0:T(8,128)(2,1)S(1)}, u32[]{:S(2)}, u32[]{:S(2)}) collective-permute-start(bf16[512,128]{1,0:T(8,128)(2,1)S(1)} %shard_map.67), channel_id=1, source_target_pairs={{0,64},{64,128},{128,192},{1,65},{65,129},{129,193},{2,66},{66,130... | collective-permute-start | bytes 393224 | tf_op jit(solution)/shard_map/ppermute | solution.py:200
  129.5 6.9 %collective-permute-start.13 = (bf16[512,128]{1,0:T(8,128)(2,1)S(1)}, bf16[512,128]{1,0:T(8,128)(2,1)S(1)}, u32[]{:S(2)}, u32[]{:S(2)}) collective-permute-start(bf16[512,128]{1,0:T(8,128)(2,1)S(1)} %shard_map.68), channel_id=1, source_target_pairs={{0,64},{64,128},{128,192},{1,65},{65,129},{129,193},{2,66},{66,130... | collective-permute-start | bytes 393224 | tf_op jit(solution)/shard_map/ppermute | solution.py:200
  141.6 6.9 %collective-permute-start.14 = (bf16[512,128]{1,0:T(8,128)(2,1)S(1)}, bf16[512,128]{1,0:T(8,128)(2,1)S(1)}, u32[]{:S(2)}, u32[]{:S(2)}) collective-permute-start(bf16[512,128]{1,0:T(8,128)(2,1)S(1)} %shard_map.69), channel_id=1, source_target_pairs={{0,64},{64,128},{128,192},{1,65},{65,129},{129,193},{2,66},{66,130... | collective-permute-start | bytes 393224 | tf_op jit(solution)/shard_map/ppermute | solution.py:200

commit v2 on v1

--- a/solution.py
+++ b/solution.py
@@ -14,6 +14,8 @@
 SLOTS = 16
 SECTIONS = 4
 CHUNKS = 4
+DELAY = 2
+EARLY = 2
 GROUP = 8
 SPAN = SLOTS * KEY_BLOCK
 SCORE_FLOOR = -1e30
@@ -151,15 +153,15 @@
     mine = lax.dynamic_slice_in_dim(
         patches.reshape(tokens, HEADS, HEAD_DIM), section * chunk_tokens, chunk_tokens, 0
     ).transpose(1, 0, 2)
-    mine = lax.all_to_all(mine, OWNERS, 0, 0, tiled=True)
-    fresh = [mine.reshape(sources * chunk_tokens, HEAD_DIM)]
+    first = jnp.concatenate([by_head[0], mine], axis=1)
+    first = lax.all_to_all(first, OWNERS, 0, 0, tiled=True)
+    first, second = lax.optimization_barrier((first, by_head[1]))
+    k_parts = spread(first[:, :tokens].reshape(sources * tokens, HEAD_DIM))
+    fresh = [first[:, tokens:].reshape(sources * chunk_tokens, HEAD_DIM)]
     for c in range(1, CHUNKS):
         fresh.append(lax.ppermute(fresh[0], "section", [(c, 0)]))
-    tables = []
-    for which in range(2):
-        moved = lax.all_to_all(by_head[which], OWNERS, 0, 0, tiled=True)
-        tables.append(spread(moved.reshape(sources * tokens, HEAD_DIM)))
-    k_parts, v_parts = tables
+    second = lax.all_to_all(second, OWNERS, 0, 0, tiled=True)
+    v_parts = spread(second.reshape(sources * tokens, HEAD_DIM))
 
     query_blocks = patch_rows // QUERY_BLOCK
     lists = lax.dynamic_index_in_dim(block_lists[0], owner, 0, keepdims=False)
@@ -181,28 +183,45 @@
     gain = lax.dynamic_index_in_dim(query_gain.reshape(HEADS, HEAD_DIM), owner, 0)
     gate = lax.dynamic_index_in_dim(branch_gate.reshape(HEADS, HEAD_DIM), owner, 0)
 
-    steps = CHUNKS + SECTIONS - 1
+    def collected(chunks):
+        done = []
+        for c in chunks:
+            own = results[c]
+            for s in range(1, SECTIONS):
+                own = jnp.where(section == s, results[c + s * DELAY], own)
+            done.append(own.reshape(sources, chunk_tokens, HEAD_DIM))
+        return jnp.concatenate(done, axis=1)
+
+    steps = CHUNKS + (SECTIONS - 1) * DELAY
     results = []
-    received = None
+    sent = []
     for step in range(steps):
-        if step == 0:
-            x = fresh[0]
+        if step < DELAY:
+            x = fresh[step]
         elif step < CHUNKS:
-            x = jnp.where(section == 0, fresh[step], received)
+            x = jnp.where(section == 0, fresh[step], sent[step - DELAY])
         else:
-            x = received
-        chunk = step - section
+            x = sent[step - DELAY]
+        if step > 0:
+            x, results[-1] = lax.optimization_barrier((x, results[-1]))
+        chunk = step - section * DELAY
         active = ((chunk >= 0) & (chunk < CHUNKS)).astype(jnp.int32)
         meta = jnp.stack([active, jnp.clip(chunk, 0, CHUNKS - 1) * chunk_entries, count])
-        result = attend(places, meta, x, gain, gate, k_parts, v_parts)
-        results.append(result)
-        if step < steps - 1:
-            received = lax.ppermute(
-                result, "section", [(s, s + 1) for s in range(SECTIONS - 1)]
+        results.append(attend(places, meta, x, gain, gate, k_parts, v_parts))
+        if step + DELAY < steps:
+            sent.append(
+                lax.ppermute(
+                    results[-1], "section", [(s, s + 1) for s in range(SECTIONS - 1)]
+                )
             )
-    done = lax.dynamic_slice_in_dim(jnp.stack(results), section, CHUNKS, 0)
-    done = done.reshape(CHUNKS, sources, chunk_tokens, HEAD_DIM).transpose(1, 0, 2, 3)
-    done = lax.all_to_all(done, OWNERS, 0, 0, tiled=True)
+        if step == EARLY - 1 + (SECTIONS - 1) * DELAY:
+            early = collected(range(EARLY))
+            early, results[-1] = lax.optimization_barrier((early, results[-1]))
+            early = lax.all_to_all(early, OWNERS, 0, 0, tiled=True)
+    late = collected(range(EARLY, CHUNKS))
+    late, early = lax.optimization_barrier((late, early))
+    late = lax.all_to_all(late, OWNERS, 0, 0, tiled=True)
+    done = jnp.concatenate([early, late], axis=1)
     done = done.reshape(HEADS, micro_count, patch_rows, HEAD_DIM).transpose(1, 2, 0, 3)
     return done.reshape(1, micro_count, patch_rows, channels)
 

time: 180 us -> 183 us (1.017); the launches traced: 179 us -> 180 us
  waiting for transfers between devices: 67.5 us -> 35.5 us
  starting transfers between devices: 21.9 us -> 35.7 us
  Pallas kernels: 17.9 us -> 29 us
  other arithmetic: 10.3 us -> 15.1 us
  local copies, waits for them, and re-layouts: 7.46 us -> 9.53 us
    ppermute x6 -> x8, waiting for transfers between devices: 42.5 us -> 8.54 us  [local(): lax.ppermute(results[-1], 'section', [(s, s + 1) for s in range(SECTIONS...]
    pallas_call x6 -> x10, Pallas kernels: 17.9 us -> 29 us  [attend(): pl.pallas_call(functools.partial(attend_kernel, pieces=pieces, groups=que...]
    all_to_all x2, starting transfers between devices: 7.08 us -> 13 us  [the longest x1 9.38 us: local(): early = lax.all_to_all(early, OWNERS, 0, 0, tiled=True)]
    another operation x7 -> x9, other arithmetic: 4.84 us -> 10.2 us  [local(): jnp.stack([active, jnp.clip(chunk, 0, CHUNKS - 1) * chunk_entries, count])]
    ppermute x3, starting transfers between devices: 4.96 us -> 10.2 us  [local(): fresh.append(lax.ppermute(fresh[0], 'section', [(c, 0)]))]
    pallas_call x1 -> x0, other arithmetic: 5.2 us -> none  [attend(): pl.pallas_call(functools.partial(attend_kernel, pieces=pieces, groups=que...]
    select_n x3 -> x6, other arithmetic: 0.05 us -> 2.93 us  [the longest x4 1.98 us: collected(): own = jnp.where(section == s, results[c + s * DELAY], own)]
    ppermute x6 -> x8, starting transfers between devices: 7.75 us -> 10.5 us  [local(): lax.ppermute(results[-1], 'section', [(s, s + 1) for s in range(SECTIONS...]
  transfers between devices with their start and end apart: 17 -> 19, of which waited for: 8 -> 7; matrix products, arithmetic and copies ran while one was open for 4% -> 9% of each run, Pallas kernels for 1% -> 16%
where the time goes in v2:
time: 183 us; the launch traced here: 180 us
  blocking collectives  54.4 us (30%)
  starting transfers between devices  35.7 us (20%)
  waiting for transfers between devices  35.5 us (19%)
  Pallas kernels  29 us (16%)
  other arithmetic  15.1 us (8%)
  local copies, waits for them, and re-layouts  9.53 us (5%)
    all_to_all x1, blocking collectives, local(): first = lax.all_to_all(first, OWNERS, 0, 0, tiled=True)  33.3 us
    pallas_call x10, Pallas kernels, attend(): pl.pallas_call(functools.partial(attend_kernel, pieces=pieces, groups=que...  29 us
    all_to_all x1, blocking collectives, local(): late = lax.all_to_all(late, OWNERS, 0, 0, tiled=True)  21.1 us
    all_to_all x1, waiting for transfers between devices, local(): second = lax.all_to_all(second, OWNERS, 0, 0, tiled=True)  17 us
    ppermute x8, starting transfers between devices, local(): lax.ppermute(results[-1], 'section', [(s, s + 1) for s in range(SECTIONS...  10.5 us
    another operation x9, other arithmetic, local(): jnp.stack([active, jnp.clip(chunk, 0, CHUNKS - 1) * chunk_entries, count])  10.2 us
    ppermute x3, starting transfers between devices, local(): fresh.append(lax.ppermute(fresh[0], 'section', [(c, 0)]))  10.2 us
    all_to_all x1, starting transfers between devices, local(): early = lax.all_to_all(early, OWNERS, 0, 0, tiled=True)  9.38 us
  transfers between devices with their start and end apart: 19, of which 7 were waited for; matrix products, arithmetic and copies ran while one was open for 9% of the time, Pallas kernels for 16%

profile of v2, /device:TPU:6, one launch (start us, length us, event | category | flops | bytes accessed | tf_op | source)
XLA Modules:
  0.0 179.9 jit_solution(8758124544130403593)
XLA Ops:
  0.0 1.3 copy.24
  3.1 33.3 %all_to_all.20 = bf16[16,160,128]{2,1,0:T(8,128)(2,1)S(1)} all-to-all(bf16[16,160,128]{2,1,0:T(8,128)(2,1)S(1)} %pad_maximum_fusion), channel_id=1, replica_groups=mesh['section'=4,'z'=8,'yh'=2,'yl'=2,'core'=2] {'z','yh'}, dimensions={0} | all-to-all | bytes 1310720 | tf_op jit(solution)/shard_map/all_to_all | solution.py:157
  36.4 3.6 %all-to-all-start.1 = ((bf16[16,128,128]{2,1,0:T(8,128)(2,1)}), bf16[16,128,128]{2,1,0:T(8,128)(2,1)S(1)}, u32[]{:S(2)}, u32[]{:S(2)}) async-start(bf16[16,128,128]{2,1,0:T(8,128)(2,1)} %get-tuple-element.30), calls=%async_computation.1 | async-start | bytes 1048576 | tf_op jit(solution)/shard_map/all_to_all | solution.py:163
  40.8 17.0 %all-to-all-done.1 = bf16[16,128,128]{2,1,0:T(8,128)(2,1)S(1)} async-done(((bf16[16,128,128]{2,1,0:T(8,128)(2,1)}), bf16[16,128,128]{2,1,0:T(8,128)(2,1)S(1)}, u32[]{:S(2)}, u32[]{:S(2)}) %all-to-all-start.1) | async-done | bytes 524320 | tf_op jit(solution)/shard_map/all_to_all | solution.py:163
  59.4 9.3 %collective-permute-done.5.rest_5_ = bf16[2048,128]{1,0:T(8,128)(2,1)S(1)} collective-permute-done((bf16[2048,128]{1,0:T(8,128)(2,1)S(1)}, bf16[2048,128]{1,0:T(8,128)(2,1)S(1)}, u32[]{:S(2)}, u32[]{:S(2)}) %collective-permute-start.5) | collective-permute-done | bytes 524320 | tf_op jit(solution)/shard_map/ppermute | solution.py:135
  70.4 1.2 add_add_fusion.3.meta
  71.6 1.2 add_add_fusion.5.meta
  74.4 1.3 collective-permute-start.9
  77.3 1.3 collective-permute-start.10
  78.6 1.2 add_add_fusion.2.meta
  79.8 1.2 add_add_fusion.6.meta
  81.0 8.2 %collective-permute-start = (bf16[512,128]{1,0:T(8,128)(2,1)S(1)}, bf16[512,128]{1,0:T(8,128)(2,1)S(1)}, u32[]{:S(2)}, u32[]{:S(2)}) collective-permute-start(bf16[512,128]{1,0:T(8,128)(2,1)S(1)} %bitcast.89), channel_id=1, source_target_pairs={{192,0},{193,1},{194,2},{195,3},{196,4},{197,5},{198,6},{199,7},{2... | collective-permute-start | bytes 393224 | tf_op jit(solution)/shard_map/ppermute | solution.py:162
  90.6 1.3 collective-permute-start.8
  93.7 1.3 collective-permute-start.12
  95.0 3.1 %collective-permute-done.8 = bf16[512,128]{1,0:T(8,128)(2,1)S(1)} collective-permute-done((bf16[512,128]{1,0:T(8,128)(2,1)S(1)}, bf16[512,128]{1,0:T(8,128)(2,1)S(1)}, u32[]{:S(2)}, u32[]{:S(2)}) %collective-permute-start.8) | collective-permute-done | bytes 131104 | tf_op jit(solution)/shard_map/ppermute | solution.py:213
  99.0 1.3 collective-permute-start.11
  100.3 1.2 add_add_fusion.1.meta
  101.5 1.2 add_add_fusion.7.meta
  104.3 1.3 collective-permute-start.14
  105.9 1.7 shard_map.69
  107.6 1.3 collective-permute-start.13
  108.9 1.2 add_add_fusion.meta
  110.1 1.2 add_add_fusion.8
  111.4 5.0 %collective-permute-done.14.x_ref = bf16[512,128]{1,0:T(8,128)(2,1)} collective-permute-done((bf16[512,128]{1,0:T(8,128)(2,1)S(1)}, bf16[512,128]{1,0:T(8,128)(2,1)}, u32[]{:S(2)}, u32[]{:S(2)}) %collective-permute-start.14) | collective-permute-done | bytes 131104 | tf_op jit(solution)/shard_map/ppermute | solution.py:213
  117.0 6.1 %shard_map.70 = bf16[512,128]{1,0:T(8,128)(2,1)} custom-call(s32[2048]{0:T(1024)S(1)} %reshape.55.places, s32[3]{0:T(128)S(1)} %copy-done.10, bf16[512,128]{1,0:T(8,128)(2,1)} %collective-permute-done.14.x_ref, f32[1,128]{1,0:T(1,128)S(1)} %get-tuple-element.58.gain_ref, f32[1,128]{1,0:T(1,128)S(1)} %get-tuple-element.57.gate_ref, ...), custom_call_target="tpu_custom_call" | custom-call | flops 134217728 | bytes 4194304 | tf_op jit(solution)/shard_map/pallas_call | solution.py:113
  123.1 1.4 collective-permute-start.16
  124.6 6.3 %shard_map.71 = bf16[512,128]{1,0:T(8,128)(2,1)} custom-call(s32[2048]{0:T(1024)S(1)} %reshape.55.places, s32[3]{0:T(128)S(1)} %copy-done.12, bf16[512,128]{1,0:T(8,128)(2,1)} %collective-permute-done.13.x_ref, f32[1,128]{1,0:T(1,128)S(1)} %get-tuple-element.58.gain_ref, f32[1,128]{1,0:T(1,128)S(1)} %get-tuple-element.57.gate_ref, ...), custom_call_target="tpu_custom_call" | custom-call | flops 134217728 | bytes 4194304 | tf_op jit(solution)/shard_map/pallas_call | solution.py:113
  130.9 1.3 collective-permute-start.15
  134.8 9.4 %all-to-all-start.2 = ((bf16[16,64,128]{2,1,0:T(8,128)(2,1)}), bf16[16,64,128]{2,1,0:T(8,128)(2,1)}, u32[]{:S(2)}, u32[]{:S(2)}) async-start(bf16[16,64,128]{2,1,0:T(8,128)(2,1)} %pad_maximum_fusion.2), calls=%async_computation.2 | async-start | bytes 524288 | tf_op jit(solution)/shard_map/all_to_all | solution.py:220
  144.9 5.4 %shard_map.72 = bf16[512,128]{1,0:T(8,128)(2,1)S(1)} custom-call(s32[2048]{0:T(1024)S(1)} %reshape.55.places, s32[3]{0:T(128)S(1)} %copy-done.6, bf16[512,128]{1,0:T(8,128)(2,1)} %collective-permute-done.16.x_ref, f32[1,128]{1,0:T(1,128)S(1)} %get-tuple-element.58.gain_ref, f32[1,128]{1,0:T(1,128)S(1)} %get-tuple-element.57.gate_ref, ...), custom_call_target="tpu_custom_call" | custom-call | flops 134217728 | bytes 4194304 | tf_op jit(solution)/shard_map/pallas_call | solution.py:113
  150.4 5.4 %shard_map.73 = bf16[512,128]{1,0:T(8,128)(2,1)S(1)} custom-call(s32[2048]{0:T(1024)S(1)} %reshape.55.places, s32[3]{0:T(128)S(1)} %copy-done.5, bf16[512,128]{1,0:T(8,128)(2,1)} %collective-permute-done.15.x_ref, f32[1,128]{1,0:T(1,128)S(1)} %get-tuple-element.58.gain_ref, f32[1,128]{1,0:T(1,128)S(1)} %get-tuple-element.57.gate_ref, ...), custom_call_target="tpu_custom_call" | custom-call | flops 134217728 | bytes 4194304 | tf_op jit(solution)/shard_map/pallas_call | solution.py:113
  156.5 21.1 %all_to_all.21 = bf16[16,64,128]{2,1,0:T(8,128)(2,1)S(1)} all-to-all(bf16[16,64,128]{2,1,0:T(8,128)(2,1)S(1)} %pad_maximum_fusion.3), channel_id=1, replica_groups=mesh['section'=4,'z'=8,'yh'=2,'yl'=2,'core'=2] {'z','yh'}, dimensions={0} | all-to-all | bytes 524288 | tf_op jit(solution)/shard_map/all_to_all | solution.py:223
  (90 shorter events, 21.8 us)
Async XLA Ops:
  0.0 58.5 %copy-start = (s32[1,16,512,16]{2,3,1,0:T(8,128)S(1)}, s32[1,16,512,16]{2,3,1,0:T(8,128)}, u32[]{:S(2)}) copy-start(s32[1,16,512,16]{2,3,1,0:T(8,128)} %param.8) | copy-start | bytes 1572868
  0.0 1.4 copy-start.15
  36.4 3.7 %copy-start.14 = (bf16[16,160,128]{2,1,0:T(8,128)(2,1)}, bf16[16,160,128]{2,1,0:T(8,128)(2,1)S(1)}, u32[]{:S(2)}) copy-start(bf16[16,160,128]{2,1,0:T(8,128)(2,1)S(1)} %all_to_all.20) | copy-start | bytes 1966084
  36.4 21.5 %all-to-all-start.1 = ((bf16[16,128,128]{2,1,0:T(8,128)(2,1)}), bf16[16,128,128]{2,1,0:T(8,128)(2,1)S(1)}, u32[]{:S(2)}, u32[]{:S(2)}) async-start(bf16[16,128,128]{2,1,0:T(8,128)(2,1)} %get-tuple-element.30), calls=%async_computation.1 | async-start | bytes 1048576 | tf_op jit(solution)/shard_map/all_to_all | solution.py:163
  40.0 29.1 %copy-start.16 = (s32[1,16]{1,0:T(1,128)S(1)}, s32[1,16]{1,0:T(1,128)}, u32[]{:S(2)}) copy-start(s32[1,16]{1,0:T(1,128)} %param.9) | copy-start | bytes 196
  40.1 18.8 %collective-permute-start.2 = (bf16[2048,128]{1,0:T(8,128)(2,1)S(1)}, bf16[2048,128]{1,0:T(8,128)(2,1)S(1)}, u32[]{:S(2)}, u32[]{:S(2)}) collective-permute-start(bf16[2048,128]{1,0:T(8,128)(2,1)S(1)} %bitcast.74), channel_id=1, source_target_pairs={{0,2},{2,0},{1,3},{3,1},{4,6},{6,4},{5,7},{7,5},{8,10},{10,8},{9,1... | collective-permute-start | bytes 1572872 | tf_op jit(solution)/shard_map/ppermute | solution.py:135
  57.9 10.9 %collective-permute-start.5 = (bf16[2048,128]{1,0:T(8,128)(2,1)S(1)}, bf16[2048,128]{1,0:T(8,128)(2,1)S(1)}, u32[]{:S(2)}, u32[]{:S(2)}) collective-permute-start(bf16[2048,128]{1,0:T(8,128)(2,1)S(1)} %bitcast.62), channel_id=1, source_target_pairs={{0,2},{2,0},{1,3},{3,1},{4,6},{6,4},{5,7},{7,5},{8,10},{10,8},{9,1... | collective-permute-start | bytes 1572872 | tf_op jit(solution)/shard_map/ppermute | solution.py:135
  58.7 17.0 %collective-permute-start.3 = (bf16[2048,128]{1,0:T(8,128)(2,1)S(1)}, bf16[2048,128]{1,0:T(8,128)(2,1)S(1)}, u32[]{:S(2)}, u32[]{:S(2)}) collective-permute-start(bf16[2048,128]{1,0:T(8,128)(2,1)S(1)} %bitcast.75), channel_id=1, source_target_pairs={{0,1},{1,0},{2,3},{3,2},{4,5},{5,4},{6,7},{7,6},{8,9},{9,8},{10,11... | collective-permute-start | bytes 1572872 | tf_op jit(solution)/shard_map/ppermute | solution.py:135
  58.8 17.6 %collective-permute-start.4 = (bf16[2048,128]{1,0:T(8,128)(2,1)S(1)}, bf16[2048,128]{1,0:T(8,128)(2,1)}, u32[]{:S(2)}, u32[]{:S(2)}) collective-permute-start(bf16[2048,128]{1,0:T(8,128)(2,1)S(1)} %collective-permute-done.2.rest_1_), channel_id=1, source_target_pairs={{0,1},{1,0},{2,3},{3,2},{4,5},{5,4},{6,7},{7,6},{8,9},{9,8},{10,11... | collective-permute-start | bytes 1572872 | tf_op jit(solution)/shard_map/ppermute | solution.py:135
  59.3 17.1 %collective-permute-start.6 = (bf16[2048,128]{1,0:T(8,128)(2,1)S(1)}, bf16[2048,128]{1,0:T(8,128)(2,1)}, u32[]{:S(2)}, u32[]{:S(2)}) collective-permute-start(bf16[2048,128]{1,0:T(8,128)(2,1)S(1)} %bitcast.63), channel_id=1, source_target_pairs={{0,1},{1,0},{2,3},{3,2},{4,5},{5,4},{6,7},{7,6},{8,9},{9,8},{10,11... | collective-permute-start | bytes 1572872 | tf_op jit(solution)/shard_map/ppermute | solution.py:135
  68.8 7.7 %collective-permute-start.7 = (bf16[2048,128]{1,0:T(8,128)(2,1)S(1)}, bf16[2048,128]{1,0:T(8,128)(2,1)}, u32[]{:S(2)}, u32[]{:S(2)}) collective-permute-start(bf16[2048,128]{1,0:T(8,128)(2,1)S(1)} %collective-permute-done.5.rest_5_), channel_id=1, source_target_pairs={{0,1},{1,0},{2,3},{3,2},{4,5},{5,4},{6,7},{7,6},{8,9},{9,8},{10,11... | collective-permute-start | bytes 1572872 | tf_op jit(solution)/shard_map/ppermute | solution.py:135
  74.4 17.5 %collective-permute-start.9 = (bf16[512,128]{1,0:T(8,128)(2,1)S(1)}, bf16[512,128]{1,0:T(8,128)(2,1)}, u32[]{:S(2)}, u32[]{:S(2)}) collective-permute-start(bf16[512,128]{1,0:T(8,128)(2,1)S(1)} %bitcast.86), channel_id=1, source_target_pairs={{128,0},{129,1},{130,2},{131,3},{132,4},{133,5},{134,6},{135,7},{1... | collective-permute-start | bytes 393224 | tf_op jit(solution)/shard_map/ppermute | solution.py:162
  75.8 13.4 %collective-permute-start.1 = (bf16[512,128]{1,0:T(8,128)(2,1)S(1)}, bf16[512,128]{1,0:T(8,128)(2,1)S(1)}, u32[]{:S(2)}, u32[]{:S(2)}) collective-permute-start(bf16[512,128]{1,0:T(8,128)(2,1)S(1)} %bitcast.87), channel_id=1, source_target_pairs={{64,0},{65,1},{66,2},{67,3},{68,4},{69,5},{70,6},{71,7},{72,8},{73... | collective-permute-start | bytes 393224 | tf_op jit(solution)/shard_map/ppermute | solution.py:162
  77.3 13.4 %copy-start.1 = (bf16[512,128]{1,0:T(8,128)(2,1)}, bf16[512,128]{1,0:T(8,128)(2,1)S(1)}, u32[]{:S(2)}) copy-start(bf16[512,128]{1,0:T(8,128)(2,1)S(1)} %shard_map.64) | copy-start | bytes 393220
  77.3 14.7 %collective-permute-start.10 = (bf16[512,128]{1,0:T(8,128)(2,1)S(1)}, bf16[512,128]{1,0:T(8,128)(2,1)}, u32[]{:S(2)}, u32[]{:S(2)}) collective-permute-start(bf16[512,128]{1,0:T(8,128)(2,1)S(1)} %shard_map.64), channel_id=1, source_target_pairs={{0,64},{64,128},{128,192},{1,65},{65,129},{129,193},{2,66},{66,130... | collective-permute-start | bytes 393224 | tf_op jit(solution)/shard_map/ppermute | solution.py:213
  81.0 11.9 %copy-start.7 = (s32[3]{0:T(128)S(1)}, s32[3]{0:T(128)}, u32[]{:S(2)}) copy-start(s32[3]{0:T(128)} %add_add_fusion.5.meta) | copy-start | bytes 40
  81.0 14.1 %collective-permute-start = (bf16[512,128]{1,0:T(8,128)(2,1)S(1)}, bf16[512,128]{1,0:T(8,128)(2,1)S(1)}, u32[]{:S(2)}, u32[]{:S(2)}) collective-permute-start(bf16[512,128]{1,0:T(8,128)(2,1)S(1)} %bitcast.89), channel_id=1, source_target_pairs={{192,0},{193,1},{194,2},{195,3},{196,4},{197,5},{198,6},{199,7},{2... | collective-permute-start | bytes 393224 | tf_op jit(solution)/shard_map/ppermute | solution.py:162
  90.6 3.1 %copy-start.3 = (bf16[512,128]{1,0:T(8,128)(2,1)}, bf16[512,128]{1,0:T(8,128)(2,1)S(1)}, u32[]{:S(2)}) copy-start(bf16[512,128]{1,0:T(8,128)(2,1)S(1)} %shard_map.65) | copy-start | bytes 393220
  90.6 7.5 %collective-permute-start.8 = (bf16[512,128]{1,0:T(8,128)(2,1)S(1)}, bf16[512,128]{1,0:T(8,128)(2,1)S(1)}, u32[]{:S(2)}, u32[]{:S(2)}) collective-permute-start(bf16[512,128]{1,0:T(8,128)(2,1)S(1)} %shard_map.65), channel_id=1, source_target_pairs={{0,64},{64,128},{128,192},{1,65},{65,129},{129,193},{2,66},{66,130... | collective-permute-start | bytes 393224 | tf_op jit(solution)/shard_map/ppermute | solution.py:213
  92.9 5.3 %copy-start.11 = (s32[3]{0:T(128)S(1)}, s32[3]{0:T(128)}, u32[]{:S(2)}) copy-start(s32[3]{0:T(128)} %add_add_fusion.2.meta) | copy-start | bytes 40
  93.7 8.9 %collective-permute-start.12 = (bf16[512,128]{1,0:T(8,128)(2,1)S(1)}, bf16[512,128]{1,0:T(8,128)(2,1)}, u32[]{:S(2)}, u32[]{:S(2)}) collective-permute-start(bf16[512,128]{1,0:T(8,128)(2,1)S(1)} %shard_map.66), channel_id=1, source_target_pairs={{0,64},{64,128},{128,192},{1,65},{65,129},{129,193},{2,66},{66,130... | collective-permute-start | bytes 393224 | tf_op jit(solution)/shard_map/ppermute | solution.py:213
  99.0 7.0 %collective-permute-start.11 = (bf16[512,128]{1,0:T(8,128)(2,1)S(1)}, bf16[512,128]{1,0:T(8,128)(2,1)}, u32[]{:S(2)}, u32[]{:S(2)}) collective-permute-start(bf16[512,128]{1,0:T(8,128)(2,1)S(1)} %shard_map.67), channel_id=1, source_target_pairs={{0,64},{64,128},{128,192},{1,65},{65,129},{129,193},{2,66},{66,130... | collective-permute-start | bytes 393224 | tf_op jit(solution)/shard_map/ppermute | solution.py:213
  103.3 2.7 %copy-start.13 = (s32[3]{0:T(128)S(1)}, s32[3]{0:T(128)}, u32[]{:S(2)}) copy-start(s32[3]{0:T(128)} %add_add_fusion.1.meta) | copy-start | bytes 40
  104.3 12.0 %collective-permute-start.14 = (bf16[512,128]{1,0:T(8,128)(2,1)S(1)}, bf16[512,128]{1,0:T(8,128)(2,1)}, u32[]{:S(2)}, u32[]{:S(2)}) collective-permute-start(bf16[512,128]{1,0:T(8,128)(2,1)S(1)} %shard_map.68), channel_id=1, source_target_pairs={{0,64},{64,128},{128,192},{1,65},{65,129},{129,193},{2,66},{66,130... | collective-permute-start | bytes 393224 | tf_op jit(solution)/shard_map/ppermute | solution.py:213
  107.6 17.0 %collective-permute-start.13 = (bf16[512,128]{1,0:T(8,128)(2,1)}, bf16[512,128]{1,0:T(8,128)(2,1)}, u32[]{:S(2)}, u32[]{:S(2)}) collective-permute-start(bf16[512,128]{1,0:T(8,128)(2,1)} %shard_map.69), channel_id=1, source_target_pairs={{0,64},{64,128},{128,192},{1,65},{65,129},{129,193},{2,66},{66,130... | collective-permute-start | bytes 393224 | tf_op jit(solution)/shard_map/ppermute | solution.py:213
  116.9 7.7 %copy-start.12 = (s32[3]{0:T(128)S(1)}, s32[3]{0:T(128)}, u32[]{:S(2)}) copy-start(s32[3]{0:T(128)} %add_add_fusion.meta) | copy-start | bytes 40
  123.1 9.1 %copy-start.4 = (bf16[512,128]{1,0:T(8,128)(2,1)S(1)}, bf16[512,128]{1,0:T(8,128)(2,1)}, u32[]{:S(2)}) copy-start(bf16[512,128]{1,0:T(8,128)(2,1)} %copy-done.3) | copy-start | bytes 393220
  123.1 10.1 %copy-start.2 = (bf16[512,128]{1,0:T(8,128)(2,1)S(1)}, bf16[512,128]{1,0:T(8,128)(2,1)}, u32[]{:S(2)}) copy-start(bf16[512,128]{1,0:T(8,128)(2,1)} %copy-done.1) | copy-start | bytes 393220
  123.1 21.1 %collective-permute-start.16 = (bf16[512,128]{1,0:T(8,128)(2,1)}, bf16[512,128]{1,0:T(8,128)(2,1)}, u32[]{:S(2)}, u32[]{:S(2)}) collective-permute-start(bf16[512,128]{1,0:T(8,128)(2,1)} %shard_map.70), channel_id=1, source_target_pairs={{0,64},{64,128},{128,192},{1,65},{65,129},{129,193},{2,66},{66,130... | collective-permute-start | bytes 393224 | tf_op jit(solution)/shard_map/ppermute | solution.py:213
  130.9 19.5 %collective-permute-start.15 = (bf16[512,128]{1,0:T(8,128)(2,1)}, bf16[512,128]{1,0:T(8,128)(2,1)}, u32[]{:S(2)}, u32[]{:S(2)}) collective-permute-start(bf16[512,128]{1,0:T(8,128)(2,1)} %shard_map.71), channel_id=1, source_target_pairs={{0,64},{64,128},{128,192},{1,65},{65,129},{129,193},{2,66},{66,130... | collective-permute-start | bytes 393224 | tf_op jit(solution)/shard_map/ppermute | solution.py:213
  134.8 21.7 %all-to-all-start.2 = ((bf16[16,64,128]{2,1,0:T(8,128)(2,1)}), bf16[16,64,128]{2,1,0:T(8,128)(2,1)}, u32[]{:S(2)}, u32[]{:S(2)}) async-start(bf16[16,64,128]{2,1,0:T(8,128)(2,1)} %pad_maximum_fusion.2), calls=%async_computation.2 | async-start | bytes 524288 | tf_op jit(solution)/shard_map/all_to_all | solution.py:220
  144.9 5.5 %copy-start.5 = (s32[3]{0:T(128)S(1)}, s32[3]{0:T(128)}, u32[]{:S(2)}) copy-start(s32[3]{0:T(128)} %get-tuple-element.56.meta) | copy-start | bytes 40
  (4 other events, 2.6 us)

commit v3 on v1

v3 whole, which is shorter than its diff:
```python
import functools

import jax
import jax.numpy as jnp
from jax import lax
from jax.experimental import pallas as pl
from jax.experimental.pallas import tpu as pltpu
from jax.sharding import Mesh, PartitionSpec as P

HEADS = 16
HEAD_DIM = 128
QUERY_BLOCK = 16
KEY_BLOCK = 32
SLOTS = 16
SECTIONS = 4
CHUNKS = 4
DELAY = 2
GROUP = 16
SPAN = SLOTS * KEY_BLOCK
SCORE_FLOOR = -1e30

OWNERS = ("z", "yh")


def gather_kernel(*refs, pieces):
    tables = refs[2 * pieces : 2 * pieces + 2]
    sems = refs[-1]
    copies = []
    for which in range(2):
        for p in range(pieces):
            part = refs[which * pieces + p]
            sources, tokens = part.shape[:2]
            copies.append(
                pltpu.make_async_copy(
                    part, tables[which].at[pl.ds(p * sources, sources)], sems.at[which, p]
                )
            )
    for copy in copies:
        copy.start()
    for copy in copies:
        copy.wait()


def gathered(k_parts, v_parts):
    pieces = len(k_parts)
    sources, tokens, width = k_parts[0].shape
    table = jax.ShapeDtypeStruct((pieces * sources, tokens, width), jnp.bfloat16)
    vmem = pl.BlockSpec(memory_space=pltpu.VMEM)
    k_tab, v_tab = pl.pallas_call(
        functools.partial(gather_kernel, pieces=pieces),
        out_shape=(table, table),
        in_specs=[pl.BlockSpec(memory_space=pl.ANY)] * (2 * pieces),
        out_specs=(vmem, vmem),
        scratch_shapes=[pltpu.SemaphoreType.DMA((2, pieces))],
        compiler_params=pltpu.CompilerParams(vmem_limit_bytes=24 * 1024 * 1024),
    )(*k_parts, *v_parts)
    rows = pieces * sources * tokens
    return k_tab.reshape(rows, width), v_tab.reshape(rows, width)


def attend_kernel(places, info, *rest, step, fresh, received):
    refs = list(rest)
    fresh_ref = refs.pop(0) if fresh else None
    received_ref = refs.pop(0) if received else None
    gain_ref, gate_ref, k_tab, v_tab = refs[:4]
    out_ref, done_ref = refs[-2:]
    section = info[0]
    chunk = step - section * DELAY
    live_keys = info[1] * KEY_BLOCK
    rows = out_ref.shape[0]
    chunk_tokens = done_ref.shape[1] // CHUNKS
    group_rows = GROUP * QUERY_BLOCK
    group_sources = group_rows // chunk_tokens

    @pl.when((chunk >= 0) & (chunk < CHUNKS))
    def _():
        base = chunk * (rows // QUERY_BLOCK * SLOTS)
        token0 = pl.multiple_of(chunk * chunk_tokens, chunk_tokens)

        def one_group(index, carry):
            row0 = pl.multiple_of(index * group_rows, group_rows)
            here = pl.ds(row0, group_rows)
            if fresh and received:
                x = jnp.where(section == 0, fresh_ref[here, :], received_ref[here, :])
            else:
                x = (fresh_ref if fresh else received_ref)[here, :]
            wide = x.astype(jnp.float32)
            mean = jnp.mean(wide * wide, axis=-1, keepdims=True)
            queries = (wide * lax.rsqrt(mean + 1e-06) * gain_ref[...]).astype(jnp.bfloat16)
            first = base + index * (GROUP * SLOTS)
            scores = []
            starts = []
            for g in range(GROUP):
                at = [
                    pl.multiple_of(places[first + g * SLOTS + j], KEY_BLOCK)
                    for j in range(SLOTS)
                ]
                starts.append(at)
                keys = jnp.concatenate(
                    [k_tab[pl.ds(a, KEY_BLOCK), :] for a in at], axis=0
                )
                scores.append(
                    lax.dot_general(
                        queries[g * QUERY_BLOCK : (g + 1) * QUERY_BLOCK],
                        keys,
                        (((1,), (1,)), ((), ())),
                        preferred_element_type=jnp.float32,
                    )
                )
            scores = jnp.concatenate(scores, axis=0) * (HEAD_DIM**-0.5)
            lane = lax.broadcasted_iota(jnp.int32, scores.shape, 1)
            scores = jnp.where(lane < live_keys, scores, SCORE_FLOOR)
            highest = jnp.max(scores, axis=-1, keepdims=True)
            exponent = jnp.exp(scores - highest)
            total = jnp.sum(exponent, axis=-1, keepdims=True)
            weights = (exponent / total).astype(jnp.bfloat16)
            summed = []
            for g in range(GROUP):
                values = jnp.concatenate(
                    [v_tab[pl.ds(a, KEY_BLOCK), :] for a in starts[g]], axis=0
                )
                summed.append(
                    jnp.dot(
                        weights[g * QUERY_BLOCK : (g + 1) * QUERY_BLOCK],
                        values,
                        preferred_element_type=jnp.float32,
                    )
                )
            heads = jnp.concatenate(summed, axis=0).astype(jnp.bfloat16)
            updated = wide + gate_ref[...] * heads.astype(jnp.float32)
            updated = updated.astype(jnp.bfloat16)
            out_ref[here, :] = updated
            done_ref[pl.ds(index * group_sources, group_sources), pl.ds(token0, chunk_tokens), :] = (
                updated.reshape(group_sources, chunk_tokens, HEAD_DIM)
            )
            return carry

        lax.fori_loop(0, rows // group_rows, one_group, 0)


def attend(step, places, info, fresh, received, gain, gate, k_tab, v_tab, done):
    inputs = [value for value in (fresh, received) if value is not None]
    rows, width = inputs[0].shape
    vmem = pl.BlockSpec(memory_space=pltpu.VMEM)
    smem = pl.BlockSpec(memory_space=pltpu.SMEM)
    inputs = [places, info, *inputs, gain, gate, k_tab, v_tab]
    aliases = {}
    done_shape = (CHUNKS * rows // HEADS // 8, HEADS * 8, width)
    if done is not None:
        aliases = {len(inputs): 1}
        inputs.append(done)
        done_shape = done.shape
    return pl.pallas_call(
        functools.partial(
            attend_kernel,
            step=step,
            fresh=fresh is not None,
            received=received is not None,
        ),
        out_shape=(
            jax.ShapeDtypeStruct((rows, width), jnp.bfloat16),
            jax.ShapeDtypeStruct(done_shape, jnp.bfloat16),
        ),
        in_specs=[smem, smem] + [vmem] * (len(inputs) - 2),
        out_specs=(vmem, vmem),
        input_output_aliases=aliases,
        compiler_params=pltpu.CompilerParams(vmem_limit_bytes=24 * 1024 * 1024),
        cost_estimate=pl.CostEstimate(
            flops=4 * rows * SPAN * HEAD_DIM,
            bytes_accessed=4 * rows * width,
            transcendentals=rows * SPAN,
        ),
    )(*inputs)


def swapped(value, axis):
    return lax.ppermute(value, axis, [(0, 1), (1, 0)])


def local(patches, stale_cache, block_lists, block_counts, query_gain, branch_gate):
    section = lax.axis_index("section")
    owner = lax.axis_index("z") * lax.axis_size("yh") + lax.axis_index("yh")
    yl, core = lax.axis_index("yl"), lax.axis_index("core")
    micro_count, patch_rows, channels = patches.shape
    sources = lax.axis_size("z") * lax.axis_size("yh")
    tokens = micro_count * patch_rows
    chunk_tokens = tokens // CHUNKS

    by_head = stale_cache[0].reshape(tokens, 2, HEADS, HEAD_DIM).transpose(2, 1, 0, 3)
    by_head = by_head.reshape(HEADS, 2 * tokens, HEAD_DIM)
    mine = lax.dynamic_slice_in_dim(
        patches.reshape(tokens, HEADS, HEAD_DIM), section * chunk_tokens, chunk_tokens, 0
    ).transpose(1, 0, 2)
    moved = lax.all_to_all(
        jnp.concatenate([by_head, mine], axis=1), OWNERS, 0, 0, tiled=True
    )
    k_own, v_own = moved[:, :tokens], moved[:, tokens : 2 * tokens]
    fresh = [moved[:, 2 * tokens :].reshape(sources * chunk_tokens, HEAD_DIM)]
    k_other = swapped(k_own, "yl")
    v_other = swapped(v_own, "yl")
    for c in range(1, CHUNKS):
        fresh.append(lax.ppermute(fresh[0], "section", [(c, 0)]))

    query_blocks = patch_rows // QUERY_BLOCK
    lists = lax.dynamic_index_in_dim(block_lists[0], owner, 0, keepdims=False)
    lists = lists.reshape(micro_count, sources, 2, 2, query_blocks, SLOTS)
    lists = lax.dynamic_slice(
        lists, (0, 0, yl, core, 0, 0), (micro_count, sources, 1, 1, query_blocks, SLOTS)
    )
    lists = lists.reshape(micro_count, sources, query_blocks, SLOTS).transpose(0, 2, 1, 3)
    lists = lists.reshape(CHUNKS, -1, sources, SLOTS).transpose(0, 2, 1, 3)
    per_shard = patch_rows // KEY_BLOCK
    per_micro = per_shard * sources * 4
    micro, rest = lists // per_micro, lists % per_micro
    shard, half = rest // per_shard, rest % per_shard
    piece = ((shard % 2) ^ core) * 2 + ((shard // 2 % 2) ^ yl)
    places = ((piece * sources + shard // 4) * micro_count + micro) * patch_rows + half * KEY_BLOCK
    places = places.reshape(-1)
    count = lax.dynamic_index_in_dim(block_counts[0], owner, 0, keepdims=False)
    info = jnp.stack([section, count]).astype(jnp.int32)
    gain = lax.dynamic_index_in_dim(query_gain.reshape(HEADS, HEAD_DIM), owner, 0)
    gate = lax.dynamic_index_in_dim(branch_gate.reshape(HEADS, HEAD_DIM), owner, 0)

    k_other, v_own, places, info, gain, gate, *fresh = lax.optimization_barrier(
        (k_other, v_own, places, info, gain, gate, *fresh)
    )
    k_parts = [k_own, k_other, swapped(k_own, "core"), swapped(k_other, "core")]
    v_parts = [v_own, v_other, swapped(v_own, "core"), swapped(v_other, "core")]
    k_tab, v_tab = gathered(k_parts, v_parts)

    steps = CHUNKS + (SECTIONS - 1) * DELAY
    sent = []
    result = done = None
    for step in range(steps):
        x = fresh[step] if step < CHUNKS else None
        received = sent[step - DELAY] if step >= DELAY else None
        result, done = attend(
            step, places, info, x, received, gain, gate, k_tab, v_tab, done
        )
        if step + DELAY < steps:
            sent.append(
                lax.ppermute(result, "section", [(s, s + 1) for s in range(SECTIONS - 1)])
            )
    done = lax.all_to_all(done, OWNERS, 0, 0, tiled=True)
    done = done.reshape(HEADS, micro_count, patch_rows, HEAD_DIM).transpose(1, 2, 0, 3)
    return done.reshape(1, micro_count, patch_rows, channels)


def solution(mesh):
    fine = Mesh(
        mesh.devices.reshape(SECTIONS, -1, 2, 2, 2), ("section", "z", "yh", "yl", "core")
    )
    seq = ("z", "yh", "yl", "core")
    return jax.shard_map(
        local,
        mesh=fine,
        in_specs=(
            P(None, seq, None),
            P("section", None, seq, None),
            P("section", None, None, None),
            P("section", None),
            P("section", None),
            P("section", None),
        ),
        out_specs=P("section", None, seq, None),
        check_vma=False,
    )
```

time: 180 us -> 142 us (0.79)
  blocking collectives: 53.4 us -> 23.7 us
  other arithmetic: 10.3 us -> 2.09 us
  starting transfers between devices: 21.9 us -> 27.9 us
  waiting for transfers between devices: 67.5 us -> 63.2 us
    all_to_all x1 -> x0, blocking collectives: 29.6 us -> none  [local(): moved = lax.all_to_all(by_head[which], OWNERS, 0, 0, tiled=True)]
    ppermute x6 -> x8, waiting for transfers between devices: 42.5 us -> 16 us  [local(): lax.ppermute(result, 'section', [(s, s + 1) for s in range(SECTIONS - 1)])]
    all_to_all x2 -> x1, waiting for transfers between devices: 15.4 us -> 32.2 us  [local(): lax.all_to_all(jnp.concatenate([by_head, mine], axis=1), OWNERS, 0, 0, ti...]
    ppermute x6, waiting for transfers between devices: 9.56 us -> 15.1 us  [swapped(): return lax.ppermute(value, axis, [(0, 1), (1, 0)])]
    pallas_call x1 -> x0, other arithmetic: 5.2 us -> none  [attend(): pl.pallas_call(functools.partial(attend_kernel, pieces=pieces, groups=que...]
    all_to_all x2 -> x1, starting transfers between devices: 7.08 us -> 11.3 us  [local(): lax.all_to_all(jnp.concatenate([by_head, mine], axis=1), OWNERS, 0, 0, ti...]
    another operation x7 -> x1, other arithmetic: 4.84 us -> 0.72 us  [local(): info = jnp.stack([section, count]).astype(jnp.int32)]
    ppermute x6 -> x8, starting transfers between devices: 7.75 us -> 10.3 us  [local(): lax.ppermute(result, 'section', [(s, s + 1) for s in range(SECTIONS - 1)])]
  transfers between devices with their start and end apart: 17 -> 18, of which waited for: 8 -> 12; matrix products, arithmetic and copies ran while one was open for 4% -> 2% of each run, Pallas kernels for 1% -> 9%
where the time goes in v3:
time: 142 us; the launch traced here: 141 us
  waiting for transfers between devices  63.2 us (45%)
  starting transfers between devices  27.9 us (20%)
  blocking collectives  23.7 us (17%)
  Pallas kernels  16.8 us (12%)
  local copies, waits for them, and re-layouts  6.99 us (5%)
  other arithmetic  2.09 us (1%)
    all_to_all x1, waiting for transfers between devices, local(): lax.all_to_all(jnp.concatenate([by_head, mine], axis=1), OWNERS, 0, 0, ti...  32.2 us
    all_to_all x1, blocking collectives, local(): done = lax.all_to_all(done, OWNERS, 0, 0, tiled=True)  23.7 us
    pallas_call x10, Pallas kernels, attend(): pl.pallas_call(functools.partial(attend_kernel, step=step, fresh=fresh is...  16.5 us
    ppermute x8, waiting for transfers between devices, local(): lax.ppermute(result, 'section', [(s, s + 1) for s in range(SECTIONS - 1)])  16 us
    ppermute x6, waiting for transfers between devices, swapped(): return lax.ppermute(value, axis, [(0, 1), (1, 0)])  15.1 us
    all_to_all x1, starting transfers between devices, local(): lax.all_to_all(jnp.concatenate([by_head, mine], axis=1), OWNERS, 0, 0, ti...  11.3 us
    ppermute x8, starting transfers between devices, local(): lax.ppermute(result, 'section', [(s, s + 1) for s in range(SECTIONS - 1)])  10.3 us
    ppermute x3, starting transfers between devices, local(): fresh.append(lax.ppermute(fresh[0], 'section', [(c, 0)]))  3.73 us
  transfers between devices with their start and end apart: 18, of which 12 were waited for; matrix products, arithmetic and copies ran while one was open for 2% of the time, Pallas kernels for 9%

profile of v3, /device:TPU:6, one launch (start us, length us, event | category | flops | bytes accessed | tf_op | source)
XLA Modules:
  0.0 141.1 jit_solution(3838265936825942109)
XLA Ops:
  0.0 1.3 copy.32
  2.1 1.1 pad_maximum_fusion
  3.2 11.3 %all-to-all-start = ((bf16[16,288,128]{2,1,0:T(8,128)(2,1)}), bf16[16,288,128]{2,1,0:T(8,128)(2,1)S(1)}, u32[]{:S(2)}, u32[]{:S(2)}) async-start(bf16[16,288,128]{2,1,0:T(8,128)(2,1)} %pad_maximum_fusion), calls=%async_computation | async-start | bytes 2359296 | tf_op jit(solution)/shard_map/all_to_all | solution.py:194
  15.3 32.2 %all-to-all-done = bf16[16,288,128]{2,1,0:T(8,128)(2,1)S(1)} async-done(((bf16[16,288,128]{2,1,0:T(8,128)(2,1)}), bf16[16,288,128]{2,1,0:T(8,128)(2,1)S(1)}, u32[]{:S(2)}, u32[]{:S(2)}) %all-to-all-start) | async-done | bytes 1179680 | tf_op jit(solution)/shard_map/all_to_all | solution.py:194
  47.6 0.9 copy-done.1
  49.2 1.3 collective-permute-start
  50.8 0.9 slice.14
  51.7 2.4 %collective-permute-start.3 = (bf16[512,128]{1,0:T(8,128)(2,1)S(1)}, bf16[512,128]{1,0:T(8,128)(2,1)S(1)}, u32[]{:S(2)}, u32[]{:S(2)}) collective-permute-start(bf16[512,128]{1,0:T(8,128)(2,1)S(1)} %bitcast.54), channel_id=1, source_target_pairs={{192,0},{193,1},{194,2},{195,3},{196,4},{197,5},{198,6},{199,7},{2... | collective-permute-start | bytes 393224 | tf_op jit(solution)/shard_map/ppermute | solution.py:202
  55.5 0.7 pad_add_fusion.info
  56.4 0.7 constant_dynamic-slice_fusion
  57.1 12.2 %collective-permute-done.refs_1_ = bf16[16,128,128]{2,1,0:T(8,128)(2,1)S(1)} collective-permute-done((bf16[16,128,128]{2,1,0:T(8,128)(2,1)S(1)}, bf16[16,128,128]{2,1,0:T(8,128)(2,1)S(1)}, u32[]{:S(2)}, u32[]{:S(2)}) %collective-permute-start) | collective-permute-done | bytes 524320 | tf_op jit(solution)/shard_map/ppermute | solution.py:177
  69.8 2.1 %collective-permute-done.8.refs_7_ = bf16[16,128,128]{2,1,0:T(8,128)(2,1)S(1)} collective-permute-done((bf16[16,128,128]{2,1,0:T(8,128)(2,1)S(1)}, bf16[16,128,128]{2,1,0:T(8,128)(2,1)S(1)}, u32[]{:S(2)}, u32[]{:S(2)}) %collective-permute-start.8) | collective-permute-done | bytes 524320 | tf_op jit(solution)/shard_map/ppermute | solution.py:177
  72.0 0.7 collective-permute-done.7.refs_6_
  73.8 1.3 collective-permute-start.10
  75.8 1.3 collective-permute-start.9
  77.1 4.3 %collective-permute-done.10.rest_1_ = bf16[512,128]{1,0:T(8,128)(2,1)S(1)} collective-permute-done((bf16[512,128]{1,0:T(8,128)(2,1)S(1)}, bf16[512,128]{1,0:T(8,128)(2,1)S(1)}, u32[]{:S(2)}, u32[]{:S(2)}) %collective-permute-start.10) | collective-permute-done | bytes 131104 | tf_op jit(solution)/shard_map/ppermute | solution.py:242
  82.0 1.3 collective-permute-start.12
  84.7 1.3 collective-permute-start.11
  86.0 3.0 %collective-permute-done.12.rest_0_ = bf16[512,128]{1,0:T(8,128)(2,1)S(1)} collective-permute-done((bf16[512,128]{1,0:T(8,128)(2,1)S(1)}, bf16[512,128]{1,0:T(8,128)(2,1)S(1)}, u32[]{:S(2)}, u32[]{:S(2)}) %collective-permute-start.12) | collective-permute-done | bytes 131104 | tf_op jit(solution)/shard_map/ppermute | solution.py:242
  89.7 1.3 collective-permute-start.14
  92.4 1.3 collective-permute-start.13
  93.7 4.5 %collective-permute-done.14.rest_0_ = bf16[512,128]{1,0:T(8,128)(2,1)S(1)} collective-permute-done((bf16[512,128]{1,0:T(8,128)(2,1)S(1)}, bf16[512,128]{1,0:T(8,128)(2,1)S(1)}, u32[]{:S(2)}, u32[]{:S(2)}) %collective-permute-start.14) | collective-permute-done | bytes 131104 | tf_op jit(solution)/shard_map/ppermute | solution.py:242
  98.2 2.9 %shard_map.71 = (bf16[512,128]{1,0:T(8,128)(2,1)S(1)}, bf16[16,128,128]{2,1,0:T(8,128)(2,1)S(1)}) custom-call(s32[2048]{0:T(1024)S(1)} %reshape.48.places, s32[2]{0:T(128)S(1)} %pad_add_fusion.info, bf16[512,128]{1,0:T(8,128)(2,1)S(1)} %collective-permute-done.14.rest_0_, ...), custom_call_target="tpu_custom_call", output_to_operand_aliasing={{1}: (7, {})} | custom-call | flops 134217728 | bytes 262144 | tf_op jit(solution)/shard_map/pallas_call | solution.py:153
  101.1 1.3 collective-permute-start.16
  102.8 2.7 %shard_map.72 = (bf16[512,128]{1,0:T(8,128)(2,1)S(1)}, bf16[16,128,128]{2,1,0:T(8,128)(2,1)S(1)}) custom-call(s32[2048]{0:T(1024)S(1)} %reshape.48.places, s32[2]{0:T(128)S(1)} %pad_add_fusion.info, bf16[512,128]{1,0:T(8,128)(2,1)S(1)} %collective-permute-done.13.rest_0_, ...), custom_call_target="tpu_custom_call", output_to_operand_aliasing={{1}: (7, {})} | custom-call | flops 134217728 | bytes 262144 | tf_op jit(solution)/shard_map/pallas_call | solution.py:153
  105.6 1.3 collective-permute-start.15
  106.9 1.1 collective-permute-done.16.rest_0_
  107.9 3.4 %shard_map.73 = (bf16[512,128]{1,0:T(8,128)(2,1)}, bf16[16,128,128]{2,1,0:T(8,128)(2,1)S(1)}) custom-call(s32[2048]{0:T(1024)S(1)} %reshape.48.places, s32[2]{0:T(128)S(1)} %pad_add_fusion.info, bf16[512,128]{1,0:T(8,128)(2,1)S(1)} %collective-permute-done.16.rest_0_, ...), custom_call_target="tpu_custom_call", output_to_operand_aliasing={{1}: (7, {})} | custom-call | flops 134217728 | bytes 262144 | tf_op jit(solution)/shard_map/pallas_call | solution.py:153
  111.3 1.3 collective-permute-done.15.rest_0_
  112.6 3.4 %shard_map.74 = (bf16[512,128]{1,0:T(8,128)(2,1)}, bf16[16,128,128]{2,1,0:T(8,128)(2,1)S(1)}) custom-call(s32[2048]{0:T(1024)S(1)} %reshape.48.places, s32[2]{0:T(128)S(1)} %pad_add_fusion.info, bf16[512,128]{1,0:T(8,128)(2,1)S(1)} %collective-permute-done.15.rest_0_, ...), custom_call_target="tpu_custom_call", output_to_operand_aliasing={{1}: (7, {})} | custom-call | flops 134217728 | bytes 262144 | tf_op jit(solution)/shard_map/pallas_call | solution.py:153
  116.0 23.7 %all_to_all.10 = bf16[16,128,128]{2,1,0:T(8,128)(2,1)S(1)} all-to-all(bf16[16,128,128]{2,1,0:T(8,128)(2,1)S(1)} %get-tuple-element.64), channel_id=1, replica_groups=mesh['section'=4,'z'=8,'yh'=2,'yl'=2,'core'=2] {'z','yh'}, dimensions={0} | all-to-all | bytes 1048576 | tf_op jit(solution)/shard_map/all_to_all | solution.py:244
  140.0 1.0 reshape.55
  (44 shorter events, 11.3 us)
Async XLA Ops:
  0.0 15.2 %copy-start = (s32[1,16,512,16]{2,3,1,0:T(8,128)S(1)}, s32[1,16,512,16]{2,3,1,0:T(8,128)}, u32[]{:S(2)}) copy-start(s32[1,16,512,16]{2,3,1,0:T(8,128)} %param.8) | copy-start | bytes 1572868
  0.0 1.4 %copy-start.2 = (bf16[1,2,64,4096]{3,2,1,0:T(8,128)(2,1)S(1)}, bf16[1,2,64,4096]{3,2,1,0:T(8,128)(2,1)}, u32[]{:S(2)}) copy-start(bf16[1,2,64,4096]{3,2,1,0:T(8,128)(2,1)} %param.7) | copy-start | bytes 3145732
  3.2 11.4 %copy-start.3 = (s32[1,16]{1,0:T(1,128)S(1)}, s32[1,16]{1,0:T(1,128)}, u32[]{:S(2)}) copy-start(s32[1,16]{1,0:T(1,128)} %param.9) | copy-start | bytes 196
  3.2 44.2 %all-to-all-start = ((bf16[16,288,128]{2,1,0:T(8,128)(2,1)}), bf16[16,288,128]{2,1,0:T(8,128)(2,1)S(1)}, u32[]{:S(2)}, u32[]{:S(2)}) async-start(bf16[16,288,128]{2,1,0:T(8,128)(2,1)} %pad_maximum_fusion), calls=%async_computation | async-start | bytes 2359296 | tf_op jit(solution)/shard_map/all_to_all | solution.py:194
  47.5 1.0 copy-start.1
  48.5 20.8 %collective-permute-start.6 = (bf16[16,128,128]{2,1,0:T(8,128)(2,1)S(1)}, bf16[16,128,128]{2,1,0:T(8,128)(2,1)S(1)}, u32[]{:S(2)}, u32[]{:S(2)}) collective-permute-start(bf16[16,128,128]{2,1,0:T(8,128)(2,1)S(1)} %get-tuple-element.42.refs_4_), channel_id=1, source_target_pairs={{0,2},{2,0},{1,3},{3,1},{4,6},{6,4},{5,7},{7,5},{8,10},{10,8},{9,1... | collective-permute-start | bytes 1572872 | tf_op jit(solution)/shard_map/ppermute | solution.py:177
  49.2 20.1 %collective-permute-start = (bf16[16,128,128]{2,1,0:T(8,128)(2,1)S(1)}, bf16[16,128,128]{2,1,0:T(8,128)(2,1)S(1)}, u32[]{:S(2)}, u32[]{:S(2)}) collective-permute-start(bf16[16,128,128]{2,1,0:T(8,128)(2,1)S(1)} %get-tuple-element.66.refs_0_), channel_id=1, source_target_pairs={{0,2},{2,0},{1,3},{3,1},{4,6},{6,4},{5,7},{7,5},{8,10},{10,8},{9,1... | collective-permute-start | bytes 1572872 | tf_op jit(solution)/shard_map/ppermute | solution.py:177
  51.7 5.4 %collective-permute-start.3 = (bf16[512,128]{1,0:T(8,128)(2,1)S(1)}, bf16[512,128]{1,0:T(8,128)(2,1)S(1)}, u32[]{:S(2)}, u32[]{:S(2)}) collective-permute-start(bf16[512,128]{1,0:T(8,128)(2,1)S(1)} %bitcast.54), channel_id=1, source_target_pairs={{192,0},{193,1},{194,2},{195,3},{196,4},{197,5},{198,6},{199,7},{2... | collective-permute-start | bytes 393224 | tf_op jit(solution)/shard_map/ppermute | solution.py:202
  54.1 3.0 %collective-permute-start.2 = (bf16[512,128]{1,0:T(8,128)(2,1)S(1)}, bf16[512,128]{1,0:T(8,128)(2,1)S(1)}, u32[]{:S(2)}, u32[]{:S(2)}) collective-permute-start(bf16[512,128]{1,0:T(8,128)(2,1)S(1)} %bitcast.55), channel_id=1, source_target_pairs={{128,0},{129,1},{130,2},{131,3},{132,4},{133,5},{134,6},{135,7},{1... | collective-permute-start | bytes 393224 | tf_op jit(solution)/shard_map/ppermute | solution.py:202
  54.8 2.3 %collective-permute-start.1 = (bf16[512,128]{1,0:T(8,128)(2,1)S(1)}, bf16[512,128]{1,0:T(8,128)(2,1)S(1)}, u32[]{:S(2)}, u32[]{:S(2)}) collective-permute-start(bf16[512,128]{1,0:T(8,128)(2,1)S(1)} %bitcast.56), channel_id=1, source_target_pairs={{64,0},{65,1},{66,2},{67,3},{68,4},{69,5},{70,6},{71,7},{72,8},{73... | collective-permute-start | bytes 393224 | tf_op jit(solution)/shard_map/ppermute | solution.py:202
  57.1 12.7 %collective-permute-start.4 = (bf16[16,128,128]{2,1,0:T(8,128)(2,1)S(1)}, bf16[16,128,128]{2,1,0:T(8,128)(2,1)S(1)}, u32[]{:S(2)}, u32[]{:S(2)}) collective-permute-start(bf16[16,128,128]{2,1,0:T(8,128)(2,1)S(1)} %get-tuple-element.66.refs_0_), channel_id=1, source_target_pairs={{0,1},{1,0},{2,3},{3,2},{4,5},{5,4},{6,7},{7,6},{8,9},{9,8},{10,11... | collective-permute-start | bytes 1572872 | tf_op jit(solution)/shard_map/ppermute | solution.py:177
  69.3 2.7 %collective-permute-start.5 = (bf16[16,128,128]{2,1,0:T(8,128)(2,1)S(1)}, bf16[16,128,128]{2,1,0:T(8,128)(2,1)S(1)}, u32[]{:S(2)}, u32[]{:S(2)}) collective-permute-start(bf16[16,128,128]{2,1,0:T(8,128)(2,1)S(1)} %collective-permute-done.refs_1_), channel_id=1, source_target_pairs={{0,1},{1,0},{2,3},{3,2},{4,5},{5,4},{6,7},{7,6},{8,9},{9,8},{10,11... | collective-permute-start | bytes 1572872 | tf_op jit(solution)/shard_map/ppermute | solution.py:177
  69.3 2.7 %collective-permute-start.8 = (bf16[16,128,128]{2,1,0:T(8,128)(2,1)S(1)}, bf16[16,128,128]{2,1,0:T(8,128)(2,1)S(1)}, u32[]{:S(2)}, u32[]{:S(2)}) collective-permute-start(bf16[16,128,128]{2,1,0:T(8,128)(2,1)S(1)} %collective-permute-done.6.refs_5_), channel_id=1, source_target_pairs={{0,1},{1,0},{2,3},{3,2},{4,5},{5,4},{6,7},{7,6},{8,9},{9,8},{10,11... | collective-permute-start | bytes 1572872 | tf_op jit(solution)/shard_map/ppermute | solution.py:177
  69.8 2.9 %collective-permute-start.7 = (bf16[16,128,128]{2,1,0:T(8,128)(2,1)S(1)}, bf16[16,128,128]{2,1,0:T(8,128)(2,1)S(1)}, u32[]{:S(2)}, u32[]{:S(2)}) collective-permute-start(bf16[16,128,128]{2,1,0:T(8,128)(2,1)S(1)} %get-tuple-element.42.refs_4_), channel_id=1, source_target_pairs={{0,1},{1,0},{2,3},{3,2},{4,5},{5,4},{6,7},{7,6},{8,9},{9,8},{10,11... | collective-permute-start | bytes 1572872 | tf_op jit(solution)/shard_map/ppermute | solution.py:177
  73.8 7.6 %collective-permute-start.10 = (bf16[512,128]{1,0:T(8,128)(2,1)S(1)}, bf16[512,128]{1,0:T(8,128)(2,1)S(1)}, u32[]{:S(2)}, u32[]{:S(2)}) collective-permute-start(bf16[512,128]{1,0:T(8,128)(2,1)S(1)} %get-tuple-element.49), channel_id=1, source_target_pairs={{0,64},{64,128},{128,192},{1,65},{65,129},{129,193},{2,66},{66,130... | collective-permute-start | bytes 393224 | tf_op jit(solution)/shard_map/ppermute | solution.py:242
  75.8 8.2 %collective-permute-start.9 = (bf16[512,128]{1,0:T(8,128)(2,1)S(1)}, bf16[512,128]{1,0:T(8,128)(2,1)S(1)}, u32[]{:S(2)}, u32[]{:S(2)}) collective-permute-start(bf16[512,128]{1,0:T(8,128)(2,1)S(1)} %get-tuple-element.47), channel_id=1, source_target_pairs={{0,64},{64,128},{128,192},{1,65},{65,129},{129,193},{2,66},{66,130... | collective-permute-start | bytes 393224 | tf_op jit(solution)/shard_map/ppermute | solution.py:242
  82.0 7.0 %collective-permute-start.12 = (bf16[512,128]{1,0:T(8,128)(2,1)S(1)}, bf16[512,128]{1,0:T(8,128)(2,1)S(1)}, u32[]{:S(2)}, u32[]{:S(2)}) collective-permute-start(bf16[512,128]{1,0:T(8,128)(2,1)S(1)} %get-tuple-element.53), channel_id=1, source_target_pairs={{0,64},{64,128},{128,192},{1,65},{65,129},{129,193},{2,66},{66,130... | collective-permute-start | bytes 393224 | tf_op jit(solution)/shard_map/ppermute | solution.py:242
  84.7 7.0 %collective-permute-start.11 = (bf16[512,128]{1,0:T(8,128)(2,1)S(1)}, bf16[512,128]{1,0:T(8,128)(2,1)S(1)}, u32[]{:S(2)}, u32[]{:S(2)}) collective-permute-start(bf16[512,128]{1,0:T(8,128)(2,1)S(1)} %get-tuple-element.52), channel_id=1, source_target_pairs={{0,64},{64,128},{128,192},{1,65},{65,129},{129,193},{2,66},{66,130... | collective-permute-start | bytes 393224 | tf_op jit(solution)/shard_map/ppermute | solution.py:242
  89.7 8.4 %collective-permute-start.14 = (bf16[512,128]{1,0:T(8,128)(2,1)S(1)}, bf16[512,128]{1,0:T(8,128)(2,1)S(1)}, u32[]{:S(2)}, u32[]{:S(2)}) collective-permute-start(bf16[512,128]{1,0:T(8,128)(2,1)S(1)} %get-tuple-element.57), channel_id=1, source_target_pairs={{0,64},{64,128},{128,192},{1,65},{65,129},{129,193},{2,66},{66,130... | collective-permute-start | bytes 393224 | tf_op jit(solution)/shard_map/ppermute | solution.py:242
  92.4 10.5 %collective-permute-start.13 = (bf16[512,128]{1,0:T(8,128)(2,1)S(1)}, bf16[512,128]{1,0:T(8,128)(2,1)S(1)}, u32[]{:S(2)}, u32[]{:S(2)}) collective-permute-start(bf16[512,128]{1,0:T(8,128)(2,1)S(1)} %get-tuple-element.56), channel_id=1, source_target_pairs={{0,64},{64,128},{128,192},{1,65},{65,129},{129,193},{2,66},{66,130... | collective-permute-start | bytes 393224 | tf_op jit(solution)/shard_map/ppermute | solution.py:242
  101.1 6.9 %collective-permute-start.16 = (bf16[512,128]{1,0:T(8,128)(2,1)S(1)}, bf16[512,128]{1,0:T(8,128)(2,1)S(1)}, u32[]{:S(2)}, u32[]{:S(2)}) collective-permute-start(bf16[512,128]{1,0:T(8,128)(2,1)S(1)} %get-tuple-element.61), channel_id=1, source_target_pairs={{0,64},{64,128},{128,192},{1,65},{65,129},{129,193},{2,66},{66,130... | collective-permute-start | bytes 393224 | tf_op jit(solution)/shard_map/ppermute | solution.py:242
  105.6 7.0 %collective-permute-start.15 = (bf16[512,128]{1,0:T(8,128)(2,1)S(1)}, bf16[512,128]{1,0:T(8,128)(2,1)S(1)}, u32[]{:S(2)}, u32[]{:S(2)}) collective-permute-start(bf16[512,128]{1,0:T(8,128)(2,1)S(1)} %get-tuple-element.60), channel_id=1, source_target_pairs={{0,64},{64,128},{128,192},{1,65},{65,129},{129,193},{2,66},{66,130... | collective-permute-start | bytes 393224 | tf_op jit(solution)/shard_map/ppermute | solution.py:242

commit v4 on v3

v4 whole, which is shorter than its diff:
```python
import functools

import jax
import jax.numpy as jnp
from jax import lax
from jax.experimental import pallas as pl
from jax.experimental.pallas import tpu as pltpu
from jax.sharding import PartitionSpec as P

HEADS = 16
HEAD_DIM = 128
QUERY_BLOCK = 16
KEY_BLOCK = 32
SLOTS = 16
SECTIONS = 4
CHUNKS = 4
DELAY = 2
GROUP = 32
SPAN = SLOTS * KEY_BLOCK
SCORE_FLOOR = -1e30

RINGS = 8
SHIFTS = (0, 1, -1, 2, -2, 3, -3, 4)
WAVES = ((0, 1, 2, 3), (4, 5, 6, 7))


def pack_kernel(cache, patches, *refs, shifts):
    outs, sems = refs[: len(shifts)], refs[-1]
    section, shard = lax.axis_index("section"), lax.axis_index("seq")
    z, upper = shard // RINGS, shard // 4 % 2
    micro_count, rows = cache.shape[:2]
    depth = len(shifts)
    channels = patches.shape[2]
    chunk_tokens = outs[0].shape[1] - 2 * micro_count * rows
    token0 = section * chunk_tokens
    fresh_rows = pl.ds(pl.multiple_of(token0 % rows, chunk_tokens), chunk_tokens)
    copies = []
    for k, shift in enumerate(shifts):
        for other in range(2):
            head = lax.rem(z + (shift + depth), depth) * 2 + (upper ^ other)
            slot = len(copies)
            for which in range(2):
                start = pl.multiple_of(which * channels + head * HEAD_DIM, HEAD_DIM)
                for m in range(micro_count):
                    copies.append(
                        pltpu.make_async_copy(
                            cache.at[m, :, pl.ds(start, HEAD_DIM)],
                            outs[k].at[other, pl.ds((which * micro_count + m) * rows, rows), :],
                            sems.at[slot + which * micro_count + m],
                        )
                    )
            start = pl.multiple_of(head * HEAD_DIM, HEAD_DIM)
            copies.append(
                pltpu.make_async_copy(
                    patches.at[token0 // rows, fresh_rows, pl.ds(start, HEAD_DIM)],
                    outs[k].at[other, pl.ds(2 * micro_count * rows, chunk_tokens), :],
                    sems.at[slot + 2 * micro_count],
                )
            )
    for copy in copies:
        copy.start()
    for copy in copies:
        copy.wait()


def packed(cache, patches):
    micro_count, rows, channels = patches.shape
    tokens = micro_count * rows
    piece = jax.ShapeDtypeStruct((2, 2 * tokens + tokens // CHUNKS, HEAD_DIM), jnp.bfloat16)
    count = len(SHIFTS)
    return pl.pallas_call(
        functools.partial(pack_kernel, shifts=SHIFTS),
        out_shape=(piece,) * count,
        in_specs=[pl.BlockSpec(memory_space=pltpu.HBM)] * 2,
        out_specs=(pl.BlockSpec(memory_space=pltpu.VMEM),) * count,
        scratch_shapes=[pltpu.SemaphoreType.DMA((count * 2 * (2 * micro_count + 1),))],
        compiler_params=pltpu.CompilerParams(vmem_limit_bytes=61 * 1024 * 1024),
    )(cache, patches)


def part_kernel(*refs, count):
    own, others, sems = refs[count], refs[count + 1 : -1], refs[-1]
    copies = []
    for wave, other in zip(WAVES, others):
        for n, k in enumerate(wave):
            copies.append(pltpu.make_async_copy(refs[k].at[1], other.at[n], sems.at[0, k]))
            copies.append(
                pltpu.make_async_copy(
                    refs[k].at[0, pl.ds(0, own.shape[1]), :], own.at[k], sems.at[1, k]
                )
            )
    for copy in copies:
        copy.start()
    for copy in copies:
        copy.wait()


def parted(pieces, rows):
    count = len(pieces)
    vmem = pl.BlockSpec(memory_space=pltpu.VMEM)
    own, *others = pl.pallas_call(
        functools.partial(part_kernel, count=count),
        out_shape=(
            jax.ShapeDtypeStruct((count, rows, HEAD_DIM), jnp.bfloat16),
            *(
                jax.ShapeDtypeStruct((len(wave), *pieces[0].shape[1:]), jnp.bfloat16)
                for wave in WAVES
            ),
        ),
        in_specs=[pl.BlockSpec(memory_space=pl.ANY)] * count,
        out_specs=(vmem,) * (1 + len(WAVES)),
        scratch_shapes=[pltpu.SemaphoreType.DMA((2, count))],
        compiler_params=pltpu.CompilerParams(vmem_limit_bytes=8 * 1024 * 1024),
    )(*pieces)
    return own, others


def arrange_kernel(info, *refs, skip):
    count = len(SHIFTS)
    pieces, crosses, out = refs[:count], refs[count:-1], refs[-1]
    z, upper = info[2], info[3]
    chunk_tokens = pieces[0].shape[1] - skip
    for wave, cross in zip(WAVES, crosses):
        for n, k in enumerate(wave):
            source = lax.rem(z + (count - SHIFTS[k]), count) * 2
            for part, index, lane in ((pieces[k], 0, upper), (cross, n, 1 - upper)):
                place = pl.multiple_of((source + lane) * chunk_tokens, chunk_tokens)
                out[pl.ds(place, chunk_tokens), :] = part[index, skip : skip + chunk_tokens, :]


def arranged(info, pieces, crosses, tokens, chunk_tokens):
    inputs = [*pieces, *crosses]
    rows = 2 * len(pieces) * chunk_tokens
    vmem = pl.BlockSpec(memory_space=pltpu.VMEM)
    return pl.pallas_call(
        functools.partial(arrange_kernel, skip=2 * tokens),
        out_shape=jax.ShapeDtypeStruct((rows, HEAD_DIM), jnp.bfloat16),
        in_specs=[pl.BlockSpec(memory_space=pltpu.SMEM)] + [vmem] * len(inputs),
        out_specs=vmem,
        compiler_params=pltpu.CompilerParams(vmem_limit_bytes=8 * 1024 * 1024),
    )(info, *inputs)


def gather_kernel(*refs, rows):
    parts, out, sems = refs[:-2], refs[-2], refs[-1]
    copies = []
    place = 0
    for n, part in enumerate(parts):
        size = part.shape[0]
        copies.append(
            pltpu.make_async_copy(
                part.at[:, pl.ds(0, rows), :], out.at[pl.ds(place, size)], sems.at[n]
            )
        )
        place += size
    for copy in copies:
        copy.start()
    for copy in copies:
        copy.wait()


def gathered(parts, rows):
    entries = sum(part.shape[0] for part in parts)
    return pl.pallas_call(
        functools.partial(gather_kernel, rows=rows),
        out_shape=jax.ShapeDtypeStruct((entries, rows, HEAD_DIM), jnp.bfloat16),
        in_specs=[pl.BlockSpec(memory_space=pl.ANY)] * len(parts),
        out_specs=pl.BlockSpec(memory_space=pltpu.VMEM),
        scratch_shapes=[pltpu.SemaphoreType.DMA((len(parts),))],
        compiler_params=pltpu.CompilerParams(vmem_limit_bytes=8 * 1024 * 1024),
    )(*parts)


def attend_kernel(places, info, *rest, step, fresh, received):
    refs = list(rest)
    fresh_ref = refs.pop(0) if fresh else None
    received_ref = refs.pop(0) if received else None
    gain_ref, gate_ref, table = refs[:3]
    out_ref, done_ref = refs[-2:]
    section = info[0]
    chunk = step - section * DELAY
    live_keys = info[1] * KEY_BLOCK
    rows = out_ref.shape[0]
    chunk_tokens = done_ref.shape[1] // CHUNKS
    group_rows = GROUP * QUERY_BLOCK
    value_rows = done_ref.shape[1]
    group_sources = group_rows // chunk_tokens

    @pl.when((chunk >= 0) & (chunk < CHUNKS))
    def _():
        base = chunk * (rows // QUERY_BLOCK * SLOTS)
        token0 = pl.multiple_of(chunk * chunk_tokens, chunk_tokens)

        def one_group(index, carry):
            row0 = pl.multiple_of(index * group_rows, group_rows)
            here = pl.ds(row0, group_rows)
            if fresh and received:
                x = jnp.where(section == 0, fresh_ref[here, :], received_ref[here, :])
            else:
                x = (fresh_ref if fresh else received_ref)[here, :]
            wide = x.astype(jnp.float32)
            mean = jnp.mean(wide * wide, axis=-1, keepdims=True)
            queries = (wide * lax.rsqrt(mean + 1e-06) * gain_ref[...]).astype(jnp.bfloat16)
            first = base + index * (GROUP * SLOTS)
            scores = []
            starts = []
            for g in range(GROUP):
                at = [
                    pl.multiple_of(places[first + g * SLOTS + j], KEY_BLOCK)
                    for j in range(SLOTS)
                ]
                starts.append(at)
                keys = jnp.concatenate(
                    [table[pl.ds(a, KEY_BLOCK), :] for a in at], axis=0
                )
                scores.append(
                    lax.dot_general(
                        queries[g * QUERY_BLOCK : (g + 1) * QUERY_BLOCK],
                        keys,
                        (((1,), (1,)), ((), ())),
                        preferred_element_type=jnp.float32,
                    )
                )
            scores = jnp.concatenate(scores, axis=0) * (HEAD_DIM**-0.5)
            lane = lax.broadcasted_iota(jnp.int32, scores.shape, 1)
            scores = jnp.where(lane < live_keys, scores, SCORE_FLOOR)
            highest = jnp.max(scores, axis=-1, keepdims=True)
            exponent = jnp.exp(scores - highest)
            total = jnp.sum(exponent, axis=-1, keepdims=True)
            weights = (exponent / total).astype(jnp.bfloat16)
            summed = []
            for g in range(GROUP):
                values = jnp.concatenate(
                    [table[pl.ds(a + value_rows, KEY_BLOCK), :] for a in starts[g]],
                    axis=0,
                )
                summed.append(
                    jnp.dot(
                        weights[g * QUERY_BLOCK : (g + 1) * QUERY_BLOCK],
                        values,
                        preferred_element_type=jnp.float32,
                    )
                )
            heads = jnp.concatenate(summed, axis=0).astype(jnp.bfloat16)
            updated = wide + gate_ref[...] * heads.astype(jnp.float32)
            updated = updated.astype(jnp.bfloat16)
            out_ref[here, :] = updated
            done_ref[pl.ds(index * group_sources, group_sources), pl.ds(token0, chunk_tokens), :] = (
                updated.reshape(group_sources, chunk_tokens, HEAD_DIM)
            )
            return carry

        lax.fori_loop(0, rows // group_rows, one_group, 0)


def attend(step, places, info, fresh, received, gain, gate, table, done):
    inputs = [value for value in (fresh, received) if value is not None]
    rows, width = inputs[0].shape
    vmem = pl.BlockSpec(memory_space=pltpu.VMEM)
    smem = pl.BlockSpec(memory_space=pltpu.SMEM)
    inputs = [places, info, *inputs, gain, gate, table]
    aliases = {}
    done_shape = (CHUNKS * rows // HEADS // 8, HEADS * 8, width)
    if done is not None:
        aliases = {len(inputs): 1}
        inputs.append(done)
        done_shape = done.shape
    return pl.pallas_call(
        functools.partial(
            attend_kernel,
            step=step,
            fresh=fresh is not None,
            received=received is not None,
        ),
        out_shape=(
            jax.ShapeDtypeStruct((rows, width), jnp.bfloat16),
            jax.ShapeDtypeStruct(done_shape, jnp.bfloat16),
        ),
        in_specs=[smem, smem] + [vmem] * (len(inputs) - 2),
        out_specs=(vmem, vmem),
        input_output_aliases=aliases,
        compiler_params=pltpu.CompilerParams(vmem_limit_bytes=8 * 1024 * 1024),
        cost_estimate=pl.CostEstimate(
            flops=4 * rows * SPAN * HEAD_DIM,
            bytes_accessed=4 * rows * width,
            transcendentals=rows * SPAN,
        ),
    )(*inputs)


def moved(value, rule):
    total = lax.axis_size("seq")
    pairs = []
    for place in range(total):
        z, y, core = place // RINGS, place // 2 % 4, place % 2
        z, y, core = rule(z, y, core)
        pairs.append((place, z % (total // RINGS) * RINGS + y * 2 + core))
    return lax.ppermute(value, "seq", pairs)


def across(value):
    return moved(value, lambda z, y, core: (z, 3 - y, core))


def beside(value):
    return moved(value, lambda z, y, core: (z, y ^ 1, core))


def twin(value):
    return moved(value, lambda z, y, core: (z, y, core ^ 1))


def local(patches, stale_cache, block_lists, block_counts, query_gain, branch_gate):
    section = lax.axis_index("section")
    shard = lax.axis_index("seq")
    depth = lax.axis_size("seq") // RINGS
    z, y, core = shard // RINGS, shard // 2 % 4, shard % 2
    upper = y // 2
    lane = jnp.minimum(y, 3 - y)
    owner = z * 2 + upper
    micro_count, patch_rows, channels = patches.shape
    sources = 2 * depth
    tokens = micro_count * patch_rows
    chunk_tokens = tokens // CHUNKS

    count = lax.dynamic_index_in_dim(block_counts[0], owner, 0, keepdims=False)
    info = jnp.stack([section, count, z, upper]).astype(jnp.int32)
    pieces = list(packed(stale_cache[0], patches))
    for k in range(1, len(SHIFTS)):
        shift = SHIFTS[k]
        pieces[k] = moved(pieces[k], lambda z, y, core: (z + shift, y, core))

    own, others = parted(pieces, 2 * tokens)
    own_beside = beside(own)
    crosses = [across(other) for other in others]
    cross = [value[:, : 2 * tokens] for value in crosses]
    parts = [own, own_beside, *cross, *(beside(value) for value in cross)]
    parts = parts + [twin(part) for part in parts]

    fresh = [arranged(info, pieces, crosses, tokens, chunk_tokens)]
    for c in range(1, CHUNKS):
        fresh.append(lax.ppermute(fresh[0], "section", [(c, 0)]))

    query_blocks = patch_rows // QUERY_BLOCK
    lists = lax.dynamic_index_in_dim(block_lists[0], owner, 0, keepdims=False)
    lists = lists.reshape(micro_count, depth, 4, 2, query_blocks, SLOTS)
    lists = lax.dynamic_index_in_dim(lists, core, 3, keepdims=False)
    lists = jnp.stack(
        [
            lax.dynamic_index_in_dim(lists, lane, 2, keepdims=False),
            lax.dynamic_index_in_dim(lists, 3 - lane, 2, keepdims=False),
        ],
        axis=2,
    )
    lists = lists.reshape(micro_count, sources, query_blocks, SLOTS).transpose(0, 2, 1, 3)
    lists = lists.reshape(CHUNKS, -1, sources, SLOTS).transpose(0, 2, 1, 3)
    per_shard = patch_rows // KEY_BLOCK
    per_micro = per_shard * depth * RINGS
    micro, rest = lists // per_micro, lists % per_micro
    holder, half = rest // per_shard, rest % per_shard
    back = (z + depth - holder // RINGS) % depth
    slot = jnp.where(back <= depth // 2, jnp.maximum(2 * back - 1, 0), 2 * (depth - back))
    row = holder // 2 % 4
    side = jnp.where(
        row == y, 0, jnp.where(row == (y ^ 1), 1, jnp.where(row == 3 - y, 2, 3))
    )
    entry = ((holder % 2 ^ core) * 4 + side) * depth + slot
    places = (entry * 2 * micro_count + micro) * patch_rows + half * KEY_BLOCK
    places = places.reshape(-1)
    gain = lax.dynamic_index_in_dim(query_gain.reshape(HEADS, HEAD_DIM), owner, 0)
    gate = lax.dynamic_index_in_dim(branch_gate.reshape(HEADS, HEAD_DIM), owner, 0)

    table = gathered(parts, 2 * tokens)
    table = table.reshape(-1, HEAD_DIM)

    steps = CHUNKS + (SECTIONS - 1) * DELAY
    sent = []
    result = done = None
    for step in range(steps):
        x = fresh[step] if step < CHUNKS else None
        received = sent[step - DELAY] if step >= DELAY else None
        result, done = attend(
            step, places, info, x, received, gain, gate, table, done
        )
        if step + DELAY < steps:
            sent.append(
                lax.ppermute(result, "section", [(s, s + 1) for s in range(SECTIONS - 1)])
            )
    groups = [
        [place * RINGS + row * 2 + c for place in range(depth) for row in (first, 3 - first)]
        for first in range(2)
        for c in range(2)
    ]
    done = lax.all_to_all(done, "seq", 0, 0, axis_index_groups=groups, tiled=True)
    done = done.reshape(HEADS, micro_count, patch_rows, HEAD_DIM).transpose(1, 2, 0, 3)
    return done.reshape(1, micro_count, patch_rows, channels)


def solution(mesh):
    return jax.shard_map(
        local,
        mesh=mesh,
        in_specs=(
            P(None, "seq", None),
            P("section", None, "seq", None),
            P("section", None, None, None),
            P("section", None),
            P("section", None),
            P("section", None),
        ),
        out_specs=P("section", None, "seq", None),
        check_vma=False,
    )
```

time: 142 us -> 137 us (0.965)
  waiting for transfers between devices: 63.2 us -> 38.2 us
  starting transfers between devices: 27.9 us -> 42.6 us
  Pallas kernels: 16.8 us -> 23.1 us
  blocking collectives: 23.7 us -> 26.1 us
  local copies, waits for them, and re-layouts: 6.99 us -> 5.56 us
    all_to_all x1 -> x0, waiting for transfers between devices: 32.2 us -> none  [local(): lax.all_to_all(jnp.concatenate([by_head, mine], axis=1), OWNERS, 0, 0, ti...]
    ppermute x6 -> x18, starting transfers between devices: 2.54 us -> 26 us  [moved(): return lax.ppermute(value, 'seq', pairs)]
    all_to_all x1 -> x0, starting transfers between devices: 11.3 us -> none  [local(): lax.all_to_all(jnp.concatenate([by_head, mine], axis=1), OWNERS, 0, 0, ti...]
    ppermute x6 -> x18, waiting for transfers between devices: 15.1 us -> 25.3 us  [moved(): return lax.ppermute(value, 'seq', pairs)]
    pallas_call x1 -> x4, Pallas kernels: 0.37 us -> 6.94 us  [the longest x1 3.04 us: packed(): pl.pallas_call(functools.partial(pack_kernel, shifts=SHIFTS), out_shape=(...]
    ppermute x8, waiting for transfers between devices: 16 us -> 12.9 us  [local(): lax.ppermute(result, 'section', [(s, s + 1) for s in range(SECTIONS - 1)])]
    ppermute x3, starting transfers between devices: 3.73 us -> 6.27 us  [local(): fresh.append(lax.ppermute(fresh[0], 'section', [(c, 0)]))]
    all_to_all x1, blocking collectives: 23.7 us -> 26.1 us  [local(): lax.all_to_all(done, 'seq', 0, 0, axis_index_groups=groups, tiled=True)]
  transfers between devices with their start and end apart: 18 -> 29, of which waited for: 12 -> 14; matrix products, arithmetic and copies ran while one was open for 2% -> 2% of each run, Pallas kernels for 9% -> 11%
where the time goes in v4:
time: 137 us
  starting transfers between devices  42.6 us (31%)
  waiting for transfers between devices  38.2 us (28%)
  blocking collectives  26.1 us (19%)
  Pallas kernels  23.1 us (17%)
  local copies, waits for them, and re-layouts  5.56 us (4%)
    all_to_all x1, blocking collectives, local(): lax.all_to_all(done, 'seq', 0, 0, axis_index_groups=groups, tiled=True)  26.1 us
    ppermute x18, starting transfers between devices, moved(): return lax.ppermute(value, 'seq', pairs)  26 us
    ppermute x18, waiting for transfers between devices, moved(): return lax.ppermute(value, 'seq', pairs)  25.3 us
    pallas_call x10, Pallas kernels, attend(): pl.pallas_call(functools.partial(attend_kernel, step=step, fresh=fresh is...  16.1 us
    ppermute x8, waiting for transfers between devices, local(): lax.ppermute(result, 'section', [(s, s + 1) for s in range(SECTIONS - 1)])  12.9 us
    ppermute x8, starting transfers between devices, local(): lax.ppermute(result, 'section', [(s, s + 1) for s in range(SECTIONS - 1)])  10.3 us
    ppermute x3, starting transfers between devices, local(): fresh.append(lax.ppermute(fresh[0], 'section', [(c, 0)]))  6.27 us
    pallas_call x1, Pallas kernels, packed(): pl.pallas_call(functools.partial(pack_kernel, shifts=SHIFTS), out_shape=(...  3.04 us
  transfers between devices with their start and end apart: 29, of which 14 were waited for; matrix products, arithmetic and copies ran while one was open for 2% of the time, Pallas kernels for 11%

profile of v4, /device:TPU:6, one launch (start us, length us, event | category | flops | bytes accessed | tf_op | source)
XLA Modules:
  0.0 137.0 jit_solution(5566932663643128502)
XLA Ops:
  0.0 3.0 %shard_map.64 = (bf16[2,288,128]{2,1,0:T(8,128)(2,1)}, bf16[2,288,128]{2,1,0:T(8,128)(2,1)}, bf16[2,288,128]{2,1,0:T(8,128)(2,1)}, bf16[2,288,128]{2,1,0:T(8,128...) custom-call(bf16[2,64,4096]{2,1,0:T(8,128)(2,1)} %bitcast.36, ...), custom_call_target="tpu_custom_call" | custom-call | tf_op jit(solution)/shard_map/pallas_call | solution.py:71
  3.1 2.0 %collective-permute-start = (bf16[2,288,128]{2,1,0:T(8,128)(2,1)}, bf16[2,288,128]{2,1,0:T(8,128)(2,1)S(1)}, u32[]{:S(2)}, u32[]{:S(2)}) collective-permute-start(bf16[2,288,128]{2,1,0:T(8,128)(2,1)} %get-tuple-element.35), channel_id=1, source_target_pairs={{0,8},{1,9},{2,10},{3,11},{4,12},{5,13},{6,14},{7,15},{8,16},{9,17... | collective-permute-start | bytes 442376 | tf_op jit(solution)/shard_map/ppermute | solution.py:298
  5.0 4.0 %collective-permute-start.1 = (bf16[2,288,128]{2,1,0:T(8,128)(2,1)}, bf16[2,288,128]{2,1,0:T(8,128)(2,1)S(1)}, u32[]{:S(2)}, u32[]{:S(2)}) collective-permute-start(bf16[2,288,128]{2,1,0:T(8,128)(2,1)} %get-tuple-element.36), channel_id=1, source_target_pairs={{0,56},{1,57},{2,58},{3,59},{4,60},{5,61},{6,62},{7,63},{8,0},{9,1... | collective-permute-start | bytes 442376 | tf_op jit(solution)/shard_map/ppermute | solution.py:298
  9.1 4.1 %collective-permute-start.3 = (bf16[2,288,128]{2,1,0:T(8,128)(2,1)}, bf16[2,288,128]{2,1,0:T(8,128)(2,1)S(1)}, u32[]{:S(2)}, u32[]{:S(2)}) collective-permute-start(bf16[2,288,128]{2,1,0:T(8,128)(2,1)} %get-tuple-element.38), channel_id=1, source_target_pairs={{0,48},{1,49},{2,50},{3,51},{4,52},{5,53},{6,54},{7,55},{8,56},{9,... | collective-permute-start | bytes 442376 | tf_op jit(solution)/shard_map/ppermute | solution.py:298
  13.9 4.3 %collective-permute-start.5 = (bf16[2,288,128]{2,1,0:T(8,128)(2,1)}, bf16[2,288,128]{2,1,0:T(8,128)(2,1)S(1)}, u32[]{:S(2)}, u32[]{:S(2)}) collective-permute-start(bf16[2,288,128]{2,1,0:T(8,128)(2,1)} %get-tuple-element.40), channel_id=1, source_target_pairs={{0,40},{1,41},{2,42},{3,43},{4,44},{5,45},{6,46},{7,47},{8,48},{9,... | collective-permute-start | bytes 442376 | tf_op jit(solution)/shard_map/ppermute | solution.py:298
  18.3 4.5 %collective-permute-start.6 = (bf16[2,288,128]{2,1,0:T(8,128)(2,1)}, bf16[2,288,128]{2,1,0:T(8,128)(2,1)S(1)}, u32[]{:S(2)}, u32[]{:S(2)}) collective-permute-start(bf16[2,288,128]{2,1,0:T(8,128)(2,1)} %get-tuple-element.41), channel_id=1, source_target_pairs={{0,32},{1,33},{2,34},{3,35},{4,36},{5,37},{6,38},{7,39},{8,40},{9,... | collective-permute-start | bytes 442376 | tf_op jit(solution)/shard_map/ppermute | solution.py:298
  23.7 9.9 %collective-permute-done.4.refs_5_ = bf16[2,288,128]{2,1,0:T(8,128)(2,1)S(1)} collective-permute-done((bf16[2,288,128]{2,1,0:T(8,128)(2,1)}, bf16[2,288,128]{2,1,0:T(8,128)(2,1)S(1)}, u32[]{:S(2)}, u32[]{:S(2)}) %collective-permute-start.4) | collective-permute-done | bytes 147488 | tf_op jit(solution)/shard_map/ppermute | solution.py:298
  34.5 1.6 %shard_map.65 = (bf16[8,256,128]{2,1,0:T(8,128)(2,1)S(1)}, bf16[4,288,128]{2,1,0:T(8,128)(2,1)S(1)}, bf16[4,288,128]{2,1,0:T(8,128)(2,1)S(1)}) custom-call(bf16[2,288,128]{2,1,0:T(8,128)(2,1)S(1)} %copy-done.1, bf16[2,288,128]{2,1,0:T(8,128)(2,1)S(1)} %collective-permute-done.refs_1_, bf16[2,288,128]{2,1,0:T(8,128)(2,1)S(1)} %collective-permute-done.1.refs_2_, ...), custom_call_target="tpu_custom_call" | custom-call | tf_op jit(solution)/shard_map/pallas_call | solution.py:101
  36.1 1.7 %collective-permute-start.11 = (bf16[8,256,128]{2,1,0:T(8,128)(2,1)S(1)}, bf16[8,256,128]{2,1,0:T(8,128)(2,1)}, u32[]{:S(2)}, u32[]{:S(2)}) collective-permute-start(bf16[8,256,128]{2,1,0:T(8,128)(2,1)S(1)} %get-tuple-element.44.refs_0_), channel_id=1, source_target_pairs={{0,2},{1,3},{2,0},{3,1},{4,6},{5,7},{6,4},{7,5},{8,10},{9,11},{10,... | collective-permute-start | bytes 1572872 | tf_op jit(solution)/shard_map/ppermute | solution.py:298
  37.8 2.2 %collective-permute-start.7 = (bf16[4,288,128]{2,1,0:T(8,128)(2,1)S(1)}, bf16[4,288,128]{2,1,0:T(8,128)(2,1)S(1)}, u32[]{:S(2)}, u32[]{:S(2)}) collective-permute-start(bf16[4,288,128]{2,1,0:T(8,128)(2,1)S(1)} %get-tuple-element.42), channel_id=1, source_target_pairs={{0,6},{1,7},{2,4},{3,5},{4,2},{5,3},{6,0},{7,1},{8,14},{9,15},{10,... | collective-permute-start | bytes 884744 | tf_op jit(solution)/shard_map/ppermute | solution.py:298
  41.3 7.4 %collective-permute-done.7.refs_8_ = bf16[4,288,128]{2,1,0:T(8,128)(2,1)S(1)} collective-permute-done((bf16[4,288,128]{2,1,0:T(8,128)(2,1)S(1)}, bf16[4,288,128]{2,1,0:T(8,128)(2,1)S(1)}, u32[]{:S(2)}, u32[]{:S(2)}) %collective-permute-start.7) | collective-permute-done | bytes 294944 | tf_op jit(solution)/shard_map/ppermute | solution.py:298
  48.9 2.9 %collective-permute-done.8.refs_9_ = bf16[4,288,128]{2,1,0:T(8,128)(2,1)S(1)} collective-permute-done((bf16[4,288,128]{2,1,0:T(8,128)(2,1)S(1)}, bf16[4,288,128]{2,1,0:T(8,128)(2,1)S(1)}, u32[]{:S(2)}, u32[]{:S(2)}) %collective-permute-start.8) | collective-permute-done | bytes 294944 | tf_op jit(solution)/shard_map/ppermute | solution.py:298
  56.2 1.8 %collective-permute-done.12.refs_4_ = bf16[4,256,128]{2,1,0:T(8,128)(2,1)} collective-permute-done((bf16[4,256,128]{2,1,0:T(8,128)(2,1)S(1)}, bf16[4,256,128]{2,1,0:T(8,128)(2,1)}, u32[]{:S(2)}, u32[]{:S(2)}) %collective-permute-start.12) | collective-permute-done | bytes 262176 | tf_op jit(solution)/shard_map/ppermute | solution.py:298
  58.7 2.1 %collective-permute-done.13.refs_5_ = bf16[4,256,128]{2,1,0:T(8,128)(2,1)} collective-permute-done((bf16[4,256,128]{2,1,0:T(8,128)(2,1)S(1)}, bf16[4,256,128]{2,1,0:T(8,128)(2,1)}, u32[]{:S(2)}, u32[]{:S(2)}) %collective-permute-start.13) | collective-permute-done | bytes 262176 | tf_op jit(solution)/shard_map/ppermute | solution.py:298
  63.2 1.7 %shard_map.67 = bf16[64,256,128]{2,1,0:T(8,128)(2,1)S(1)} custom-call(bf16[8,256,128]{2,1,0:T(8,128)(2,1)S(1)} %get-tuple-element.44.refs_0_, bf16[8,256,128]{2,1,0:T(8,128)(2,1)} %collective-permute-done.11.refs_1_, bf16[4,256,128]{2,1,0:T(8,128)(2,1)S(1)} %slice.8.refs_2_, bf16[4,256,128]{2,1,0:T(8,128)(2,1)S(1)} %slice.9.refs_3_, ...), custom_call_target="tpu_custom_call" | custom-call | tf_op jit(solution)/shard_map/pallas_call | solution.py:164
  65.7 1.3 collective-permute-start.22
  67.0 5.0 %collective-permute-start.9 = (bf16[512,128]{1,0:T(8,128)(2,1)S(1)}, bf16[512,128]{1,0:T(8,128)(2,1)S(1)}, u32[]{:S(2)}, u32[]{:S(2)}) collective-permute-start(bf16[512,128]{1,0:T(8,128)(2,1)S(1)} %shard_map.66.rest_0_), channel_id=1, source_target_pairs={{192,0},{193,1},{194,2},{195,3},{196,4},{197,5},{198,6},{199,7},{2... | collective-permute-start | bytes 393224 | tf_op jit(solution)/shard_map/ppermute | solution.py:342
  72.6 1.3 collective-permute-start.20
  74.7 1.3 collective-permute-start.24
  76.0 3.8 %collective-permute-done.20.rest_1_ = bf16[512,128]{1,0:T(8,128)(2,1)S(1)} collective-permute-done((bf16[512,128]{1,0:T(8,128)(2,1)S(1)}, bf16[512,128]{1,0:T(8,128)(2,1)S(1)}, u32[]{:S(2)}, u32[]{:S(2)}) %collective-permute-start.20) | collective-permute-done | bytes 131104 | tf_op jit(solution)/shard_map/ppermute | solution.py:387
  80.5 1.3 collective-permute-start.23
  83.2 1.3 collective-permute-start.26
  84.5 2.9 %collective-permute-done.23.rest_0_ = bf16[512,128]{1,0:T(8,128)(2,1)S(1)} collective-permute-done((bf16[512,128]{1,0:T(8,128)(2,1)S(1)}, bf16[512,128]{1,0:T(8,128)(2,1)S(1)}, u32[]{:S(2)}, u32[]{:S(2)}) %collective-permute-start.23) | collective-permute-done | bytes 131104 | tf_op jit(solution)/shard_map/ppermute | solution.py:387
  89.5 2.4 %collective-permute-done.26.rest_0_ = bf16[512,128]{1,0:T(8,128)(2,1)S(1)} collective-permute-done((bf16[512,128]{1,0:T(8,128)(2,1)S(1)}, bf16[512,128]{1,0:T(8,128)(2,1)S(1)}, u32[]{:S(2)}, u32[]{:S(2)}) %collective-permute-start.26) | collective-permute-done | bytes 131104 | tf_op jit(solution)/shard_map/ppermute | solution.py:387
  91.9 2.6 %shard_map.74 = (bf16[512,128]{1,0:T(8,128)(2,1)S(1)}, bf16[16,128,128]{2,1,0:T(8,128)(2,1)S(1)}) custom-call(s32[2048]{0:T(1024)S(1)} %reshape.36.places, s32[4]{0:T(128)S(1)} %pad_add_fusion.1.info, bf16[512,128]{1,0:T(8,128)(2,1)S(1)} %collective-permute-done.26.rest_0_, ...), custom_call_target="tpu_custom_call", output_to_operand_aliasing={{1}: (6, {})} | custom-call | flops 134217728 | bytes 262144 | tf_op jit(solution)/shard_map/pallas_call | solution.py:268
  94.5 1.3 collective-permute-start.28
  96.7 2.6 %shard_map.75 = (bf16[512,128]{1,0:T(8,128)(2,1)S(1)}, bf16[16,128,128]{2,1,0:T(8,128)(2,1)S(1)}) custom-call(s32[2048]{0:T(1024)S(1)} %reshape.36.places, s32[4]{0:T(128)S(1)} %pad_add_fusion.1.info, bf16[512,128]{1,0:T(8,128)(2,1)S(1)} %collective-permute-done.25.rest_0_, ...), custom_call_target="tpu_custom_call", output_to_operand_aliasing={{1}: (6, {})} | custom-call | flops 134217728 | bytes 262144 | tf_op jit(solution)/shard_map/pallas_call | solution.py:268
  99.3 1.3 collective-permute-start.27
  101.4 3.3 %shard_map.76 = (bf16[512,128]{1,0:T(8,128)(2,1)}, bf16[16,128,128]{2,1,0:T(8,128)(2,1)S(1)}) custom-call(s32[2048]{0:T(1024)S(1)} %reshape.36.places, s32[4]{0:T(128)S(1)} %pad_add_fusion.1.info, bf16[512,128]{1,0:T(8,128)(2,1)S(1)} %collective-permute-done.28.rest_0_, ...), custom_call_target="tpu_custom_call", output_to_operand_aliasing={{1}: (6, {})} | custom-call | flops 134217728 | bytes 262144 | tf_op jit(solution)/shard_map/pallas_call | solution.py:268
  104.7 1.5 %collective-permute-done.27.rest_0_ = bf16[512,128]{1,0:T(8,128)(2,1)S(1)} collective-permute-done((bf16[512,128]{1,0:T(8,128)(2,1)S(1)}, bf16[512,128]{1,0:T(8,128)(2,1)S(1)}, u32[]{:S(2)}, u32[]{:S(2)}) %collective-permute-start.27) | collective-permute-done | bytes 131104 | tf_op jit(solution)/shard_map/ppermute | solution.py:387
  106.2 3.3 %shard_map.77 = (bf16[512,128]{1,0:T(8,128)(2,1)}, bf16[16,128,128]{2,1,0:T(8,128)(2,1)S(1)}) custom-call(s32[2048]{0:T(1024)S(1)} %reshape.36.places, s32[4]{0:T(128)S(1)} %pad_add_fusion.1.info, bf16[512,128]{1,0:T(8,128)(2,1)S(1)} %collective-permute-done.27.rest_0_, ...), custom_call_target="tpu_custom_call", output_to_operand_aliasing={{1}: (6, {})} | custom-call | flops 134217728 | bytes 262144 | tf_op jit(solution)/shard_map/pallas_call | solution.py:268
  109.5 26.1 %all_to_all.5 = bf16[16,128,128]{2,1,0:T(8,128)(2,1)S(1)} all-to-all(bf16[16,128,128]{2,1,0:T(8,128)(2,1)S(1)} %get-tuple-element.62), channel_id=1, replica_groups={{0,6,8,14,16,22,24,30,32,38,40,46,48,54,56,62},{1,7,9,15,17,23,25,31,33..., dimensions={0} | all-to-all | bytes 1048576 | tf_op jit(solution)/shard_map/all_to_all | solution.py:394
  (63 shorter events, 20.8 us)
Async XLA Ops:
  0.0 41.0 %copy-start = (s32[1,16,512,16]{2,3,1,0:T(8,128)S(1)}, s32[1,16,512,16]{2,3,1,0:T(8,128)}, u32[]{:S(2)}) copy-start(s32[1,16,512,16]{2,3,1,0:T(8,128)} %param.8) | copy-start | bytes 1572868
  3.1 10.9 %collective-permute-start = (bf16[2,288,128]{2,1,0:T(8,128)(2,1)}, bf16[2,288,128]{2,1,0:T(8,128)(2,1)S(1)}, u32[]{:S(2)}, u32[]{:S(2)}) collective-permute-start(bf16[2,288,128]{2,1,0:T(8,128)(2,1)} %get-tuple-element.35), channel_id=1, source_target_pairs={{0,8},{1,9},{2,10},{3,11},{4,12},{5,13},{6,14},{7,15},{8,16},{9,17... | collective-permute-start | bytes 442376 | tf_op jit(solution)/shard_map/ppermute | solution.py:298
  5.0 13.2 %collective-permute-start.1 = (bf16[2,288,128]{2,1,0:T(8,128)(2,1)}, bf16[2,288,128]{2,1,0:T(8,128)(2,1)S(1)}, u32[]{:S(2)}, u32[]{:S(2)}) collective-permute-start(bf16[2,288,128]{2,1,0:T(8,128)(2,1)} %get-tuple-element.36), channel_id=1, source_target_pairs={{0,56},{1,57},{2,58},{3,59},{4,60},{5,61},{6,62},{7,63},{8,0},{9,1... | collective-permute-start | bytes 442376 | tf_op jit(solution)/shard_map/ppermute | solution.py:298
  9.1 13.7 %collective-permute-start.2 = (bf16[2,288,128]{2,1,0:T(8,128)(2,1)}, bf16[2,288,128]{2,1,0:T(8,128)(2,1)S(1)}, u32[]{:S(2)}, u32[]{:S(2)}) collective-permute-start(bf16[2,288,128]{2,1,0:T(8,128)(2,1)} %get-tuple-element.37), channel_id=1, source_target_pairs={{0,16},{1,17},{2,18},{3,19},{4,20},{5,21},{6,22},{7,23},{8,24},{9,... | collective-permute-start | bytes 442376 | tf_op jit(solution)/shard_map/ppermute | solution.py:298
  9.1 14.7 %collective-permute-start.3 = (bf16[2,288,128]{2,1,0:T(8,128)(2,1)}, bf16[2,288,128]{2,1,0:T(8,128)(2,1)S(1)}, u32[]{:S(2)}, u32[]{:S(2)}) collective-permute-start(bf16[2,288,128]{2,1,0:T(8,128)(2,1)} %get-tuple-element.38), channel_id=1, source_target_pairs={{0,48},{1,49},{2,50},{3,51},{4,52},{5,53},{6,54},{7,55},{8,56},{9,... | collective-permute-start | bytes 442376 | tf_op jit(solution)/shard_map/ppermute | solution.py:298
  13.2 20.4 %collective-permute-start.4 = (bf16[2,288,128]{2,1,0:T(8,128)(2,1)}, bf16[2,288,128]{2,1,0:T(8,128)(2,1)S(1)}, u32[]{:S(2)}, u32[]{:S(2)}) collective-permute-start(bf16[2,288,128]{2,1,0:T(8,128)(2,1)} %get-tuple-element.39), channel_id=1, source_target_pairs={{0,24},{1,25},{2,26},{3,27},{4,28},{5,29},{6,30},{7,31},{8,32},{9,... | collective-permute-start | bytes 442376 | tf_op jit(solution)/shard_map/ppermute | solution.py:298
  13.9 19.7 %collective-permute-start.5 = (bf16[2,288,128]{2,1,0:T(8,128)(2,1)}, bf16[2,288,128]{2,1,0:T(8,128)(2,1)S(1)}, u32[]{:S(2)}, u32[]{:S(2)}) collective-permute-start(bf16[2,288,128]{2,1,0:T(8,128)(2,1)} %get-tuple-element.40), channel_id=1, source_target_pairs={{0,40},{1,41},{2,42},{3,43},{4,44},{5,45},{6,46},{7,47},{8,48},{9,... | collective-permute-start | bytes 442376 | tf_op jit(solution)/shard_map/ppermute | solution.py:298
  18.3 15.4 %collective-permute-start.6 = (bf16[2,288,128]{2,1,0:T(8,128)(2,1)}, bf16[2,288,128]{2,1,0:T(8,128)(2,1)S(1)}, u32[]{:S(2)}, u32[]{:S(2)}) collective-permute-start(bf16[2,288,128]{2,1,0:T(8,128)(2,1)} %get-tuple-element.41), channel_id=1, source_target_pairs={{0,32},{1,33},{2,34},{3,35},{4,36},{5,37},{6,38},{7,39},{8,40},{9,... | collective-permute-start | bytes 442376 | tf_op jit(solution)/shard_map/ppermute | solution.py:298
  33.6 0.9 copy-start.1
  36.1 15.9 %collective-permute-start.11 = (bf16[8,256,128]{2,1,0:T(8,128)(2,1)S(1)}, bf16[8,256,128]{2,1,0:T(8,128)(2,1)}, u32[]{:S(2)}, u32[]{:S(2)}) collective-permute-start(bf16[8,256,128]{2,1,0:T(8,128)(2,1)S(1)} %get-tuple-element.44.refs_0_), channel_id=1, source_target_pairs={{0,2},{1,3},{2,0},{3,1},{4,6},{5,7},{6,4},{7,5},{8,10},{9,11},{10,... | collective-permute-start | bytes 1572872 | tf_op jit(solution)/shard_map/ppermute | solution.py:298
  37.8 10.9 %collective-permute-start.7 = (bf16[4,288,128]{2,1,0:T(8,128)(2,1)S(1)}, bf16[4,288,128]{2,1,0:T(8,128)(2,1)S(1)}, u32[]{:S(2)}, u32[]{:S(2)}) collective-permute-start(bf16[4,288,128]{2,1,0:T(8,128)(2,1)S(1)} %get-tuple-element.42), channel_id=1, source_target_pairs={{0,6},{1,7},{2,4},{3,5},{4,2},{5,3},{6,0},{7,1},{8,14},{9,15},{10,... | collective-permute-start | bytes 884744 | tf_op jit(solution)/shard_map/ppermute | solution.py:298
  40.0 11.9 %collective-permute-start.8 = (bf16[4,288,128]{2,1,0:T(8,128)(2,1)S(1)}, bf16[4,288,128]{2,1,0:T(8,128)(2,1)S(1)}, u32[]{:S(2)}, u32[]{:S(2)}) collective-permute-start(bf16[4,288,128]{2,1,0:T(8,128)(2,1)S(1)} %get-tuple-element.43), channel_id=1, source_target_pairs={{0,6},{1,7},{2,4},{3,5},{4,2},{5,3},{6,0},{7,1},{8,14},{9,15},{10,... | collective-permute-start | bytes 884744 | tf_op jit(solution)/shard_map/ppermute | solution.py:298
  41.2 14.4 %collective-permute-start.14 = (bf16[8,256,128]{2,1,0:T(8,128)(2,1)S(1)}, bf16[8,256,128]{2,1,0:T(8,128)(2,1)}, u32[]{:S(2)}, u32[]{:S(2)}) collective-permute-start(bf16[8,256,128]{2,1,0:T(8,128)(2,1)S(1)} %get-tuple-element.44.refs_0_), channel_id=1, source_target_pairs={{0,1},{1,0},{2,3},{3,2},{4,5},{5,4},{6,7},{7,6},{8,9},{9,8},{10,11... | collective-permute-start | bytes 1572872 | tf_op jit(solution)/shard_map/ppermute | solution.py:298
  48.7 9.3 %collective-permute-start.12 = (bf16[4,256,128]{2,1,0:T(8,128)(2,1)S(1)}, bf16[4,256,128]{2,1,0:T(8,128)(2,1)}, u32[]{:S(2)}, u32[]{:S(2)}) collective-permute-start(bf16[4,256,128]{2,1,0:T(8,128)(2,1)S(1)} %slice.8.refs_2_), channel_id=1, source_target_pairs={{0,2},{1,3},{2,0},{3,1},{4,6},{5,7},{6,4},{7,5},{8,10},{9,11},{10,... | collective-permute-start | bytes 786440 | tf_op jit(solution)/shard_map/ppermute | solution.py:298
  48.8 12.0 %collective-permute-start.16 = (bf16[4,256,128]{2,1,0:T(8,128)(2,1)S(1)}, bf16[4,256,128]{2,1,0:T(8,128)(2,1)}, u32[]{:S(2)}, u32[]{:S(2)}) collective-permute-start(bf16[4,256,128]{2,1,0:T(8,128)(2,1)S(1)} %slice.8.refs_2_), channel_id=1, source_target_pairs={{0,1},{1,0},{2,3},{3,2},{4,5},{5,4},{6,7},{7,6},{8,9},{9,8},{10,11... | collective-permute-start | bytes 786440 | tf_op jit(solution)/shard_map/ppermute | solution.py:298
  51.9 9.0 %collective-permute-start.13 = (bf16[4,256,128]{2,1,0:T(8,128)(2,1)S(1)}, bf16[4,256,128]{2,1,0:T(8,128)(2,1)}, u32[]{:S(2)}, u32[]{:S(2)}) collective-permute-start(bf16[4,256,128]{2,1,0:T(8,128)(2,1)S(1)} %slice.9.refs_3_), channel_id=1, source_target_pairs={{0,2},{1,3},{2,0},{3,1},{4,6},{5,7},{6,4},{7,5},{8,10},{9,11},{10,... | collective-permute-start | bytes 786440 | tf_op jit(solution)/shard_map/ppermute | solution.py:298
  52.0 11.2 %collective-permute-start.15 = (bf16[8,256,128]{2,1,0:T(8,128)(2,1)}, bf16[8,256,128]{2,1,0:T(8,128)(2,1)}, u32[]{:S(2)}, u32[]{:S(2)}) collective-permute-start(bf16[8,256,128]{2,1,0:T(8,128)(2,1)} %collective-permute-done.11.refs_1_), channel_id=1, source_target_pairs={{0,1},{1,0},{2,3},{3,2},{4,5},{5,4},{6,7},{7,6},{8,9},{9,8},{10,11... | collective-permute-start | bytes 1572872 | tf_op jit(solution)/shard_map/ppermute | solution.py:298
  54.1 0.9 copy-start.2
  55.6 6.9 %collective-permute-start.17 = (bf16[4,256,128]{2,1,0:T(8,128)(2,1)S(1)}, bf16[4,256,128]{2,1,0:T(8,128)(2,1)S(1)}, u32[]{:S(2)}, u32[]{:S(2)}) collective-permute-start(bf16[4,256,128]{2,1,0:T(8,128)(2,1)S(1)} %slice.9.refs_3_), channel_id=1, source_target_pairs={{0,1},{1,0},{2,3},{3,2},{4,5},{5,4},{6,7},{7,6},{8,9},{9,8},{10,11... | collective-permute-start | bytes 786440 | tf_op jit(solution)/shard_map/ppermute | solution.py:298
  58.0 13.9 %collective-permute-start.10 = (bf16[512,128]{1,0:T(8,128)(2,1)S(1)}, bf16[512,128]{1,0:T(8,128)(2,1)S(1)}, u32[]{:S(2)}, u32[]{:S(2)}) collective-permute-start(bf16[512,128]{1,0:T(8,128)(2,1)S(1)} %shard_map.66.rest_0_), channel_id=1, source_target_pairs={{64,0},{65,1},{66,2},{67,3},{68,4},{69,5},{70,6},{71,7},{72,8},{73... | collective-permute-start | bytes 393224 | tf_op jit(solution)/shard_map/ppermute | solution.py:342
  60.8 2.4 %collective-permute-start.18 = (bf16[4,256,128]{2,1,0:T(8,128)(2,1)}, bf16[4,256,128]{2,1,0:T(8,128)(2,1)S(1)}, u32[]{:S(2)}, u32[]{:S(2)}) collective-permute-start(bf16[4,256,128]{2,1,0:T(8,128)(2,1)} %collective-permute-done.12.refs_4_), channel_id=1, source_target_pairs={{0,1},{1,0},{2,3},{3,2},{4,5},{5,4},{6,7},{7,6},{8,9},{9,8},{10,11... | collective-permute-start | bytes 786440 | tf_op jit(solution)/shard_map/ppermute | solution.py:298
  60.8 2.4 %collective-permute-start.19 = (bf16[4,256,128]{2,1,0:T(8,128)(2,1)}, bf16[4,256,128]{2,1,0:T(8,128)(2,1)S(1)}, u32[]{:S(2)}, u32[]{:S(2)}) collective-permute-start(bf16[4,256,128]{2,1,0:T(8,128)(2,1)} %collective-permute-done.13.refs_5_), channel_id=1, source_target_pairs={{0,1},{1,0},{2,3},{3,2},{4,5},{5,4},{6,7},{7,6},{8,9},{9,8},{10,11... | collective-permute-start | bytes 786440 | tf_op jit(solution)/shard_map/ppermute | solution.py:298
  62.5 11.4 %collective-permute-start.21 = (bf16[512,128]{1,0:T(8,128)(2,1)S(1)}, bf16[512,128]{1,0:T(8,128)(2,1)S(1)}, u32[]{:S(2)}, u32[]{:S(2)}) collective-permute-start(bf16[512,128]{1,0:T(8,128)(2,1)S(1)} %shard_map.66.rest_0_), channel_id=1, source_target_pairs={{128,0},{129,1},{130,2},{131,3},{132,4},{133,5},{134,6},{135,7},{1... | collective-permute-start | bytes 393224 | tf_op jit(solution)/shard_map/ppermute | solution.py:342
  65.7 8.3 %collective-permute-start.22 = (bf16[512,128]{1,0:T(8,128)(2,1)S(1)}, bf16[512,128]{1,0:T(8,128)(2,1)S(1)}, u32[]{:S(2)}, u32[]{:S(2)}) collective-permute-start(bf16[512,128]{1,0:T(8,128)(2,1)S(1)} %get-tuple-element.47), channel_id=1, source_target_pairs={{0,64},{64,128},{128,192},{1,65},{65,129},{129,193},{2,66},{66,130... | collective-permute-start | bytes 393224 | tf_op jit(solution)/shard_map/ppermute | solution.py:387
  67.0 9.0 %collective-permute-start.9 = (bf16[512,128]{1,0:T(8,128)(2,1)S(1)}, bf16[512,128]{1,0:T(8,128)(2,1)S(1)}, u32[]{:S(2)}, u32[]{:S(2)}) collective-permute-start(bf16[512,128]{1,0:T(8,128)(2,1)S(1)} %shard_map.66.rest_0_), channel_id=1, source_target_pairs={{192,0},{193,1},{194,2},{195,3},{196,4},{197,5},{198,6},{199,7},{2... | collective-permute-start | bytes 393224 | tf_op jit(solution)/shard_map/ppermute | solution.py:342
  72.6 7.1 %collective-permute-start.20 = (bf16[512,128]{1,0:T(8,128)(2,1)S(1)}, bf16[512,128]{1,0:T(8,128)(2,1)S(1)}, u32[]{:S(2)}, u32[]{:S(2)}) collective-permute-start(bf16[512,128]{1,0:T(8,128)(2,1)S(1)} %get-tuple-element.46), channel_id=1, source_target_pairs={{0,64},{64,128},{128,192},{1,65},{65,129},{129,193},{2,66},{66,130... | collective-permute-start | bytes 393224 | tf_op jit(solution)/shard_map/ppermute | solution.py:387
  74.7 7.8 %collective-permute-start.24 = (bf16[512,128]{1,0:T(8,128)(2,1)S(1)}, bf16[512,128]{1,0:T(8,128)(2,1)S(1)}, u32[]{:S(2)}, u32[]{:S(2)}) collective-permute-start(bf16[512,128]{1,0:T(8,128)(2,1)S(1)} %get-tuple-element.51), channel_id=1, source_target_pairs={{0,64},{64,128},{128,192},{1,65},{65,129},{129,193},{2,66},{66,130... | collective-permute-start | bytes 393224 | tf_op jit(solution)/shard_map/ppermute | solution.py:387
  80.5 6.9 %collective-permute-start.23 = (bf16[512,128]{1,0:T(8,128)(2,1)S(1)}, bf16[512,128]{1,0:T(8,128)(2,1)S(1)}, u32[]{:S(2)}, u32[]{:S(2)}) collective-permute-start(bf16[512,128]{1,0:T(8,128)(2,1)S(1)} %get-tuple-element.50), channel_id=1, source_target_pairs={{0,64},{64,128},{128,192},{1,65},{65,129},{129,193},{2,66},{66,130... | collective-permute-start | bytes 393224 | tf_op jit(solution)/shard_map/ppermute | solution.py:387
  83.2 8.7 %collective-permute-start.26 = (bf16[512,128]{1,0:T(8,128)(2,1)S(1)}, bf16[512,128]{1,0:T(8,128)(2,1)S(1)}, u32[]{:S(2)}, u32[]{:S(2)}) collective-permute-start(bf16[512,128]{1,0:T(8,128)(2,1)S(1)} %get-tuple-element.55), channel_id=1, source_target_pairs={{0,64},{64,128},{128,192},{1,65},{65,129},{129,193},{2,66},{66,130... | collective-permute-start | bytes 393224 | tf_op jit(solution)/shard_map/ppermute | solution.py:387
  88.2 8.5 %collective-permute-start.25 = (bf16[512,128]{1,0:T(8,128)(2,1)S(1)}, bf16[512,128]{1,0:T(8,128)(2,1)S(1)}, u32[]{:S(2)}, u32[]{:S(2)}) collective-permute-start(bf16[512,128]{1,0:T(8,128)(2,1)S(1)} %get-tuple-element.54), channel_id=1, source_target_pairs={{0,64},{64,128},{128,192},{1,65},{65,129},{129,193},{2,66},{66,130... | collective-permute-start | bytes 393224 | tf_op jit(solution)/shard_map/ppermute | solution.py:387
  94.5 6.9 %collective-permute-start.28 = (bf16[512,128]{1,0:T(8,128)(2,1)S(1)}, bf16[512,128]{1,0:T(8,128)(2,1)S(1)}, u32[]{:S(2)}, u32[]{:S(2)}) collective-permute-start(bf16[512,128]{1,0:T(8,128)(2,1)S(1)} %get-tuple-element.59), channel_id=1, source_target_pairs={{0,64},{64,128},{128,192},{1,65},{65,129},{129,193},{2,66},{66,130... | collective-permute-start | bytes 393224 | tf_op jit(solution)/shard_map/ppermute | solution.py:387
  99.3 6.9 %collective-permute-start.27 = (bf16[512,128]{1,0:T(8,128)(2,1)S(1)}, bf16[512,128]{1,0:T(8,128)(2,1)S(1)}, u32[]{:S(2)}, u32[]{:S(2)}) collective-permute-start(bf16[512,128]{1,0:T(8,128)(2,1)S(1)} %get-tuple-element.58), channel_id=1, source_target_pairs={{0,64},{64,128},{128,192},{1,65},{65,129},{129,193},{2,66},{66,130... | collective-permute-start | bytes 393224 | tf_op jit(solution)/shard_map/ppermute | solution.py:387

commit v5 on v4

--- a/solution.py
+++ b/solution.py
@@ -21,6 +21,7 @@
 
 RINGS = 8
 SHIFTS = (0, 1, -1, 2, -2, 3, -3, 4)
+FIRST, REST = (1, 2, 3, 4), (0, 5, 6, 7)
 WAVES = ((0, 1, 2, 3), (4, 5, 6, 7))
 
 
@@ -28,52 +29,47 @@
     outs, sems = refs[: len(shifts)], refs[-1]
     section, shard = lax.axis_index("section"), lax.axis_index("seq")
     z, upper = shard // RINGS, shard // 4 % 2
-    micro_count, rows = cache.shape[:2]
-    depth = len(shifts)
-    channels = patches.shape[2]
-    chunk_tokens = outs[0].shape[1] - 2 * micro_count * rows
-    token0 = section * chunk_tokens
-    fresh_rows = pl.ds(pl.multiple_of(token0 % rows, chunk_tokens), chunk_tokens)
+    tokens, channels = patches.shape
+    chunk_tokens = outs[0].shape[1] - 2 * tokens
+    token0 = pl.multiple_of((section ^ (section // 2)) * chunk_tokens, chunk_tokens)
     copies = []
     for k, shift in enumerate(shifts):
         for other in range(2):
-            head = lax.rem(z + (shift + depth), depth) * 2 + (upper ^ other)
-            slot = len(copies)
-            for which in range(2):
-                start = pl.multiple_of(which * channels + head * HEAD_DIM, HEAD_DIM)
-                for m in range(micro_count):
-                    copies.append(
-                        pltpu.make_async_copy(
-                            cache.at[m, :, pl.ds(start, HEAD_DIM)],
-                            outs[k].at[other, pl.ds((which * micro_count + m) * rows, rows), :],
-                            sems.at[slot + which * micro_count + m],
-                        )
+            head = lax.rem(z + (shift + len(SHIFTS)), len(SHIFTS)) * 2 + (upper ^ other)
+            key0 = pl.multiple_of(head * HEAD_DIM, HEAD_DIM)
+            value0 = pl.multiple_of(channels + head * HEAD_DIM, HEAD_DIM)
+            for which, (source, place, size) in enumerate(
+                (
+                    (cache.at[:, pl.ds(key0, HEAD_DIM)], 0, tokens),
+                    (cache.at[:, pl.ds(value0, HEAD_DIM)], tokens, tokens),
+                    (
+                        patches.at[pl.ds(token0, chunk_tokens), pl.ds(key0, HEAD_DIM)],
+                        2 * tokens,
+                        chunk_tokens,
+                    ),
+                )
+            ):
+                copies.append(
+                    pltpu.make_async_copy(
+                        source, outs[k].at[other, pl.ds(place, size), :], sems.at[len(copies)]
                     )
-            start = pl.multiple_of(head * HEAD_DIM, HEAD_DIM)
-            copies.append(
-                pltpu.make_async_copy(
-                    patches.at[token0 // rows, fresh_rows, pl.ds(start, HEAD_DIM)],
-                    outs[k].at[other, pl.ds(2 * micro_count * rows, chunk_tokens), :],
-                    sems.at[slot + 2 * micro_count],
-                )
-            )
+                )
     for copy in copies:
         copy.start()
     for copy in copies:
         copy.wait()
 
 
-def packed(cache, patches):
-    micro_count, rows, channels = patches.shape
-    tokens = micro_count * rows
+def packed(cache, patches, shifts):
+    tokens = patches.shape[0]
     piece = jax.ShapeDtypeStruct((2, 2 * tokens + tokens // CHUNKS, HEAD_DIM), jnp.bfloat16)
-    count = len(SHIFTS)
+    count = len(shifts)
     return pl.pallas_call(
-        functools.partial(pack_kernel, shifts=SHIFTS),
+        functools.partial(pack_kernel, shifts=shifts),
         out_shape=(piece,) * count,
         in_specs=[pl.BlockSpec(memory_space=pltpu.HBM)] * 2,
         out_specs=(pl.BlockSpec(memory_space=pltpu.VMEM),) * count,
-        scratch_shapes=[pltpu.SemaphoreType.DMA((count * 2 * (2 * micro_count + 1),))],
+        scratch_shapes=[pltpu.SemaphoreType.DMA((count * 6,))],
         compiler_params=pltpu.CompilerParams(vmem_limit_bytes=61 * 1024 * 1024),
     )(cache, patches)
 
@@ -97,7 +93,6 @@
 
 def parted(pieces, rows):
     count = len(pieces)
-    vmem = pl.BlockSpec(memory_space=pltpu.VMEM)
     own, *others = pl.pallas_call(
         functools.partial(part_kernel, count=count),
         out_shape=(
@@ -108,7 +103,7 @@
             ),
         ),
         in_specs=[pl.BlockSpec(memory_space=pl.ANY)] * count,
-        out_specs=(vmem,) * (1 + len(WAVES)),
+        out_specs=(pl.BlockSpec(memory_space=pl.ANY),) * (1 + len(WAVES)),
         scratch_shapes=[pltpu.SemaphoreType.DMA((2, count))],
         compiler_params=pltpu.CompilerParams(vmem_limit_bytes=8 * 1024 * 1024),
     )(*pieces)
@@ -171,10 +166,7 @@
     )(*parts)
 
 
-def attend_kernel(places, info, *rest, step, fresh, received):
-    refs = list(rest)
-    fresh_ref = refs.pop(0) if fresh else None
-    received_ref = refs.pop(0) if received else None
+def attend_kernel(places, info, x_ref, *refs, step):
     gain_ref, gate_ref, table = refs[:3]
     out_ref, done_ref = refs[-2:]
     section = info[0]
@@ -194,11 +186,7 @@
         def one_group(index, carry):
             row0 = pl.multiple_of(index * group_rows, group_rows)
             here = pl.ds(row0, group_rows)
-            if fresh and received:
-                x = jnp.where(section == 0, fresh_ref[here, :], received_ref[here, :])
-            else:
-                x = (fresh_ref if fresh else received_ref)[here, :]
-            wide = x.astype(jnp.float32)
+            wide = x_ref[here, :].astype(jnp.float32)
             mean = jnp.mean(wide * wide, axis=-1, keepdims=True)
             queries = (wide * lax.rsqrt(mean + 1e-06) * gain_ref[...]).astype(jnp.bfloat16)
             first = base + index * (GROUP * SLOTS)
@@ -252,13 +240,18 @@
 
         lax.fori_loop(0, rows // group_rows, one_group, 0)
 
-
-def attend(step, places, info, fresh, received, gain, gate, table, done):
-    inputs = [value for value in (fresh, received) if value is not None]
-    rows, width = inputs[0].shape
+    if step < DELAY:
+
+        @pl.when(section == SECTIONS - 1)
+        def _():
+            out_ref[...] = x_ref[...]
+
+
+def attend(step, places, info, x, gain, gate, table, done):
+    rows, width = x.shape
     vmem = pl.BlockSpec(memory_space=pltpu.VMEM)
     smem = pl.BlockSpec(memory_space=pltpu.SMEM)
-    inputs = [places, info, *inputs, gain, gate, table]
+    inputs = [places, info, x, gain, gate, table]
     aliases = {}
     done_shape = (CHUNKS * rows // HEADS // 8, HEADS * 8, width)
     if done is not None:
@@ -266,12 +259,7 @@
         inputs.append(done)
         done_shape = done.shape
     return pl.pallas_call(
-        functools.partial(
-            attend_kernel,
-            step=step,
-            fresh=fresh is not None,
-            received=received is not None,
-        ),
+        functools.partial(attend_kernel, step=step),
         out_shape=(
             jax.ShapeDtypeStruct((rows, width), jnp.bfloat16),
             jax.ShapeDtypeStruct(done_shape, jnp.bfloat16),
@@ -325,7 +313,11 @@
 
     count = lax.dynamic_index_in_dim(block_counts[0], owner, 0, keepdims=False)
     info = jnp.stack([section, count, z, upper]).astype(jnp.int32)
-    pieces = list(packed(stale_cache[0], patches))
+    rows_in = (stale_cache.reshape(tokens, 2 * channels), patches.reshape(tokens, channels))
+    pieces = [None] * depth
+    for part in FIRST, REST:
+        for k, piece in zip(part, packed(*rows_in, tuple(SHIFTS[k] for k in part))):
+            pieces[k] = piece
     for k in range(1, len(SHIFTS)):
         shift = SHIFTS[k]
         pieces[k] = moved(pieces[k], lambda z, y, core: (z + shift, y, core))
@@ -338,8 +330,7 @@
     parts = parts + [twin(part) for part in parts]
 
     fresh = [arranged(info, pieces, crosses, tokens, chunk_tokens)]
-    for c in range(1, CHUNKS):
-        fresh.append(lax.ppermute(fresh[0], "section", [(c, 0)]))
+    fresh.append(lax.ppermute(fresh[0], "section", [(1, 0), (2, 3)]))
 
     query_blocks = patch_rows // QUERY_BLOCK
     lists = lax.dynamic_index_in_dim(block_lists[0], owner, 0, keepdims=False)
@@ -377,15 +368,12 @@
     sent = []
     result = done = None
     for step in range(steps):
-        x = fresh[step] if step < CHUNKS else None
-        received = sent[step - DELAY] if step >= DELAY else None
-        result, done = attend(
-            step, places, info, x, received, gain, gate, table, done
-        )
+        x = fresh[step] if step < DELAY else sent[step - DELAY]
+        result, done = attend(step, places, info, x, gain, gate, table, done)
         if step + DELAY < steps:
-            sent.append(
-                lax.ppermute(result, "section", [(s, s + 1) for s in range(SECTIONS - 1)])
-            )
+            targets = SECTIONS if step < DELAY else SECTIONS - 1
+            pairs = [(s, (s + 1) % SECTIONS) for s in range(targets)]
+            sent.append(lax.ppermute(result, "section", pairs))
     groups = [
         [place * RINGS + row * 2 + c for place in range(depth) for row in (first, 3 - first)]
         for first in range(2)

time: 137 us -> 135 us (0.985)
  starting transfers between devices: 42.6 us -> 39.2 us
  Pallas kernels: 23.1 us -> 24.7 us
    ppermute x11 -> x9, starting transfers between devices: 16.6 us -> 13.6 us  [the longest x8 12.3 us: local(): sent.append(lax.ppermute(result, 'section', pairs))]
    pallas_call x11 -> x12, Pallas kernels: 19.2 us -> 20.7 us  [the longest x10 16.4 us: attend(): pl.pallas_call(functools.partial(attend_kernel, step=step), out_shape=(ja...]
    ppermute x11 -> x9, waiting for transfers between devices: 12.9 us -> 12.7 us  [the longest x8 12.7 us: local(): sent.append(lax.ppermute(result, 'section', pairs))]
  transfers between devices with their start and end apart: 29 -> 27, of which waited for: 14 -> 14; matrix products, arithmetic and copies ran while one was open for 2% -> 2% of each run, Pallas kernels for 11% -> 13%
where the time goes in v5:
time: 135 us
  starting transfers between devices  39.2 us (29%)
  waiting for transfers between devices  39.2 us (29%)
  blocking collectives  25.6 us (19%)
  Pallas kernels  24.7 us (18%)
  local copies, waits for them, and re-layouts  4.9 us (4%)
    ppermute x18, waiting for transfers between devices, moved(): return lax.ppermute(value, 'seq', pairs)  26.4 us
    ppermute x18, starting transfers between devices, moved(): return lax.ppermute(value, 'seq', pairs)  25.6 us
    all_to_all x1, blocking collectives, local(): lax.all_to_all(done, 'seq', 0, 0, axis_index_groups=groups, tiled=True)  25.6 us
    pallas_call x10, Pallas kernels, attend(): pl.pallas_call(functools.partial(attend_kernel, step=step), out_shape=(ja...  16.4 us
    ppermute x8, waiting for transfers between devices, local(): sent.append(lax.ppermute(result, 'section', pairs))  12.7 us
    ppermute x8, starting transfers between devices, local(): sent.append(lax.ppermute(result, 'section', pairs))  12.3 us
    pallas_call x2, Pallas kernels, packed(): pl.pallas_call(functools.partial(pack_kernel, shifts=shifts), out_shape=(...  4.28 us
  transfers between devices with their start and end apart: 27, of which 14 were waited for; matrix products, arithmetic and copies ran while one was open for 2% of the time, Pallas kernels for 13%

profile of v5, /device:TPU:6, one launch (start us, length us, event | category | flops | bytes accessed | tf_op | source)
XLA Modules:
  0.0 134.9 jit_solution(5022287985988755314)
XLA Ops:
  0.0 2.2 %shard_map.65 = (bf16[2,288,128]{2,1,0:T(8,128)(2,1)}, bf16[2,288,128]{2,1,0:T(8,128)(2,1)}, bf16[2,288,128]{2,1,0:T(8,128)(2,1)}, bf16[2,288,128]{2,1,0:T(8,128)(2,1)}) custom-call(bf16[128,4096]{1,0:T(8,128)(2,1)} %bitcast.36, bf16[128,2048]{1,0:T(8,128)(2,1)} %bitcast.38), custom_call_target="tpu_custom_call" | custom-call | tf_op jit(solution)/shard_map/pallas_call | solution.py:67
  2.2 2.0 %collective-permute-start = (bf16[2,288,128]{2,1,0:T(8,128)(2,1)}, bf16[2,288,128]{2,1,0:T(8,128)(2,1)S(1)}, u32[]{:S(2)}, u32[]{:S(2)}) collective-permute-start(bf16[2,288,128]{2,1,0:T(8,128)(2,1)} %get-tuple-element.35), channel_id=1, source_target_pairs={{0,8},{1,9},{2,10},{3,11},{4,12},{5,13},{6,14},{7,15},{8,16},{9,17... | collective-permute-start | bytes 442376 | tf_op jit(solution)/shard_map/ppermute | solution.py:286
  4.2 4.0 %collective-permute-start.1 = (bf16[2,288,128]{2,1,0:T(8,128)(2,1)}, bf16[2,288,128]{2,1,0:T(8,128)(2,1)S(1)}, u32[]{:S(2)}, u32[]{:S(2)}) collective-permute-start(bf16[2,288,128]{2,1,0:T(8,128)(2,1)} %get-tuple-element.36), channel_id=1, source_target_pairs={{0,56},{1,57},{2,58},{3,59},{4,60},{5,61},{6,62},{7,63},{8,0},{9,1... | collective-permute-start | bytes 442376 | tf_op jit(solution)/shard_map/ppermute | solution.py:286
  8.2 4.1 %collective-permute-start.3 = (bf16[2,288,128]{2,1,0:T(8,128)(2,1)}, bf16[2,288,128]{2,1,0:T(8,128)(2,1)S(1)}, u32[]{:S(2)}, u32[]{:S(2)}) collective-permute-start(bf16[2,288,128]{2,1,0:T(8,128)(2,1)} %get-tuple-element.38), channel_id=1, source_target_pairs={{0,48},{1,49},{2,50},{3,51},{4,52},{5,53},{6,54},{7,55},{8,56},{9,... | collective-permute-start | bytes 442376 | tf_op jit(solution)/shard_map/ppermute | solution.py:286
  12.4 2.1 %shard_map.64 = (bf16[2,288,128]{2,1,0:T(8,128)(2,1)}, bf16[2,288,128]{2,1,0:T(8,128)(2,1)}, bf16[2,288,128]{2,1,0:T(8,128)(2,1)}, bf16[2,288,128]{2,1,0:T(8,128)(2,1)}) custom-call(bf16[128,4096]{1,0:T(8,128)(2,1)} %bitcast.37, bf16[128,2048]{1,0:T(8,128)(2,1)} %bitcast.39), custom_call_target="tpu_custom_call" | custom-call | tf_op jit(solution)/shard_map/pallas_call | solution.py:67
  15.1 4.4 %collective-permute-start.5 = (bf16[2,288,128]{2,1,0:T(8,128)(2,1)}, bf16[2,288,128]{2,1,0:T(8,128)(2,1)S(1)}, u32[]{:S(2)}, u32[]{:S(2)}) collective-permute-start(bf16[2,288,128]{2,1,0:T(8,128)(2,1)} %get-tuple-element.40), channel_id=1, source_target_pairs={{0,40},{1,41},{2,42},{3,43},{4,44},{5,45},{6,46},{7,47},{8,48},{9,... | collective-permute-start | bytes 442376 | tf_op jit(solution)/shard_map/ppermute | solution.py:286
  19.6 4.5 %collective-permute-start.6 = (bf16[2,288,128]{2,1,0:T(8,128)(2,1)}, bf16[2,288,128]{2,1,0:T(8,128)(2,1)S(1)}, u32[]{:S(2)}, u32[]{:S(2)}) collective-permute-start(bf16[2,288,128]{2,1,0:T(8,128)(2,1)} %get-tuple-element.41), channel_id=1, source_target_pairs={{0,32},{1,33},{2,34},{3,35},{4,36},{5,37},{6,38},{7,39},{8,40},{9,... | collective-permute-start | bytes 442376 | tf_op jit(solution)/shard_map/ppermute | solution.py:286
  24.1 8.8 %collective-permute-done.4.refs_5_ = bf16[2,288,128]{2,1,0:T(8,128)(2,1)S(1)} collective-permute-done((bf16[2,288,128]{2,1,0:T(8,128)(2,1)}, bf16[2,288,128]{2,1,0:T(8,128)(2,1)S(1)}, u32[]{:S(2)}, u32[]{:S(2)}) %collective-permute-start.4) | collective-permute-done | bytes 147488 | tf_op jit(solution)/shard_map/ppermute | solution.py:286
  33.8 1.7 %shard_map.66 = (bf16[8,256,128]{2,1,0:T(8,128)(2,1)S(1)}, bf16[4,288,128]{2,1,0:T(8,128)(2,1)S(1)}, bf16[4,288,128]{2,1,0:T(8,128)(2,1)}) custom-call(bf16[2,288,128]{2,1,0:T(8,128)(2,1)S(1)} %copy-done.1, bf16[2,288,128]{2,1,0:T(8,128)(2,1)S(1)} %collective-permute-done.refs_1_, bf16[2,288,128]{2,1,0:T(8,128)(2,1)S(1)} %collective-permute-done.1.refs_2_, ...), custom_call_target="tpu_custom_call" | custom-call | tf_op jit(solution)/shard_map/pallas_call | solution.py:96
  35.5 1.7 %collective-permute-start.10 = (bf16[8,256,128]{2,1,0:T(8,128)(2,1)S(1)}, bf16[8,256,128]{2,1,0:T(8,128)(2,1)}, u32[]{:S(2)}, u32[]{:S(2)}) collective-permute-start(bf16[8,256,128]{2,1,0:T(8,128)(2,1)S(1)} %get-tuple-element.44.refs_0_), channel_id=1, source_target_pairs={{0,2},{1,3},{2,0},{3,1},{4,6},{5,7},{6,4},{7,5},{8,10},{9,11},{10,... | collective-permute-start | bytes 1572872 | tf_op jit(solution)/shard_map/ppermute | solution.py:286
  37.2 2.2 %collective-permute-start.7 = (bf16[4,288,128]{2,1,0:T(8,128)(2,1)S(1)}, bf16[4,288,128]{2,1,0:T(8,128)(2,1)S(1)}, u32[]{:S(2)}, u32[]{:S(2)}) collective-permute-start(bf16[4,288,128]{2,1,0:T(8,128)(2,1)S(1)} %get-tuple-element.42), channel_id=1, source_target_pairs={{0,6},{1,7},{2,4},{3,5},{4,2},{5,3},{6,0},{7,1},{8,14},{9,15},{10,... | collective-permute-start | bytes 884744 | tf_op jit(solution)/shard_map/ppermute | solution.py:286
  40.7 7.6 %collective-permute-done.7.refs_8_ = bf16[4,288,128]{2,1,0:T(8,128)(2,1)S(1)} collective-permute-done((bf16[4,288,128]{2,1,0:T(8,128)(2,1)S(1)}, bf16[4,288,128]{2,1,0:T(8,128)(2,1)S(1)}, u32[]{:S(2)}, u32[]{:S(2)}) %collective-permute-start.7) | collective-permute-done | bytes 294944 | tf_op jit(solution)/shard_map/ppermute | solution.py:286
  48.6 4.1 %collective-permute-done.8.refs_9_ = bf16[4,288,128]{2,1,0:T(8,128)(2,1)S(1)} collective-permute-done((bf16[4,288,128]{2,1,0:T(8,128)(2,1)}, bf16[4,288,128]{2,1,0:T(8,128)(2,1)S(1)}, u32[]{:S(2)}, u32[]{:S(2)}) %collective-permute-start.8) | collective-permute-done | bytes 294944 | tf_op jit(solution)/shard_map/ppermute | solution.py:286
  56.3 1.3 collective-permute-start.9
  57.8 5.1 %collective-permute-done.12.refs_5_ = bf16[4,256,128]{2,1,0:T(8,128)(2,1)} collective-permute-done((bf16[4,256,128]{2,1,0:T(8,128)(2,1)S(1)}, bf16[4,256,128]{2,1,0:T(8,128)(2,1)}, u32[]{:S(2)}, u32[]{:S(2)}) %collective-permute-start.12) | collective-permute-done | bytes 262176 | tf_op jit(solution)/shard_map/ppermute | solution.py:286
  64.7 1.7 %shard_map.68 = bf16[64,256,128]{2,1,0:T(8,128)(2,1)S(1)} custom-call(bf16[8,256,128]{2,1,0:T(8,128)(2,1)S(1)} %get-tuple-element.44.refs_0_, bf16[8,256,128]{2,1,0:T(8,128)(2,1)} %collective-permute-done.10.refs_1_, bf16[4,256,128]{2,1,0:T(8,128)(2,1)S(1)} %slice.8.refs_2_, bf16[4,256,128]{2,1,0:T(8,128)(2,1)S(1)} %slice.9.refs_3_, ...), custom_call_target="tpu_custom_call" | custom-call | tf_op jit(solution)/shard_map/pallas_call | solution.py:159
  67.1 2.5 %collective-permute-start.20 = (bf16[512,128]{1,0:T(8,128)(2,1)S(1)}, bf16[512,128]{1,0:T(8,128)(2,1)S(1)}, u32[]{:S(2)}, u32[]{:S(2)}) collective-permute-start(bf16[512,128]{1,0:T(8,128)(2,1)S(1)} %get-tuple-element.47), channel_id=1, source_target_pairs={{0,64},{64,128},{128,192},{192,0},{1,65},{65,129},{129,193},{193,1... | collective-permute-start | bytes 393224 | tf_op jit(solution)/shard_map/ppermute | solution.py:376
  70.3 2.0 %collective-permute-start.19 = (bf16[512,128]{1,0:T(8,128)(2,1)S(1)}, bf16[512,128]{1,0:T(8,128)(2,1)S(1)}, u32[]{:S(2)}, u32[]{:S(2)}) collective-permute-start(bf16[512,128]{1,0:T(8,128)(2,1)S(1)} %get-tuple-element.46), channel_id=1, source_target_pairs={{0,64},{64,128},{128,192},{192,0},{1,65},{65,129},{129,193},{193,1... | collective-permute-start | bytes 393224 | tf_op jit(solution)/shard_map/ppermute | solution.py:376
  73.4 1.3 collective-permute-start.22
  76.3 1.3 collective-permute-start.21
  77.6 2.9 %collective-permute-done.22.x_ref = bf16[512,128]{1,0:T(8,128)(2,1)S(1)} collective-permute-done((bf16[512,128]{1,0:T(8,128)(2,1)S(1)}, bf16[512,128]{1,0:T(8,128)(2,1)S(1)}, u32[]{:S(2)}, u32[]{:S(2)}) %collective-permute-start.22) | collective-permute-done | bytes 131104 | tf_op jit(solution)/shard_map/ppermute | solution.py:376
  81.4 1.3 collective-permute-start.24
  83.9 1.3 collective-permute-start.23
  85.2 5.2 %collective-permute-done.24.x_ref = bf16[512,128]{1,0:T(8,128)(2,1)S(1)} collective-permute-done((bf16[512,128]{1,0:T(8,128)(2,1)S(1)}, bf16[512,128]{1,0:T(8,128)(2,1)S(1)}, u32[]{:S(2)}, u32[]{:S(2)}) %collective-permute-start.24) | collective-permute-done | bytes 131104 | tf_op jit(solution)/shard_map/ppermute | solution.py:376
  90.3 2.6 %shard_map.75 = (bf16[512,128]{1,0:T(8,128)(2,1)S(1)}, bf16[16,128,128]{2,1,0:T(8,128)(2,1)S(1)}) custom-call(s32[2048]{0:T(1024)S(1)} %reshape.42.places, s32[4]{0:T(128)S(1)} %pad_add_fusion.1.info, bf16[512,128]{1,0:T(8,128)(2,1)S(1)} %collective-permute-done.24.x_ref, f32[1,128]{1,0:T(1,128)S(1)} %get-tuple-element.66.refs_0_, ...), custom_call_target="tpu_custom_call", output_to_operand_aliasing={{1}: (6, {})} | custom-call | flops 134217728 | bytes 262144 | tf_op jit(solution)/shard_map/pallas_call | solution.py:261
  93.0 1.3 collective-permute-start.26
  94.9 2.6 %shard_map.76 = (bf16[512,128]{1,0:T(8,128)(2,1)S(1)}, bf16[16,128,128]{2,1,0:T(8,128)(2,1)S(1)}) custom-call(s32[2048]{0:T(1024)S(1)} %reshape.42.places, s32[4]{0:T(128)S(1)} %pad_add_fusion.1.info, bf16[512,128]{1,0:T(8,128)(2,1)S(1)} %collective-permute-done.23.x_ref, f32[1,128]{1,0:T(1,128)S(1)} %get-tuple-element.66.refs_0_, ...), custom_call_target="tpu_custom_call", output_to_operand_aliasing={{1}: (6, {})} | custom-call | flops 134217728 | bytes 262144 | tf_op jit(solution)/shard_map/pallas_call | solution.py:261
  97.5 1.3 collective-permute-start.25
  99.8 3.3 %shard_map.77 = (bf16[512,128]{1,0:T(8,128)(2,1)}, bf16[16,128,128]{2,1,0:T(8,128)(2,1)S(1)}) custom-call(s32[2048]{0:T(1024)S(1)} %reshape.42.places, s32[4]{0:T(128)S(1)} %pad_add_fusion.1.info, bf16[512,128]{1,0:T(8,128)(2,1)S(1)} %collective-permute-done.26.x_ref, f32[1,128]{1,0:T(1,128)S(1)} %get-tuple-element.66.refs_0_, ...), custom_call_target="tpu_custom_call", output_to_operand_aliasing={{1}: (6, {})} | custom-call | flops 134217728 | bytes 262144 | tf_op jit(solution)/shard_map/pallas_call | solution.py:261
  103.1 1.3 collective-permute-done.25.x_ref
  104.4 3.6 %shard_map.78 = (bf16[512,128]{1,0:T(8,128)(2,1)}, bf16[16,128,128]{2,1,0:T(8,128)(2,1)S(1)}) custom-call(s32[2048]{0:T(1024)S(1)} %reshape.42.places, s32[4]{0:T(128)S(1)} %pad_add_fusion.1.info, bf16[512,128]{1,0:T(8,128)(2,1)S(1)} %collective-permute-done.25.x_ref, f32[1,128]{1,0:T(1,128)S(1)} %get-tuple-element.66.refs_0_, ...), custom_call_target="tpu_custom_call", output_to_operand_aliasing={{1}: (6, {})} | custom-call | flops 134217728 | bytes 262144 | tf_op jit(solution)/shard_map/pallas_call | solution.py:261
  108.0 25.6 %all_to_all.5 = bf16[16,128,128]{2,1,0:T(8,128)(2,1)S(1)} all-to-all(bf16[16,128,128]{2,1,0:T(8,128)(2,1)S(1)} %get-tuple-element.62), channel_id=1, replica_groups={{0,6,8,14,16,22,24,30,32,38,40,46,48,54,56,62},{1,7,9,15,17,23,25,31,33..., dimensions={0} | all-to-all | bytes 1048576 | tf_op jit(solution)/shard_map/all_to_all | solution.py:382
  (62 shorter events, 17.7 us)
Async XLA Ops:
  0.0 40.4 %copy-start = (s32[1,16,512,16]{2,3,1,0:T(8,128)S(1)}, s32[1,16,512,16]{2,3,1,0:T(8,128)}, u32[]{:S(2)}) copy-start(s32[1,16,512,16]{2,3,1,0:T(8,128)} %param.8) | copy-start | bytes 1572868
  0.0 52.8 %copy-start.3 = (s32[1,16]{1,0:T(1,128)S(1)}, s32[1,16]{1,0:T(1,128)}, u32[]{:S(2)}) copy-start(s32[1,16]{1,0:T(1,128)} %param.9) | copy-start | bytes 196
  2.2 12.9 %collective-permute-start = (bf16[2,288,128]{2,1,0:T(8,128)(2,1)}, bf16[2,288,128]{2,1,0:T(8,128)(2,1)S(1)}, u32[]{:S(2)}, u32[]{:S(2)}) collective-permute-start(bf16[2,288,128]{2,1,0:T(8,128)(2,1)} %get-tuple-element.35), channel_id=1, source_target_pairs={{0,8},{1,9},{2,10},{3,11},{4,12},{5,13},{6,14},{7,15},{8,16},{9,17... | collective-permute-start | bytes 442376 | tf_op jit(solution)/shard_map/ppermute | solution.py:286
  4.2 15.4 %collective-permute-start.1 = (bf16[2,288,128]{2,1,0:T(8,128)(2,1)}, bf16[2,288,128]{2,1,0:T(8,128)(2,1)S(1)}, u32[]{:S(2)}, u32[]{:S(2)}) collective-permute-start(bf16[2,288,128]{2,1,0:T(8,128)(2,1)} %get-tuple-element.36), channel_id=1, source_target_pairs={{0,56},{1,57},{2,58},{3,59},{4,60},{5,61},{6,62},{7,63},{8,0},{9,1... | collective-permute-start | bytes 442376 | tf_op jit(solution)/shard_map/ppermute | solution.py:286
  8.2 15.8 %collective-permute-start.2 = (bf16[2,288,128]{2,1,0:T(8,128)(2,1)}, bf16[2,288,128]{2,1,0:T(8,128)(2,1)S(1)}, u32[]{:S(2)}, u32[]{:S(2)}) collective-permute-start(bf16[2,288,128]{2,1,0:T(8,128)(2,1)} %get-tuple-element.37), channel_id=1, source_target_pairs={{0,16},{1,17},{2,18},{3,19},{4,20},{5,21},{6,22},{7,23},{8,24},{9,... | collective-permute-start | bytes 442376 | tf_op jit(solution)/shard_map/ppermute | solution.py:286
  8.2 15.8 %collective-permute-start.3 = (bf16[2,288,128]{2,1,0:T(8,128)(2,1)}, bf16[2,288,128]{2,1,0:T(8,128)(2,1)S(1)}, u32[]{:S(2)}, u32[]{:S(2)}) collective-permute-start(bf16[2,288,128]{2,1,0:T(8,128)(2,1)} %get-tuple-element.38), channel_id=1, source_target_pairs={{0,48},{1,49},{2,50},{3,51},{4,52},{5,53},{6,54},{7,55},{8,56},{9,... | collective-permute-start | bytes 442376 | tf_op jit(solution)/shard_map/ppermute | solution.py:286
  14.5 18.4 %collective-permute-start.4 = (bf16[2,288,128]{2,1,0:T(8,128)(2,1)}, bf16[2,288,128]{2,1,0:T(8,128)(2,1)S(1)}, u32[]{:S(2)}, u32[]{:S(2)}) collective-permute-start(bf16[2,288,128]{2,1,0:T(8,128)(2,1)} %get-tuple-element.39), channel_id=1, source_target_pairs={{0,24},{1,25},{2,26},{3,27},{4,28},{5,29},{6,30},{7,31},{8,32},{9,... | collective-permute-start | bytes 442376 | tf_op jit(solution)/shard_map/ppermute | solution.py:286
  15.1 17.7 %collective-permute-start.5 = (bf16[2,288,128]{2,1,0:T(8,128)(2,1)}, bf16[2,288,128]{2,1,0:T(8,128)(2,1)S(1)}, u32[]{:S(2)}, u32[]{:S(2)}) collective-permute-start(bf16[2,288,128]{2,1,0:T(8,128)(2,1)} %get-tuple-element.40), channel_id=1, source_target_pairs={{0,40},{1,41},{2,42},{3,43},{4,44},{5,45},{6,46},{7,47},{8,48},{9,... | collective-permute-start | bytes 442376 | tf_op jit(solution)/shard_map/ppermute | solution.py:286
  19.6 13.3 %collective-permute-start.6 = (bf16[2,288,128]{2,1,0:T(8,128)(2,1)}, bf16[2,288,128]{2,1,0:T(8,128)(2,1)S(1)}, u32[]{:S(2)}, u32[]{:S(2)}) collective-permute-start(bf16[2,288,128]{2,1,0:T(8,128)(2,1)} %get-tuple-element.41), channel_id=1, source_target_pairs={{0,32},{1,33},{2,34},{3,35},{4,36},{5,37},{6,38},{7,39},{8,40},{9,... | collective-permute-start | bytes 442376 | tf_op jit(solution)/shard_map/ppermute | solution.py:286
  32.9 0.9 copy-start.1
  35.5 17.9 %collective-permute-start.10 = (bf16[8,256,128]{2,1,0:T(8,128)(2,1)S(1)}, bf16[8,256,128]{2,1,0:T(8,128)(2,1)}, u32[]{:S(2)}, u32[]{:S(2)}) collective-permute-start(bf16[8,256,128]{2,1,0:T(8,128)(2,1)S(1)} %get-tuple-element.44.refs_0_), channel_id=1, source_target_pairs={{0,2},{1,3},{2,0},{3,1},{4,6},{5,7},{6,4},{7,5},{8,10},{9,11},{10,... | collective-permute-start | bytes 1572872 | tf_op jit(solution)/shard_map/ppermute | solution.py:286
  37.2 11.2 %collective-permute-start.7 = (bf16[4,288,128]{2,1,0:T(8,128)(2,1)S(1)}, bf16[4,288,128]{2,1,0:T(8,128)(2,1)S(1)}, u32[]{:S(2)}, u32[]{:S(2)}) collective-permute-start(bf16[4,288,128]{2,1,0:T(8,128)(2,1)S(1)} %get-tuple-element.42), channel_id=1, source_target_pairs={{0,6},{1,7},{2,4},{3,5},{4,2},{5,3},{6,0},{7,1},{8,14},{9,15},{10,... | collective-permute-start | bytes 884744 | tf_op jit(solution)/shard_map/ppermute | solution.py:286
  39.4 13.3 %collective-permute-start.8 = (bf16[4,288,128]{2,1,0:T(8,128)(2,1)}, bf16[4,288,128]{2,1,0:T(8,128)(2,1)S(1)}, u32[]{:S(2)}, u32[]{:S(2)}) collective-permute-start(bf16[4,288,128]{2,1,0:T(8,128)(2,1)} %get-tuple-element.43), channel_id=1, source_target_pairs={{0,6},{1,7},{2,4},{3,5},{4,2},{5,3},{6,0},{7,1},{8,14},{9,15},{10,... | collective-permute-start | bytes 884744 | tf_op jit(solution)/shard_map/ppermute | solution.py:286
  40.6 15.2 %collective-permute-start.13 = (bf16[8,256,128]{2,1,0:T(8,128)(2,1)S(1)}, bf16[8,256,128]{2,1,0:T(8,128)(2,1)}, u32[]{:S(2)}, u32[]{:S(2)}) collective-permute-start(bf16[8,256,128]{2,1,0:T(8,128)(2,1)S(1)} %get-tuple-element.44.refs_0_), channel_id=1, source_target_pairs={{0,1},{1,0},{2,3},{3,2},{4,5},{5,4},{6,7},{7,6},{8,9},{9,8},{10,11... | collective-permute-start | bytes 1572872 | tf_op jit(solution)/shard_map/ppermute | solution.py:286
  48.4 8.0 %collective-permute-start.15 = (bf16[4,256,128]{2,1,0:T(8,128)(2,1)S(1)}, bf16[4,256,128]{2,1,0:T(8,128)(2,1)}, u32[]{:S(2)}, u32[]{:S(2)}) collective-permute-start(bf16[4,256,128]{2,1,0:T(8,128)(2,1)S(1)} %slice.8.refs_2_), channel_id=1, source_target_pairs={{0,1},{1,0},{2,3},{3,2},{4,5},{5,4},{6,7},{7,6},{8,9},{9,8},{10,11... | collective-permute-start | bytes 786440 | tf_op jit(solution)/shard_map/ppermute | solution.py:286
  48.5 9.3 %collective-permute-start.11 = (bf16[4,256,128]{2,1,0:T(8,128)(2,1)S(1)}, bf16[4,256,128]{2,1,0:T(8,128)(2,1)}, u32[]{:S(2)}, u32[]{:S(2)}) collective-permute-start(bf16[4,256,128]{2,1,0:T(8,128)(2,1)S(1)} %slice.8.refs_2_), channel_id=1, source_target_pairs={{0,2},{1,3},{2,0},{3,1},{4,6},{5,7},{6,4},{7,5},{8,10},{9,11},{10,... | collective-permute-start | bytes 786440 | tf_op jit(solution)/shard_map/ppermute | solution.py:286
  52.7 10.2 %collective-permute-start.12 = (bf16[4,256,128]{2,1,0:T(8,128)(2,1)S(1)}, bf16[4,256,128]{2,1,0:T(8,128)(2,1)}, u32[]{:S(2)}, u32[]{:S(2)}) collective-permute-start(bf16[4,256,128]{2,1,0:T(8,128)(2,1)S(1)} %slice.9.refs_3_), channel_id=1, source_target_pairs={{0,2},{1,3},{2,0},{3,1},{4,6},{5,7},{6,4},{7,5},{8,10},{9,11},{10,... | collective-permute-start | bytes 786440 | tf_op jit(solution)/shard_map/ppermute | solution.py:286
  53.4 11.3 %collective-permute-start.14 = (bf16[8,256,128]{2,1,0:T(8,128)(2,1)}, bf16[8,256,128]{2,1,0:T(8,128)(2,1)}, u32[]{:S(2)}, u32[]{:S(2)}) collective-permute-start(bf16[8,256,128]{2,1,0:T(8,128)(2,1)} %collective-permute-done.10.refs_1_), channel_id=1, source_target_pairs={{0,1},{1,0},{2,3},{3,2},{4,5},{5,4},{6,7},{7,6},{8,9},{9,8},{10,11... | collective-permute-start | bytes 1572872 | tf_op jit(solution)/shard_map/ppermute | solution.py:286
  54.2 0.9 copy-start.2
  55.7 8.4 %collective-permute-start.16 = (bf16[4,256,128]{2,1,0:T(8,128)(2,1)S(1)}, bf16[4,256,128]{2,1,0:T(8,128)(2,1)S(1)}, u32[]{:S(2)}, u32[]{:S(2)}) collective-permute-start(bf16[4,256,128]{2,1,0:T(8,128)(2,1)S(1)} %slice.9.refs_3_), channel_id=1, source_target_pairs={{0,1},{1,0},{2,3},{3,2},{4,5},{5,4},{6,7},{7,6},{8,9},{9,8},{10,11... | collective-permute-start | bytes 786440 | tf_op jit(solution)/shard_map/ppermute | solution.py:286
  56.3 13.3 %collective-permute-start.9 = (bf16[512,128]{1,0:T(8,128)(2,1)S(1)}, bf16[512,128]{1,0:T(8,128)(2,1)S(1)}, u32[]{:S(2)}, u32[]{:S(2)}) collective-permute-start(bf16[512,128]{1,0:T(8,128)(2,1)S(1)} %shard_map.67.x_ref), channel_id=1, source_target_pairs={{64,0},{128,192},{65,1},{129,193},{66,2},{130,194},{67,3},{131,195... | collective-permute-start | bytes 393224 | tf_op jit(solution)/shard_map/ppermute | solution.py:333
  57.8 6.3 %collective-permute-start.17 = (bf16[4,256,128]{2,1,0:T(8,128)(2,1)}, bf16[4,256,128]{2,1,0:T(8,128)(2,1)S(1)}, u32[]{:S(2)}, u32[]{:S(2)}) collective-permute-start(bf16[4,256,128]{2,1,0:T(8,128)(2,1)} %collective-permute-done.11.refs_4_), channel_id=1, source_target_pairs={{0,1},{1,0},{2,3},{3,2},{4,5},{5,4},{6,7},{7,6},{8,9},{9,8},{10,11... | collective-permute-start | bytes 786440 | tf_op jit(solution)/shard_map/ppermute | solution.py:286
  62.9 1.7 %collective-permute-start.18 = (bf16[4,256,128]{2,1,0:T(8,128)(2,1)}, bf16[4,256,128]{2,1,0:T(8,128)(2,1)S(1)}, u32[]{:S(2)}, u32[]{:S(2)}) collective-permute-start(bf16[4,256,128]{2,1,0:T(8,128)(2,1)} %collective-permute-done.12.refs_5_), channel_id=1, source_target_pairs={{0,1},{1,0},{2,3},{3,2},{4,5},{5,4},{6,7},{7,6},{8,9},{9,8},{10,11... | collective-permute-start | bytes 786440 | tf_op jit(solution)/shard_map/ppermute | solution.py:286
  67.1 5.6 %collective-permute-start.20 = (bf16[512,128]{1,0:T(8,128)(2,1)S(1)}, bf16[512,128]{1,0:T(8,128)(2,1)S(1)}, u32[]{:S(2)}, u32[]{:S(2)}) collective-permute-start(bf16[512,128]{1,0:T(8,128)(2,1)S(1)} %get-tuple-element.47), channel_id=1, source_target_pairs={{0,64},{64,128},{128,192},{192,0},{1,65},{65,129},{129,193},{193,1... | collective-permute-start | bytes 393224 | tf_op jit(solution)/shard_map/ppermute | solution.py:376
  70.3 5.3 %collective-permute-start.19 = (bf16[512,128]{1,0:T(8,128)(2,1)S(1)}, bf16[512,128]{1,0:T(8,128)(2,1)S(1)}, u32[]{:S(2)}, u32[]{:S(2)}) collective-permute-start(bf16[512,128]{1,0:T(8,128)(2,1)S(1)} %get-tuple-element.46), channel_id=1, source_target_pairs={{0,64},{64,128},{128,192},{192,0},{1,65},{65,129},{129,193},{193,1... | collective-permute-start | bytes 393224 | tf_op jit(solution)/shard_map/ppermute | solution.py:376
  73.4 7.1 %collective-permute-start.22 = (bf16[512,128]{1,0:T(8,128)(2,1)S(1)}, bf16[512,128]{1,0:T(8,128)(2,1)S(1)}, u32[]{:S(2)}, u32[]{:S(2)}) collective-permute-start(bf16[512,128]{1,0:T(8,128)(2,1)S(1)} %get-tuple-element.51), channel_id=1, source_target_pairs={{0,64},{64,128},{128,192},{1,65},{65,129},{129,193},{2,66},{66,130... | collective-permute-start | bytes 393224 | tf_op jit(solution)/shard_map/ppermute | solution.py:376
  76.3 6.9 %collective-permute-start.21 = (bf16[512,128]{1,0:T(8,128)(2,1)S(1)}, bf16[512,128]{1,0:T(8,128)(2,1)S(1)}, u32[]{:S(2)}, u32[]{:S(2)}) collective-permute-start(bf16[512,128]{1,0:T(8,128)(2,1)S(1)} %get-tuple-element.50), channel_id=1, source_target_pairs={{0,64},{64,128},{128,192},{1,65},{65,129},{129,193},{2,66},{66,130... | collective-permute-start | bytes 393224 | tf_op jit(solution)/shard_map/ppermute | solution.py:376
  81.4 8.9 %collective-permute-start.24 = (bf16[512,128]{1,0:T(8,128)(2,1)S(1)}, bf16[512,128]{1,0:T(8,128)(2,1)S(1)}, u32[]{:S(2)}, u32[]{:S(2)}) collective-permute-start(bf16[512,128]{1,0:T(8,128)(2,1)S(1)} %get-tuple-element.55), channel_id=1, source_target_pairs={{0,64},{64,128},{128,192},{1,65},{65,129},{129,193},{2,66},{66,130... | collective-permute-start | bytes 393224 | tf_op jit(solution)/shard_map/ppermute | solution.py:376
  83.9 11.0 %collective-permute-start.23 = (bf16[512,128]{1,0:T(8,128)(2,1)S(1)}, bf16[512,128]{1,0:T(8,128)(2,1)S(1)}, u32[]{:S(2)}, u32[]{:S(2)}) collective-permute-start(bf16[512,128]{1,0:T(8,128)(2,1)S(1)} %get-tuple-element.54), channel_id=1, source_target_pairs={{0,64},{64,128},{128,192},{1,65},{65,129},{129,193},{2,66},{66,130... | collective-permute-start | bytes 393224 | tf_op jit(solution)/shard_map/ppermute | solution.py:376
  93.0 6.9 %collective-permute-start.26 = (bf16[512,128]{1,0:T(8,128)(2,1)S(1)}, bf16[512,128]{1,0:T(8,128)(2,1)S(1)}, u32[]{:S(2)}, u32[]{:S(2)}) collective-permute-start(bf16[512,128]{1,0:T(8,128)(2,1)S(1)} %get-tuple-element.59), channel_id=1, source_target_pairs={{0,64},{64,128},{128,192},{1,65},{65,129},{129,193},{2,66},{66,130... | collective-permute-start | bytes 393224 | tf_op jit(solution)/shard_map/ppermute | solution.py:376
  97.5 6.9 %collective-permute-start.25 = (bf16[512,128]{1,0:T(8,128)(2,1)S(1)}, bf16[512,128]{1,0:T(8,128)(2,1)S(1)}, u32[]{:S(2)}, u32[]{:S(2)}) collective-permute-start(bf16[512,128]{1,0:T(8,128)(2,1)S(1)} %get-tuple-element.58), channel_id=1, source_target_pairs={{0,64},{64,128},{128,192},{1,65},{65,129},{129,193},{2,66},{66,130... | collective-permute-start | bytes 393224 | tf_op jit(solution)/shard_map/ppermute | solution.py:376

commit v6 on v5

--- a/solution.py
+++ b/solution.py
@@ -274,6 +274,30 @@
             transcendentals=rows * SPAN,
         ),
     )(*inputs)
+
+
+def merge_kernel(done, out, sems):
+    copies = []
+    for head in range(HEADS):
+        lanes = pl.ds(head * HEAD_DIM, HEAD_DIM)
+        copies.append(pltpu.make_async_copy(done.at[head], out.at[:, lanes], sems.at[head]))
+    for copy in copies:
+        copy.start()
+    for copy in copies:
+        copy.wait()
+
+
+def merged(done):
+    heads, tokens, width = done.shape
+    space = pl.BlockSpec(memory_space=pl.ANY)
+    return pl.pallas_call(
+        merge_kernel,
+        out_shape=jax.ShapeDtypeStruct((tokens, heads * width), jnp.bfloat16),
+        in_specs=[space],
+        out_specs=space,
+        scratch_shapes=[pltpu.SemaphoreType.DMA((heads,))],
+        compiler_params=pltpu.CompilerParams(vmem_limit_bytes=8 * 1024 * 1024),
+    )(done)
 
 
 def moved(value, rule):
@@ -380,8 +404,7 @@
         for c in range(2)
     ]
     done = lax.all_to_all(done, "seq", 0, 0, axis_index_groups=groups, tiled=True)
-    done = done.reshape(HEADS, micro_count, patch_rows, HEAD_DIM).transpose(1, 2, 0, 3)
-    return done.reshape(1, micro_count, patch_rows, channels)
+    return merged(done).reshape(1, micro_count, patch_rows, channels)
 
 
 def solution(mesh):

time: 135 us -> 135 us (level)
  local copies, waits for them, and re-layouts: 4.9 us -> 3.54 us
where the time goes in v6:
time: 135 us; the launch traced here: 134 us
  starting transfers between devices  39.2 us (29%)
  waiting for transfers between devices  39.2 us (29%)
  blocking collectives  25.6 us (19%)
  Pallas kernels  25.4 us (19%)
  local copies, waits for them, and re-layouts  3.54 us (3%)
    ppermute x18, waiting for transfers between devices, moved(): return lax.ppermute(value, 'seq', pairs)  26.4 us
    ppermute x18, starting transfers between devices, moved(): return lax.ppermute(value, 'seq', pairs)  25.6 us
    all_to_all x1, blocking collectives, local(): lax.all_to_all(done, 'seq', 0, 0, axis_index_groups=groups, tiled=True)  25.6 us
    pallas_call x10, Pallas kernels, attend(): pl.pallas_call(functools.partial(attend_kernel, step=step), out_shape=(ja...  16.2 us
    ppermute x8, waiting for transfers between devices, local(): sent.append(lax.ppermute(result, 'section', pairs))  12.7 us
    ppermute x8, starting transfers between devices, local(): sent.append(lax.ppermute(result, 'section', pairs))  12.3 us
    pallas_call x2, Pallas kernels, packed(): pl.pallas_call(functools.partial(pack_kernel, shifts=shifts), out_shape=(...  4.28 us
  transfers between devices with their start and end apart: 27, of which 14 were waited for; matrix products, arithmetic and copies ran while one was open for 2% of the time, Pallas kernels for 13%

profile of v6, /device:TPU:6, one launch (start us, length us, event | category | flops | bytes accessed | tf_op | source)
XLA Modules:
  0.0 134.3 jit_solution(7099128802392018295)
XLA Ops:
  0.0 2.2 %shard_map.65 = (bf16[2,288,128]{2,1,0:T(8,128)(2,1)}, bf16[2,288,128]{2,1,0:T(8,128)(2,1)}, bf16[2,288,128]{2,1,0:T(8,128)(2,1)}, bf16[2,288,128]{2,1,0:T(8,128)(2,1)}) custom-call(bf16[128,4096]{1,0:T(8,128)(2,1)} %bitcast.32, bf16[128,2048]{1,0:T(8,128)(2,1)} %bitcast.34), custom_call_target="tpu_custom_call" | custom-call | tf_op jit(solution)/shard_map/pallas_call | solution.py:67
  2.2 2.0 %collective-permute-start = (bf16[2,288,128]{2,1,0:T(8,128)(2,1)}, bf16[2,288,128]{2,1,0:T(8,128)(2,1)S(1)}, u32[]{:S(2)}, u32[]{:S(2)}) collective-permute-start(bf16[2,288,128]{2,1,0:T(8,128)(2,1)} %get-tuple-element.35), channel_id=1, source_target_pairs={{0,8},{1,9},{2,10},{3,11},{4,12},{5,13},{6,14},{7,15},{8,16},{9,17... | collective-permute-start | bytes 442376 | tf_op jit(solution)/shard_map/ppermute | solution.py:310
  4.2 4.0 %collective-permute-start.1 = (bf16[2,288,128]{2,1,0:T(8,128)(2,1)}, bf16[2,288,128]{2,1,0:T(8,128)(2,1)S(1)}, u32[]{:S(2)}, u32[]{:S(2)}) collective-permute-start(bf16[2,288,128]{2,1,0:T(8,128)(2,1)} %get-tuple-element.36), channel_id=1, source_target_pairs={{0,56},{1,57},{2,58},{3,59},{4,60},{5,61},{6,62},{7,63},{8,0},{9,1... | collective-permute-start | bytes 442376 | tf_op jit(solution)/shard_map/ppermute | solution.py:310
  8.2 4.1 %collective-permute-start.3 = (bf16[2,288,128]{2,1,0:T(8,128)(2,1)}, bf16[2,288,128]{2,1,0:T(8,128)(2,1)S(1)}, u32[]{:S(2)}, u32[]{:S(2)}) collective-permute-start(bf16[2,288,128]{2,1,0:T(8,128)(2,1)} %get-tuple-element.38), channel_id=1, source_target_pairs={{0,48},{1,49},{2,50},{3,51},{4,52},{5,53},{6,54},{7,55},{8,56},{9,... | collective-permute-start | bytes 442376 | tf_op jit(solution)/shard_map/ppermute | solution.py:310
  12.4 2.1 %shard_map.64 = (bf16[2,288,128]{2,1,0:T(8,128)(2,1)}, bf16[2,288,128]{2,1,0:T(8,128)(2,1)}, bf16[2,288,128]{2,1,0:T(8,128)(2,1)}, bf16[2,288,128]{2,1,0:T(8,128)(2,1)}) custom-call(bf16[128,4096]{1,0:T(8,128)(2,1)} %bitcast.33, bf16[128,2048]{1,0:T(8,128)(2,1)} %bitcast.35), custom_call_target="tpu_custom_call" | custom-call | tf_op jit(solution)/shard_map/pallas_call | solution.py:67
  15.1 4.4 %collective-permute-start.5 = (bf16[2,288,128]{2,1,0:T(8,128)(2,1)}, bf16[2,288,128]{2,1,0:T(8,128)(2,1)S(1)}, u32[]{:S(2)}, u32[]{:S(2)}) collective-permute-start(bf16[2,288,128]{2,1,0:T(8,128)(2,1)} %get-tuple-element.40), channel_id=1, source_target_pairs={{0,40},{1,41},{2,42},{3,43},{4,44},{5,45},{6,46},{7,47},{8,48},{9,... | collective-permute-start | bytes 442376 | tf_op jit(solution)/shard_map/ppermute | solution.py:310
  19.6 4.5 %collective-permute-start.6 = (bf16[2,288,128]{2,1,0:T(8,128)(2,1)}, bf16[2,288,128]{2,1,0:T(8,128)(2,1)S(1)}, u32[]{:S(2)}, u32[]{:S(2)}) collective-permute-start(bf16[2,288,128]{2,1,0:T(8,128)(2,1)} %get-tuple-element.41), channel_id=1, source_target_pairs={{0,32},{1,33},{2,34},{3,35},{4,36},{5,37},{6,38},{7,39},{8,40},{9,... | collective-permute-start | bytes 442376 | tf_op jit(solution)/shard_map/ppermute | solution.py:310
  24.1 8.8 %collective-permute-done.4.refs_5_ = bf16[2,288,128]{2,1,0:T(8,128)(2,1)S(1)} collective-permute-done((bf16[2,288,128]{2,1,0:T(8,128)(2,1)}, bf16[2,288,128]{2,1,0:T(8,128)(2,1)S(1)}, u32[]{:S(2)}, u32[]{:S(2)}) %collective-permute-start.4) | collective-permute-done | bytes 147488 | tf_op jit(solution)/shard_map/ppermute | solution.py:310
  33.8 1.7 %shard_map.66 = (bf16[8,256,128]{2,1,0:T(8,128)(2,1)S(1)}, bf16[4,288,128]{2,1,0:T(8,128)(2,1)S(1)}, bf16[4,288,128]{2,1,0:T(8,128)(2,1)}) custom-call(bf16[2,288,128]{2,1,0:T(8,128)(2,1)S(1)} %copy-done.1, bf16[2,288,128]{2,1,0:T(8,128)(2,1)S(1)} %collective-permute-done.refs_1_, bf16[2,288,128]{2,1,0:T(8,128)(2,1)S(1)} %collective-permute-done.1.refs_2_, ...), custom_call_target="tpu_custom_call" | custom-call | tf_op jit(solution)/shard_map/pallas_call | solution.py:96
  35.5 1.7 %collective-permute-start.10 = (bf16[8,256,128]{2,1,0:T(8,128)(2,1)S(1)}, bf16[8,256,128]{2,1,0:T(8,128)(2,1)}, u32[]{:S(2)}, u32[]{:S(2)}) collective-permute-start(bf16[8,256,128]{2,1,0:T(8,128)(2,1)S(1)} %get-tuple-element.44.refs_0_), channel_id=1, source_target_pairs={{0,2},{1,3},{2,0},{3,1},{4,6},{5,7},{6,4},{7,5},{8,10},{9,11},{10,... | collective-permute-start | bytes 1572872 | tf_op jit(solution)/shard_map/ppermute | solution.py:310
  37.2 2.2 %collective-permute-start.7 = (bf16[4,288,128]{2,1,0:T(8,128)(2,1)S(1)}, bf16[4,288,128]{2,1,0:T(8,128)(2,1)S(1)}, u32[]{:S(2)}, u32[]{:S(2)}) collective-permute-start(bf16[4,288,128]{2,1,0:T(8,128)(2,1)S(1)} %get-tuple-element.42), channel_id=1, source_target_pairs={{0,6},{1,7},{2,4},{3,5},{4,2},{5,3},{6,0},{7,1},{8,14},{9,15},{10,... | collective-permute-start | bytes 884744 | tf_op jit(solution)/shard_map/ppermute | solution.py:310
  40.7 7.6 %collective-permute-done.7.refs_8_ = bf16[4,288,128]{2,1,0:T(8,128)(2,1)S(1)} collective-permute-done((bf16[4,288,128]{2,1,0:T(8,128)(2,1)S(1)}, bf16[4,288,128]{2,1,0:T(8,128)(2,1)S(1)}, u32[]{:S(2)}, u32[]{:S(2)}) %collective-permute-start.7) | collective-permute-done | bytes 294944 | tf_op jit(solution)/shard_map/ppermute | solution.py:310
  48.6 4.1 %collective-permute-done.8.refs_9_ = bf16[4,288,128]{2,1,0:T(8,128)(2,1)S(1)} collective-permute-done((bf16[4,288,128]{2,1,0:T(8,128)(2,1)}, bf16[4,288,128]{2,1,0:T(8,128)(2,1)S(1)}, u32[]{:S(2)}, u32[]{:S(2)}) %collective-permute-start.8) | collective-permute-done | bytes 294944 | tf_op jit(solution)/shard_map/ppermute | solution.py:310
  56.3 1.3 collective-permute-start.9
  57.8 5.1 %collective-permute-done.12.refs_5_ = bf16[4,256,128]{2,1,0:T(8,128)(2,1)} collective-permute-done((bf16[4,256,128]{2,1,0:T(8,128)(2,1)S(1)}, bf16[4,256,128]{2,1,0:T(8,128)(2,1)}, u32[]{:S(2)}, u32[]{:S(2)}) %collective-permute-start.12) | collective-permute-done | bytes 262176 | tf_op jit(solution)/shard_map/ppermute | solution.py:310
  64.7 1.7 %shard_map.68 = bf16[64,256,128]{2,1,0:T(8,128)(2,1)S(1)} custom-call(bf16[8,256,128]{2,1,0:T(8,128)(2,1)S(1)} %get-tuple-element.44.refs_0_, bf16[8,256,128]{2,1,0:T(8,128)(2,1)} %collective-permute-done.10.refs_1_, bf16[4,256,128]{2,1,0:T(8,128)(2,1)S(1)} %slice.8.refs_2_, bf16[4,256,128]{2,1,0:T(8,128)(2,1)S(1)} %slice.9.refs_3_, ...), custom_call_target="tpu_custom_call" | custom-call | tf_op jit(solution)/shard_map/pallas_call | solution.py:159
  67.1 2.5 %collective-permute-start.20 = (bf16[512,128]{1,0:T(8,128)(2,1)S(1)}, bf16[512,128]{1,0:T(8,128)(2,1)S(1)}, u32[]{:S(2)}, u32[]{:S(2)}) collective-permute-start(bf16[512,128]{1,0:T(8,128)(2,1)S(1)} %get-tuple-element.47), channel_id=1, source_target_pairs={{0,64},{64,128},{128,192},{192,0},{1,65},{65,129},{129,193},{193,1... | collective-permute-start | bytes 393224 | tf_op jit(solution)/shard_map/ppermute | solution.py:400
  70.3 2.0 %collective-permute-start.19 = (bf16[512,128]{1,0:T(8,128)(2,1)S(1)}, bf16[512,128]{1,0:T(8,128)(2,1)S(1)}, u32[]{:S(2)}, u32[]{:S(2)}) collective-permute-start(bf16[512,128]{1,0:T(8,128)(2,1)S(1)} %get-tuple-element.46), channel_id=1, source_target_pairs={{0,64},{64,128},{128,192},{192,0},{1,65},{65,129},{129,193},{193,1... | collective-permute-start | bytes 393224 | tf_op jit(solution)/shard_map/ppermute | solution.py:400
  73.4 1.3 collective-permute-start.22
  76.3 1.3 collective-permute-start.21
  77.6 2.9 %collective-permute-done.22.x_ref = bf16[512,128]{1,0:T(8,128)(2,1)S(1)} collective-permute-done((bf16[512,128]{1,0:T(8,128)(2,1)S(1)}, bf16[512,128]{1,0:T(8,128)(2,1)S(1)}, u32[]{:S(2)}, u32[]{:S(2)}) %collective-permute-start.22) | collective-permute-done | bytes 131104 | tf_op jit(solution)/shard_map/ppermute | solution.py:400
  81.4 1.3 collective-permute-start.24
  83.9 1.3 collective-permute-start.23
  85.2 5.1 %collective-permute-done.24.x_ref = bf16[512,128]{1,0:T(8,128)(2,1)S(1)} collective-permute-done((bf16[512,128]{1,0:T(8,128)(2,1)S(1)}, bf16[512,128]{1,0:T(8,128)(2,1)S(1)}, u32[]{:S(2)}, u32[]{:S(2)}) %collective-permute-start.24) | collective-permute-done | bytes 131104 | tf_op jit(solution)/shard_map/ppermute | solution.py:400
  90.3 2.6 %shard_map.75 = (bf16[512,128]{1,0:T(8,128)(2,1)S(1)}, bf16[16,128,128]{2,1,0:T(8,128)(2,1)S(1)}) custom-call(s32[2048]{0:T(1024)S(1)} %reshape.39.places, s32[4]{0:T(128)S(1)} %pad_add_fusion.1.info, bf16[512,128]{1,0:T(8,128)(2,1)S(1)} %collective-permute-done.24.x_ref, f32[1,128]{1,0:T(1,128)S(1)} %get-tuple-element.66.refs_0_, ...), custom_call_target="tpu_custom_call", output_to_operand_aliasing={{1}: (6, {})} | custom-call | flops 134217728 | bytes 262144 | tf_op jit(solution)/shard_map/pallas_call | solution.py:261
  93.0 1.3 collective-permute-start.26
  94.9 2.6 %shard_map.76 = (bf16[512,128]{1,0:T(8,128)(2,1)S(1)}, bf16[16,128,128]{2,1,0:T(8,128)(2,1)S(1)}) custom-call(s32[2048]{0:T(1024)S(1)} %reshape.39.places, s32[4]{0:T(128)S(1)} %pad_add_fusion.1.info, bf16[512,128]{1,0:T(8,128)(2,1)S(1)} %collective-permute-done.23.x_ref, f32[1,128]{1,0:T(1,128)S(1)} %get-tuple-element.66.refs_0_, ...), custom_call_target="tpu_custom_call", output_to_operand_aliasing={{1}: (6, {})} | custom-call | flops 134217728 | bytes 262144 | tf_op jit(solution)/shard_map/pallas_call | solution.py:261
  97.5 1.3 collective-permute-start.25
  99.8 3.3 %shard_map.77 = (bf16[512,128]{1,0:T(8,128)(2,1)}, bf16[16,128,128]{2,1,0:T(8,128)(2,1)S(1)}) custom-call(s32[2048]{0:T(1024)S(1)} %reshape.39.places, s32[4]{0:T(128)S(1)} %pad_add_fusion.1.info, bf16[512,128]{1,0:T(8,128)(2,1)S(1)} %collective-permute-done.26.x_ref, f32[1,128]{1,0:T(1,128)S(1)} %get-tuple-element.66.refs_0_, ...), custom_call_target="tpu_custom_call", output_to_operand_aliasing={{1}: (6, {})} | custom-call | flops 134217728 | bytes 262144 | tf_op jit(solution)/shard_map/pallas_call | solution.py:261
  103.1 1.3 collective-permute-done.25.x_ref
  104.4 3.3 %shard_map.78 = (bf16[512,128]{1,0:T(8,128)(2,1)}, bf16[16,128,128]{2,1,0:T(8,128)(2,1)S(1)}) custom-call(s32[2048]{0:T(1024)S(1)} %reshape.39.places, s32[4]{0:T(128)S(1)} %pad_add_fusion.1.info, bf16[512,128]{1,0:T(8,128)(2,1)S(1)} %collective-permute-done.25.x_ref, f32[1,128]{1,0:T(1,128)S(1)} %get-tuple-element.66.refs_0_, ...), custom_call_target="tpu_custom_call", output_to_operand_aliasing={{1}: (6, {})} | custom-call | flops 134217728 | bytes 262144 | tf_op jit(solution)/shard_map/pallas_call | solution.py:261
  107.7 25.6 %all_to_all.5.done = bf16[16,128,128]{2,1,0:T(8,128)(2,1)S(1)} all-to-all(bf16[16,128,128]{2,1,0:T(8,128)(2,1)S(1)} %get-tuple-element.62), channel_id=1, replica_groups={{0,6,8,14,16,22,24,30,32,38,40,46,48,54,56,62},{1,7,9,15,17,23,25,31,33..., dimensions={0} | all-to-all | bytes 1048576 | tf_op jit(solution)/shard_map/all_to_all | solution.py:406
  (61 shorter events, 17.3 us)
Async XLA Ops:
  0.0 40.4 %copy-start = (s32[1,16,512,16]{2,3,1,0:T(8,128)S(1)}, s32[1,16,512,16]{2,3,1,0:T(8,128)}, u32[]{:S(2)}) copy-start(s32[1,16,512,16]{2,3,1,0:T(8,128)} %param.8) | copy-start | bytes 1572868
  0.0 52.8 %copy-start.3 = (s32[1,16]{1,0:T(1,128)S(1)}, s32[1,16]{1,0:T(1,128)}, u32[]{:S(2)}) copy-start(s32[1,16]{1,0:T(1,128)} %param.9) | copy-start | bytes 196
  2.2 12.9 %collective-permute-start = (bf16[2,288,128]{2,1,0:T(8,128)(2,1)}, bf16[2,288,128]{2,1,0:T(8,128)(2,1)S(1)}, u32[]{:S(2)}, u32[]{:S(2)}) collective-permute-start(bf16[2,288,128]{2,1,0:T(8,128)(2,1)} %get-tuple-element.35), channel_id=1, source_target_pairs={{0,8},{1,9},{2,10},{3,11},{4,12},{5,13},{6,14},{7,15},{8,16},{9,17... | collective-permute-start | bytes 442376 | tf_op jit(solution)/shard_map/ppermute | solution.py:310
  4.2 15.4 %collective-permute-start.1 = (bf16[2,288,128]{2,1,0:T(8,128)(2,1)}, bf16[2,288,128]{2,1,0:T(8,128)(2,1)S(1)}, u32[]{:S(2)}, u32[]{:S(2)}) collective-permute-start(bf16[2,288,128]{2,1,0:T(8,128)(2,1)} %get-tuple-element.36), channel_id=1, source_target_pairs={{0,56},{1,57},{2,58},{3,59},{4,60},{5,61},{6,62},{7,63},{8,0},{9,1... | collective-permute-start | bytes 442376 | tf_op jit(solution)/shard_map/ppermute | solution.py:310
  8.2 15.8 %collective-permute-start.2 = (bf16[2,288,128]{2,1,0:T(8,128)(2,1)}, bf16[2,288,128]{2,1,0:T(8,128)(2,1)S(1)}, u32[]{:S(2)}, u32[]{:S(2)}) collective-permute-start(bf16[2,288,128]{2,1,0:T(8,128)(2,1)} %get-tuple-element.37), channel_id=1, source_target_pairs={{0,16},{1,17},{2,18},{3,19},{4,20},{5,21},{6,22},{7,23},{8,24},{9,... | collective-permute-start | bytes 442376 | tf_op jit(solution)/shard_map/ppermute | solution.py:310
  8.2 15.8 %collective-permute-start.3 = (bf16[2,288,128]{2,1,0:T(8,128)(2,1)}, bf16[2,288,128]{2,1,0:T(8,128)(2,1)S(1)}, u32[]{:S(2)}, u32[]{:S(2)}) collective-permute-start(bf16[2,288,128]{2,1,0:T(8,128)(2,1)} %get-tuple-element.38), channel_id=1, source_target_pairs={{0,48},{1,49},{2,50},{3,51},{4,52},{5,53},{6,54},{7,55},{8,56},{9,... | collective-permute-start | bytes 442376 | tf_op jit(solution)/shard_map/ppermute | solution.py:310
  14.5 18.4 %collective-permute-start.4 = (bf16[2,288,128]{2,1,0:T(8,128)(2,1)}, bf16[2,288,128]{2,1,0:T(8,128)(2,1)S(1)}, u32[]{:S(2)}, u32[]{:S(2)}) collective-permute-start(bf16[2,288,128]{2,1,0:T(8,128)(2,1)} %get-tuple-element.39), channel_id=1, source_target_pairs={{0,24},{1,25},{2,26},{3,27},{4,28},{5,29},{6,30},{7,31},{8,32},{9,... | collective-permute-start | bytes 442376 | tf_op jit(solution)/shard_map/ppermute | solution.py:310
  15.1 17.7 %collective-permute-start.5 = (bf16[2,288,128]{2,1,0:T(8,128)(2,1)}, bf16[2,288,128]{2,1,0:T(8,128)(2,1)S(1)}, u32[]{:S(2)}, u32[]{:S(2)}) collective-permute-start(bf16[2,288,128]{2,1,0:T(8,128)(2,1)} %get-tuple-element.40), channel_id=1, source_target_pairs={{0,40},{1,41},{2,42},{3,43},{4,44},{5,45},{6,46},{7,47},{8,48},{9,... | collective-permute-start | bytes 442376 | tf_op jit(solution)/shard_map/ppermute | solution.py:310
  19.6 13.3 %collective-permute-start.6 = (bf16[2,288,128]{2,1,0:T(8,128)(2,1)}, bf16[2,288,128]{2,1,0:T(8,128)(2,1)S(1)}, u32[]{:S(2)}, u32[]{:S(2)}) collective-permute-start(bf16[2,288,128]{2,1,0:T(8,128)(2,1)} %get-tuple-element.41), channel_id=1, source_target_pairs={{0,32},{1,33},{2,34},{3,35},{4,36},{5,37},{6,38},{7,39},{8,40},{9,... | collective-permute-start | bytes 442376 | tf_op jit(solution)/shard_map/ppermute | solution.py:310
  32.9 0.9 copy-start.1
  35.5 17.9 %collective-permute-start.10 = (bf16[8,256,128]{2,1,0:T(8,128)(2,1)S(1)}, bf16[8,256,128]{2,1,0:T(8,128)(2,1)}, u32[]{:S(2)}, u32[]{:S(2)}) collective-permute-start(bf16[8,256,128]{2,1,0:T(8,128)(2,1)S(1)} %get-tuple-element.44.refs_0_), channel_id=1, source_target_pairs={{0,2},{1,3},{2,0},{3,1},{4,6},{5,7},{6,4},{7,5},{8,10},{9,11},{10,... | collective-permute-start | bytes 1572872 | tf_op jit(solution)/shard_map/ppermute | solution.py:310
  37.2 11.2 %collective-permute-start.7 = (bf16[4,288,128]{2,1,0:T(8,128)(2,1)S(1)}, bf16[4,288,128]{2,1,0:T(8,128)(2,1)S(1)}, u32[]{:S(2)}, u32[]{:S(2)}) collective-permute-start(bf16[4,288,128]{2,1,0:T(8,128)(2,1)S(1)} %get-tuple-element.42), channel_id=1, source_target_pairs={{0,6},{1,7},{2,4},{3,5},{4,2},{5,3},{6,0},{7,1},{8,14},{9,15},{10,... | collective-permute-start | bytes 884744 | tf_op jit(solution)/shard_map/ppermute | solution.py:310
  39.4 13.3 %collective-permute-start.8 = (bf16[4,288,128]{2,1,0:T(8,128)(2,1)}, bf16[4,288,128]{2,1,0:T(8,128)(2,1)S(1)}, u32[]{:S(2)}, u32[]{:S(2)}) collective-permute-start(bf16[4,288,128]{2,1,0:T(8,128)(2,1)} %get-tuple-element.43), channel_id=1, source_target_pairs={{0,6},{1,7},{2,4},{3,5},{4,2},{5,3},{6,0},{7,1},{8,14},{9,15},{10,... | collective-permute-start | bytes 884744 | tf_op jit(solution)/shard_map/ppermute | solution.py:310
  40.6 15.2 %collective-permute-start.13 = (bf16[8,256,128]{2,1,0:T(8,128)(2,1)S(1)}, bf16[8,256,128]{2,1,0:T(8,128)(2,1)}, u32[]{:S(2)}, u32[]{:S(2)}) collective-permute-start(bf16[8,256,128]{2,1,0:T(8,128)(2,1)S(1)} %get-tuple-element.44.refs_0_), channel_id=1, source_target_pairs={{0,1},{1,0},{2,3},{3,2},{4,5},{5,4},{6,7},{7,6},{8,9},{9,8},{10,11... | collective-permute-start | bytes 1572872 | tf_op jit(solution)/shard_map/ppermute | solution.py:310
  48.4 8.0 %collective-permute-start.15 = (bf16[4,256,128]{2,1,0:T(8,128)(2,1)S(1)}, bf16[4,256,128]{2,1,0:T(8,128)(2,1)}, u32[]{:S(2)}, u32[]{:S(2)}) collective-permute-start(bf16[4,256,128]{2,1,0:T(8,128)(2,1)S(1)} %slice.8.refs_2_), channel_id=1, source_target_pairs={{0,1},{1,0},{2,3},{3,2},{4,5},{5,4},{6,7},{7,6},{8,9},{9,8},{10,11... | collective-permute-start | bytes 786440 | tf_op jit(solution)/shard_map/ppermute | solution.py:310
  48.5 9.3 %collective-permute-start.11 = (bf16[4,256,128]{2,1,0:T(8,128)(2,1)S(1)}, bf16[4,256,128]{2,1,0:T(8,128)(2,1)}, u32[]{:S(2)}, u32[]{:S(2)}) collective-permute-start(bf16[4,256,128]{2,1,0:T(8,128)(2,1)S(1)} %slice.8.refs_2_), channel_id=1, source_target_pairs={{0,2},{1,3},{2,0},{3,1},{4,6},{5,7},{6,4},{7,5},{8,10},{9,11},{10,... | collective-permute-start | bytes 786440 | tf_op jit(solution)/shard_map/ppermute | solution.py:310
  52.7 10.2 %collective-permute-start.12 = (bf16[4,256,128]{2,1,0:T(8,128)(2,1)S(1)}, bf16[4,256,128]{2,1,0:T(8,128)(2,1)}, u32[]{:S(2)}, u32[]{:S(2)}) collective-permute-start(bf16[4,256,128]{2,1,0:T(8,128)(2,1)S(1)} %slice.9.refs_3_), channel_id=1, source_target_pairs={{0,2},{1,3},{2,0},{3,1},{4,6},{5,7},{6,4},{7,5},{8,10},{9,11},{10,... | collective-permute-start | bytes 786440 | tf_op jit(solution)/shard_map/ppermute | solution.py:310
  53.4 11.3 %collective-permute-start.14 = (bf16[8,256,128]{2,1,0:T(8,128)(2,1)}, bf16[8,256,128]{2,1,0:T(8,128)(2,1)}, u32[]{:S(2)}, u32[]{:S(2)}) collective-permute-start(bf16[8,256,128]{2,1,0:T(8,128)(2,1)} %collective-permute-done.10.refs_1_), channel_id=1, source_target_pairs={{0,1},{1,0},{2,3},{3,2},{4,5},{5,4},{6,7},{7,6},{8,9},{9,8},{10,11... | collective-permute-start | bytes 1572872 | tf_op jit(solution)/shard_map/ppermute | solution.py:310
  54.2 0.9 copy-start.2
  55.7 8.4 %collective-permute-start.16 = (bf16[4,256,128]{2,1,0:T(8,128)(2,1)S(1)}, bf16[4,256,128]{2,1,0:T(8,128)(2,1)S(1)}, u32[]{:S(2)}, u32[]{:S(2)}) collective-permute-start(bf16[4,256,128]{2,1,0:T(8,128)(2,1)S(1)} %slice.9.refs_3_), channel_id=1, source_target_pairs={{0,1},{1,0},{2,3},{3,2},{4,5},{5,4},{6,7},{7,6},{8,9},{9,8},{10,11... | collective-permute-start | bytes 786440 | tf_op jit(solution)/shard_map/ppermute | solution.py:310
  56.3 13.3 %collective-permute-start.9 = (bf16[512,128]{1,0:T(8,128)(2,1)S(1)}, bf16[512,128]{1,0:T(8,128)(2,1)S(1)}, u32[]{:S(2)}, u32[]{:S(2)}) collective-permute-start(bf16[512,128]{1,0:T(8,128)(2,1)S(1)} %shard_map.67.x_ref), channel_id=1, source_target_pairs={{64,0},{128,192},{65,1},{129,193},{66,2},{130,194},{67,3},{131,195... | collective-permute-start | bytes 393224 | tf_op jit(solution)/shard_map/ppermute | solution.py:357
  57.8 6.3 %collective-permute-start.17 = (bf16[4,256,128]{2,1,0:T(8,128)(2,1)}, bf16[4,256,128]{2,1,0:T(8,128)(2,1)S(1)}, u32[]{:S(2)}, u32[]{:S(2)}) collective-permute-start(bf16[4,256,128]{2,1,0:T(8,128)(2,1)} %collective-permute-done.11.refs_4_), channel_id=1, source_target_pairs={{0,1},{1,0},{2,3},{3,2},{4,5},{5,4},{6,7},{7,6},{8,9},{9,8},{10,11... | collective-permute-start | bytes 786440 | tf_op jit(solution)/shard_map/ppermute | solution.py:310
  62.9 1.7 %collective-permute-start.18 = (bf16[4,256,128]{2,1,0:T(8,128)(2,1)}, bf16[4,256,128]{2,1,0:T(8,128)(2,1)S(1)}, u32[]{:S(2)}, u32[]{:S(2)}) collective-permute-start(bf16[4,256,128]{2,1,0:T(8,128)(2,1)} %collective-permute-done.12.refs_5_), channel_id=1, source_target_pairs={{0,1},{1,0},{2,3},{3,2},{4,5},{5,4},{6,7},{7,6},{8,9},{9,8},{10,11... | collective-permute-start | bytes 786440 | tf_op jit(solution)/shard_map/ppermute | solution.py:310
  67.1 5.6 %collective-permute-start.20 = (bf16[512,128]{1,0:T(8,128)(2,1)S(1)}, bf16[512,128]{1,0:T(8,128)(2,1)S(1)}, u32[]{:S(2)}, u32[]{:S(2)}) collective-permute-start(bf16[512,128]{1,0:T(8,128)(2,1)S(1)} %get-tuple-element.47), channel_id=1, source_target_pairs={{0,64},{64,128},{128,192},{192,0},{1,65},{65,129},{129,193},{193,1... | collective-permute-start | bytes 393224 | tf_op jit(solution)/shard_map/ppermute | solution.py:400
  70.3 5.3 %collective-permute-start.19 = (bf16[512,128]{1,0:T(8,128)(2,1)S(1)}, bf16[512,128]{1,0:T(8,128)(2,1)S(1)}, u32[]{:S(2)}, u32[]{:S(2)}) collective-permute-start(bf16[512,128]{1,0:T(8,128)(2,1)S(1)} %get-tuple-element.46), channel_id=1, source_target_pairs={{0,64},{64,128},{128,192},{192,0},{1,65},{65,129},{129,193},{193,1... | collective-permute-start | bytes 393224 | tf_op jit(solution)/shard_map/ppermute | solution.py:400
  73.4 7.1 %collective-permute-start.22 = (bf16[512,128]{1,0:T(8,128)(2,1)S(1)}, bf16[512,128]{1,0:T(8,128)(2,1)S(1)}, u32[]{:S(2)}, u32[]{:S(2)}) collective-permute-start(bf16[512,128]{1,0:T(8,128)(2,1)S(1)} %get-tuple-element.51), channel_id=1, source_target_pairs={{0,64},{64,128},{128,192},{1,65},{65,129},{129,193},{2,66},{66,130... | collective-permute-start | bytes 393224 | tf_op jit(solution)/shard_map/ppermute | solution.py:400
  76.3 6.9 %collective-permute-start.21 = (bf16[512,128]{1,0:T(8,128)(2,1)S(1)}, bf16[512,128]{1,0:T(8,128)(2,1)S(1)}, u32[]{:S(2)}, u32[]{:S(2)}) collective-permute-start(bf16[512,128]{1,0:T(8,128)(2,1)S(1)} %get-tuple-element.50), channel_id=1, source_target_pairs={{0,64},{64,128},{128,192},{1,65},{65,129},{129,193},{2,66},{66,130... | collective-permute-start | bytes 393224 | tf_op jit(solution)/shard_map/ppermute | solution.py:400
  81.4 8.9 %collective-permute-start.24 = (bf16[512,128]{1,0:T(8,128)(2,1)S(1)}, bf16[512,128]{1,0:T(8,128)(2,1)S(1)}, u32[]{:S(2)}, u32[]{:S(2)}) collective-permute-start(bf16[512,128]{1,0:T(8,128)(2,1)S(1)} %get-tuple-element.55), channel_id=1, source_target_pairs={{0,64},{64,128},{128,192},{1,65},{65,129},{129,193},{2,66},{66,130... | collective-permute-start | bytes 393224 | tf_op jit(solution)/shard_map/ppermute | solution.py:400
  83.9 11.0 %collective-permute-start.23 = (bf16[512,128]{1,0:T(8,128)(2,1)S(1)}, bf16[512,128]{1,0:T(8,128)(2,1)S(1)}, u32[]{:S(2)}, u32[]{:S(2)}) collective-permute-start(bf16[512,128]{1,0:T(8,128)(2,1)S(1)} %get-tuple-element.54), channel_id=1, source_target_pairs={{0,64},{64,128},{128,192},{1,65},{65,129},{129,193},{2,66},{66,130... | collective-permute-start | bytes 393224 | tf_op jit(solution)/shard_map/ppermute | solution.py:400
  93.0 6.9 %collective-permute-start.26 = (bf16[512,128]{1,0:T(8,128)(2,1)S(1)}, bf16[512,128]{1,0:T(8,128)(2,1)S(1)}, u32[]{:S(2)}, u32[]{:S(2)}) collective-permute-start(bf16[512,128]{1,0:T(8,128)(2,1)S(1)} %get-tuple-element.59), channel_id=1, source_target_pairs={{0,64},{64,128},{128,192},{1,65},{65,129},{129,193},{2,66},{66,130... | collective-permute-start | bytes 393224 | tf_op jit(solution)/shard_map/ppermute | solution.py:400
  97.5 6.9 %collective-permute-start.25 = (bf16[512,128]{1,0:T(8,128)(2,1)S(1)}, bf16[512,128]{1,0:T(8,128)(2,1)S(1)}, u32[]{:S(2)}, u32[]{:S(2)}) collective-permute-start(bf16[512,128]{1,0:T(8,128)(2,1)S(1)} %get-tuple-element.58), channel_id=1, source_target_pairs={{0,64},{64,128},{128,192},{1,65},{65,129},{129,193},{2,66},{66,130... | collective-permute-start | bytes 393224 | tf_op jit(solution)/shard_map/ppermute | solution.py:400

commit v7 on v6

--- a/solution.py
+++ b/solution.py
@@ -209,13 +209,13 @@
                         preferred_element_type=jnp.float32,
                     )
                 )
-            scores = jnp.concatenate(scores, axis=0) * (HEAD_DIM**-0.5)
+            scores = jnp.concatenate(scores, axis=0)
             lane = lax.broadcasted_iota(jnp.int32, scores.shape, 1)
             scores = jnp.where(lane < live_keys, scores, SCORE_FLOOR)
             highest = jnp.max(scores, axis=-1, keepdims=True)
-            exponent = jnp.exp(scores - highest)
+            exponent = jnp.exp((scores - highest) * (HEAD_DIM**-0.5))
             total = jnp.sum(exponent, axis=-1, keepdims=True)
-            weights = (exponent / total).astype(jnp.bfloat16)
+            weights = (exponent * (1.0 / total)).astype(jnp.bfloat16)
             summed = []
             for g in range(GROUP):
                 values = jnp.concatenate(

time: 135 us -> 135 us (level)
  no operation moved by 1% of the time
where the time goes in v7:
time: 135 us; the launch traced here: 134 us
  starting transfers between devices  39.2 us (29%)
  waiting for transfers between devices  39.2 us (29%)
  blocking collectives  25.5 us (19%)
  Pallas kernels  25.4 us (19%)
  local copies, waits for them, and re-layouts  3.54 us (3%)
    ppermute x18, waiting for transfers between devices, moved(): return lax.ppermute(value, 'seq', pairs)  26.4 us
    ppermute x18, starting transfers between devices, moved(): return lax.ppermute(value, 'seq', pairs)  25.6 us
    all_to_all x1, blocking collectives, local(): lax.all_to_all(done, 'seq', 0, 0, axis_index_groups=groups, tiled=True)  25.5 us
    pallas_call x10, Pallas kernels, attend(): pl.pallas_call(functools.partial(attend_kernel, step=step), out_shape=(ja...  16.2 us
    ppermute x8, waiting for transfers between devices, local(): sent.append(lax.ppermute(result, 'section', pairs))  12.7 us
    ppermute x8, starting transfers between devices, local(): sent.append(lax.ppermute(result, 'section', pairs))  12.3 us
    pallas_call x2, Pallas kernels, packed(): pl.pallas_call(functools.partial(pack_kernel, shifts=shifts), out_shape=(...  4.28 us
  transfers between devices with their start and end apart: 27, of which 14 were waited for; matrix products, arithmetic and copies ran while one was open for 2% of the time, Pallas kernels for 13%

profile of v7, /device:TPU:6, one launch (start us, length us, event | category | flops | bytes accessed | tf_op | source)
XLA Modules:
  0.0 134.4 jit_solution(5553982714574049759)
XLA Ops:
  0.0 2.2 %shard_map.65 = (bf16[2,288,128]{2,1,0:T(8,128)(2,1)}, bf16[2,288,128]{2,1,0:T(8,128)(2,1)}, bf16[2,288,128]{2,1,0:T(8,128)(2,1)}, bf16[2,288,128]{2,1,0:T(8,128)(2,1)}) custom-call(bf16[128,4096]{1,0:T(8,128)(2,1)} %bitcast.32, bf16[128,2048]{1,0:T(8,128)(2,1)} %bitcast.34), custom_call_target="tpu_custom_call" | custom-call | tf_op jit(solution)/shard_map/pallas_call | solution.py:67
  2.2 2.0 %collective-permute-start = (bf16[2,288,128]{2,1,0:T(8,128)(2,1)}, bf16[2,288,128]{2,1,0:T(8,128)(2,1)S(1)}, u32[]{:S(2)}, u32[]{:S(2)}) collective-permute-start(bf16[2,288,128]{2,1,0:T(8,128)(2,1)} %get-tuple-element.35), channel_id=1, source_target_pairs={{0,8},{1,9},{2,10},{3,11},{4,12},{5,13},{6,14},{7,15},{8,16},{9,17... | collective-permute-start | bytes 442376 | tf_op jit(solution)/shard_map/ppermute | solution.py:310
  4.2 4.0 %collective-permute-start.1 = (bf16[2,288,128]{2,1,0:T(8,128)(2,1)}, bf16[2,288,128]{2,1,0:T(8,128)(2,1)S(1)}, u32[]{:S(2)}, u32[]{:S(2)}) collective-permute-start(bf16[2,288,128]{2,1,0:T(8,128)(2,1)} %get-tuple-element.36), channel_id=1, source_target_pairs={{0,56},{1,57},{2,58},{3,59},{4,60},{5,61},{6,62},{7,63},{8,0},{9,1... | collective-permute-start | bytes 442376 | tf_op jit(solution)/shard_map/ppermute | solution.py:310
  8.2 4.1 %collective-permute-start.3 = (bf16[2,288,128]{2,1,0:T(8,128)(2,1)}, bf16[2,288,128]{2,1,0:T(8,128)(2,1)S(1)}, u32[]{:S(2)}, u32[]{:S(2)}) collective-permute-start(bf16[2,288,128]{2,1,0:T(8,128)(2,1)} %get-tuple-element.38), channel_id=1, source_target_pairs={{0,48},{1,49},{2,50},{3,51},{4,52},{5,53},{6,54},{7,55},{8,56},{9,... | collective-permute-start | bytes 442376 | tf_op jit(solution)/shard_map/ppermute | solution.py:310
  12.4 2.1 %shard_map.64 = (bf16[2,288,128]{2,1,0:T(8,128)(2,1)}, bf16[2,288,128]{2,1,0:T(8,128)(2,1)}, bf16[2,288,128]{2,1,0:T(8,128)(2,1)}, bf16[2,288,128]{2,1,0:T(8,128)(2,1)}) custom-call(bf16[128,4096]{1,0:T(8,128)(2,1)} %bitcast.33, bf16[128,2048]{1,0:T(8,128)(2,1)} %bitcast.35), custom_call_target="tpu_custom_call" | custom-call | tf_op jit(solution)/shard_map/pallas_call | solution.py:67
  15.1 4.4 %collective-permute-start.5 = (bf16[2,288,128]{2,1,0:T(8,128)(2,1)}, bf16[2,288,128]{2,1,0:T(8,128)(2,1)S(1)}, u32[]{:S(2)}, u32[]{:S(2)}) collective-permute-start(bf16[2,288,128]{2,1,0:T(8,128)(2,1)} %get-tuple-element.40), channel_id=1, source_target_pairs={{0,40},{1,41},{2,42},{3,43},{4,44},{5,45},{6,46},{7,47},{8,48},{9,... | collective-permute-start | bytes 442376 | tf_op jit(solution)/shard_map/ppermute | solution.py:310
  19.6 4.5 %collective-permute-start.6 = (bf16[2,288,128]{2,1,0:T(8,128)(2,1)}, bf16[2,288,128]{2,1,0:T(8,128)(2,1)S(1)}, u32[]{:S(2)}, u32[]{:S(2)}) collective-permute-start(bf16[2,288,128]{2,1,0:T(8,128)(2,1)} %get-tuple-element.41), channel_id=1, source_target_pairs={{0,32},{1,33},{2,34},{3,35},{4,36},{5,37},{6,38},{7,39},{8,40},{9,... | collective-permute-start | bytes 442376 | tf_op jit(solution)/shard_map/ppermute | solution.py:310
  24.1 8.8 %collective-permute-done.4.refs_5_ = bf16[2,288,128]{2,1,0:T(8,128)(2,1)S(1)} collective-permute-done((bf16[2,288,128]{2,1,0:T(8,128)(2,1)}, bf16[2,288,128]{2,1,0:T(8,128)(2,1)S(1)}, u32[]{:S(2)}, u32[]{:S(2)}) %collective-permute-start.4) | collective-permute-done | bytes 147488 | tf_op jit(solution)/shard_map/ppermute | solution.py:310
  33.8 1.7 %shard_map.66 = (bf16[8,256,128]{2,1,0:T(8,128)(2,1)S(1)}, bf16[4,288,128]{2,1,0:T(8,128)(2,1)S(1)}, bf16[4,288,128]{2,1,0:T(8,128)(2,1)}) custom-call(bf16[2,288,128]{2,1,0:T(8,128)(2,1)S(1)} %copy-done.1, bf16[2,288,128]{2,1,0:T(8,128)(2,1)S(1)} %collective-permute-done.refs_1_, bf16[2,288,128]{2,1,0:T(8,128)(2,1)S(1)} %collective-permute-done.1.refs_2_, ...), custom_call_target="tpu_custom_call" | custom-call | tf_op jit(solution)/shard_map/pallas_call | solution.py:96
  35.5 1.7 %collective-permute-start.10 = (bf16[8,256,128]{2,1,0:T(8,128)(2,1)S(1)}, bf16[8,256,128]{2,1,0:T(8,128)(2,1)}, u32[]{:S(2)}, u32[]{:S(2)}) collective-permute-start(bf16[8,256,128]{2,1,0:T(8,128)(2,1)S(1)} %get-tuple-element.44.refs_0_), channel_id=1, source_target_pairs={{0,2},{1,3},{2,0},{3,1},{4,6},{5,7},{6,4},{7,5},{8,10},{9,11},{10,... | collective-permute-start | bytes 1572872 | tf_op jit(solution)/shard_map/ppermute | solution.py:310
  37.2 2.2 %collective-permute-start.7 = (bf16[4,288,128]{2,1,0:T(8,128)(2,1)S(1)}, bf16[4,288,128]{2,1,0:T(8,128)(2,1)S(1)}, u32[]{:S(2)}, u32[]{:S(2)}) collective-permute-start(bf16[4,288,128]{2,1,0:T(8,128)(2,1)S(1)} %get-tuple-element.42), channel_id=1, source_target_pairs={{0,6},{1,7},{2,4},{3,5},{4,2},{5,3},{6,0},{7,1},{8,14},{9,15},{10,... | collective-permute-start | bytes 884744 | tf_op jit(solution)/shard_map/ppermute | solution.py:310
  40.7 7.6 %collective-permute-done.7.refs_8_ = bf16[4,288,128]{2,1,0:T(8,128)(2,1)S(1)} collective-permute-done((bf16[4,288,128]{2,1,0:T(8,128)(2,1)S(1)}, bf16[4,288,128]{2,1,0:T(8,128)(2,1)S(1)}, u32[]{:S(2)}, u32[]{:S(2)}) %collective-permute-start.7) | collective-permute-done | bytes 294944 | tf_op jit(solution)/shard_map/ppermute | solution.py:310
  48.6 4.1 %collective-permute-done.8.refs_9_ = bf16[4,288,128]{2,1,0:T(8,128)(2,1)S(1)} collective-permute-done((bf16[4,288,128]{2,1,0:T(8,128)(2,1)}, bf16[4,288,128]{2,1,0:T(8,128)(2,1)S(1)}, u32[]{:S(2)}, u32[]{:S(2)}) %collective-permute-start.8) | collective-permute-done | bytes 294944 | tf_op jit(solution)/shard_map/ppermute | solution.py:310
  56.3 1.3 collective-permute-start.9
  57.8 5.1 %collective-permute-done.12.refs_5_ = bf16[4,256,128]{2,1,0:T(8,128)(2,1)} collective-permute-done((bf16[4,256,128]{2,1,0:T(8,128)(2,1)S(1)}, bf16[4,256,128]{2,1,0:T(8,128)(2,1)}, u32[]{:S(2)}, u32[]{:S(2)}) %collective-permute-start.12) | collective-permute-done | bytes 262176 | tf_op jit(solution)/shard_map/ppermute | solution.py:310
  64.7 1.7 %shard_map.68 = bf16[64,256,128]{2,1,0:T(8,128)(2,1)S(1)} custom-call(bf16[8,256,128]{2,1,0:T(8,128)(2,1)S(1)} %get-tuple-element.44.refs_0_, bf16[8,256,128]{2,1,0:T(8,128)(2,1)} %collective-permute-done.10.refs_1_, bf16[4,256,128]{2,1,0:T(8,128)(2,1)S(1)} %slice.8.refs_2_, bf16[4,256,128]{2,1,0:T(8,128)(2,1)S(1)} %slice.9.refs_3_, ...), custom_call_target="tpu_custom_call" | custom-call | tf_op jit(solution)/shard_map/pallas_call | solution.py:159
  67.1 2.5 %collective-permute-start.20 = (bf16[512,128]{1,0:T(8,128)(2,1)S(1)}, bf16[512,128]{1,0:T(8,128)(2,1)S(1)}, u32[]{:S(2)}, u32[]{:S(2)}) collective-permute-start(bf16[512,128]{1,0:T(8,128)(2,1)S(1)} %get-tuple-element.47), channel_id=1, source_target_pairs={{0,64},{64,128},{128,192},{192,0},{1,65},{65,129},{129,193},{193,1... | collective-permute-start | bytes 393224 | tf_op jit(solution)/shard_map/ppermute | solution.py:400
  70.3 2.0 %collective-permute-start.19 = (bf16[512,128]{1,0:T(8,128)(2,1)S(1)}, bf16[512,128]{1,0:T(8,128)(2,1)S(1)}, u32[]{:S(2)}, u32[]{:S(2)}) collective-permute-start(bf16[512,128]{1,0:T(8,128)(2,1)S(1)} %get-tuple-element.46), channel_id=1, source_target_pairs={{0,64},{64,128},{128,192},{192,0},{1,65},{65,129},{129,193},{193,1... | collective-permute-start | bytes 393224 | tf_op jit(solution)/shard_map/ppermute | solution.py:400
  73.4 1.3 collective-permute-start.22
  76.4 1.3 collective-permute-start.21
  77.7 2.9 %collective-permute-done.22.x_ref = bf16[512,128]{1,0:T(8,128)(2,1)S(1)} collective-permute-done((bf16[512,128]{1,0:T(8,128)(2,1)S(1)}, bf16[512,128]{1,0:T(8,128)(2,1)S(1)}, u32[]{:S(2)}, u32[]{:S(2)}) %collective-permute-start.22) | collective-permute-done | bytes 131104 | tf_op jit(solution)/shard_map/ppermute | solution.py:400
  81.4 1.3 collective-permute-start.24
  83.9 1.3 collective-permute-start.23
  85.2 5.2 %collective-permute-done.24.x_ref = bf16[512,128]{1,0:T(8,128)(2,1)S(1)} collective-permute-done((bf16[512,128]{1,0:T(8,128)(2,1)S(1)}, bf16[512,128]{1,0:T(8,128)(2,1)S(1)}, u32[]{:S(2)}, u32[]{:S(2)}) %collective-permute-start.24) | collective-permute-done | bytes 131104 | tf_op jit(solution)/shard_map/ppermute | solution.py:400
  90.4 2.6 %shard_map.75 = (bf16[512,128]{1,0:T(8,128)(2,1)S(1)}, bf16[16,128,128]{2,1,0:T(8,128)(2,1)S(1)}) custom-call(s32[2048]{0:T(1024)S(1)} %reshape.39.places, s32[4]{0:T(128)S(1)} %pad_add_fusion.1.info, bf16[512,128]{1,0:T(8,128)(2,1)S(1)} %collective-permute-done.24.x_ref, f32[1,128]{1,0:T(1,128)S(1)} %get-tuple-element.66.refs_0_, ...), custom_call_target="tpu_custom_call", output_to_operand_aliasing={{1}: (6, {})} | custom-call | flops 134217728 | bytes 262144 | tf_op jit(solution)/shard_map/pallas_call | solution.py:261
  93.0 1.3 collective-permute-start.26
  94.9 2.6 %shard_map.76 = (bf16[512,128]{1,0:T(8,128)(2,1)S(1)}, bf16[16,128,128]{2,1,0:T(8,128)(2,1)S(1)}) custom-call(s32[2048]{0:T(1024)S(1)} %reshape.39.places, s32[4]{0:T(128)S(1)} %pad_add_fusion.1.info, bf16[512,128]{1,0:T(8,128)(2,1)S(1)} %collective-permute-done.23.x_ref, f32[1,128]{1,0:T(1,128)S(1)} %get-tuple-element.66.refs_0_, ...), custom_call_target="tpu_custom_call", output_to_operand_aliasing={{1}: (6, {})} | custom-call | flops 134217728 | bytes 262144 | tf_op jit(solution)/shard_map/pallas_call | solution.py:261
  97.6 1.3 collective-permute-start.25
  99.9 3.3 %shard_map.77 = (bf16[512,128]{1,0:T(8,128)(2,1)}, bf16[16,128,128]{2,1,0:T(8,128)(2,1)S(1)}) custom-call(s32[2048]{0:T(1024)S(1)} %reshape.39.places, s32[4]{0:T(128)S(1)} %pad_add_fusion.1.info, bf16[512,128]{1,0:T(8,128)(2,1)S(1)} %collective-permute-done.26.x_ref, f32[1,128]{1,0:T(1,128)S(1)} %get-tuple-element.66.refs_0_, ...), custom_call_target="tpu_custom_call", output_to_operand_aliasing={{1}: (6, {})} | custom-call | flops 134217728 | bytes 262144 | tf_op jit(solution)/shard_map/pallas_call | solution.py:261
  103.2 1.3 collective-permute-done.25.x_ref
  104.4 3.3 %shard_map.78 = (bf16[512,128]{1,0:T(8,128)(2,1)}, bf16[16,128,128]{2,1,0:T(8,128)(2,1)S(1)}) custom-call(s32[2048]{0:T(1024)S(1)} %reshape.39.places, s32[4]{0:T(128)S(1)} %pad_add_fusion.1.info, bf16[512,128]{1,0:T(8,128)(2,1)S(1)} %collective-permute-done.25.x_ref, f32[1,128]{1,0:T(1,128)S(1)} %get-tuple-element.66.refs_0_, ...), custom_call_target="tpu_custom_call", output_to_operand_aliasing={{1}: (6, {})} | custom-call | flops 134217728 | bytes 262144 | tf_op jit(solution)/shard_map/pallas_call | solution.py:261
  107.7 25.5 %all_to_all.5.done = bf16[16,128,128]{2,1,0:T(8,128)(2,1)S(1)} all-to-all(bf16[16,128,128]{2,1,0:T(8,128)(2,1)S(1)} %get-tuple-element.62), channel_id=1, replica_groups={{0,6,8,14,16,22,24,30,32,38,40,46,48,54,56,62},{1,7,9,15,17,23,25,31,33..., dimensions={0} | all-to-all | bytes 1048576 | tf_op jit(solution)/shard_map/all_to_all | solution.py:406
  (61 shorter events, 17.3 us)
Async XLA Ops:
  0.0 40.4 %copy-start = (s32[1,16,512,16]{2,3,1,0:T(8,128)S(1)}, s32[1,16,512,16]{2,3,1,0:T(8,128)}, u32[]{:S(2)}) copy-start(s32[1,16,512,16]{2,3,1,0:T(8,128)} %param.8) | copy-start | bytes 1572868
  0.0 52.8 %copy-start.3 = (s32[1,16]{1,0:T(1,128)S(1)}, s32[1,16]{1,0:T(1,128)}, u32[]{:S(2)}) copy-start(s32[1,16]{1,0:T(1,128)} %param.9) | copy-start | bytes 196
  2.2 12.9 %collective-permute-start = (bf16[2,288,128]{2,1,0:T(8,128)(2,1)}, bf16[2,288,128]{2,1,0:T(8,128)(2,1)S(1)}, u32[]{:S(2)}, u32[]{:S(2)}) collective-permute-start(bf16[2,288,128]{2,1,0:T(8,128)(2,1)} %get-tuple-element.35), channel_id=1, source_target_pairs={{0,8},{1,9},{2,10},{3,11},{4,12},{5,13},{6,14},{7,15},{8,16},{9,17... | collective-permute-start | bytes 442376 | tf_op jit(solution)/shard_map/ppermute | solution.py:310
  4.2 15.4 %collective-permute-start.1 = (bf16[2,288,128]{2,1,0:T(8,128)(2,1)}, bf16[2,288,128]{2,1,0:T(8,128)(2,1)S(1)}, u32[]{:S(2)}, u32[]{:S(2)}) collective-permute-start(bf16[2,288,128]{2,1,0:T(8,128)(2,1)} %get-tuple-element.36), channel_id=1, source_target_pairs={{0,56},{1,57},{2,58},{3,59},{4,60},{5,61},{6,62},{7,63},{8,0},{9,1... | collective-permute-start | bytes 442376 | tf_op jit(solution)/shard_map/ppermute | solution.py:310
  8.2 15.8 %collective-permute-start.2 = (bf16[2,288,128]{2,1,0:T(8,128)(2,1)}, bf16[2,288,128]{2,1,0:T(8,128)(2,1)S(1)}, u32[]{:S(2)}, u32[]{:S(2)}) collective-permute-start(bf16[2,288,128]{2,1,0:T(8,128)(2,1)} %get-tuple-element.37), channel_id=1, source_target_pairs={{0,16},{1,17},{2,18},{3,19},{4,20},{5,21},{6,22},{7,23},{8,24},{9,... | collective-permute-start | bytes 442376 | tf_op jit(solution)/shard_map/ppermute | solution.py:310
  8.2 15.8 %collective-permute-start.3 = (bf16[2,288,128]{2,1,0:T(8,128)(2,1)}, bf16[2,288,128]{2,1,0:T(8,128)(2,1)S(1)}, u32[]{:S(2)}, u32[]{:S(2)}) collective-permute-start(bf16[2,288,128]{2,1,0:T(8,128)(2,1)} %get-tuple-element.38), channel_id=1, source_target_pairs={{0,48},{1,49},{2,50},{3,51},{4,52},{5,53},{6,54},{7,55},{8,56},{9,... | collective-permute-start | bytes 442376 | tf_op jit(solution)/shard_map/ppermute | solution.py:310
  14.5 18.4 %collective-permute-start.4 = (bf16[2,288,128]{2,1,0:T(8,128)(2,1)}, bf16[2,288,128]{2,1,0:T(8,128)(2,1)S(1)}, u32[]{:S(2)}, u32[]{:S(2)}) collective-permute-start(bf16[2,288,128]{2,1,0:T(8,128)(2,1)} %get-tuple-element.39), channel_id=1, source_target_pairs={{0,24},{1,25},{2,26},{3,27},{4,28},{5,29},{6,30},{7,31},{8,32},{9,... | collective-permute-start | bytes 442376 | tf_op jit(solution)/shard_map/ppermute | solution.py:310
  15.1 17.7 %collective-permute-start.5 = (bf16[2,288,128]{2,1,0:T(8,128)(2,1)}, bf16[2,288,128]{2,1,0:T(8,128)(2,1)S(1)}, u32[]{:S(2)}, u32[]{:S(2)}) collective-permute-start(bf16[2,288,128]{2,1,0:T(8,128)(2,1)} %get-tuple-element.40), channel_id=1, source_target_pairs={{0,40},{1,41},{2,42},{3,43},{4,44},{5,45},{6,46},{7,47},{8,48},{9,... | collective-permute-start | bytes 442376 | tf_op jit(solution)/shard_map/ppermute | solution.py:310
  19.6 13.3 %collective-permute-start.6 = (bf16[2,288,128]{2,1,0:T(8,128)(2,1)}, bf16[2,288,128]{2,1,0:T(8,128)(2,1)S(1)}, u32[]{:S(2)}, u32[]{:S(2)}) collective-permute-start(bf16[2,288,128]{2,1,0:T(8,128)(2,1)} %get-tuple-element.41), channel_id=1, source_target_pairs={{0,32},{1,33},{2,34},{3,35},{4,36},{5,37},{6,38},{7,39},{8,40},{9,... | collective-permute-start | bytes 442376 | tf_op jit(solution)/shard_map/ppermute | solution.py:310
  32.9 0.9 copy-start.1
  35.5 17.9 %collective-permute-start.10 = (bf16[8,256,128]{2,1,0:T(8,128)(2,1)S(1)}, bf16[8,256,128]{2,1,0:T(8,128)(2,1)}, u32[]{:S(2)}, u32[]{:S(2)}) collective-permute-start(bf16[8,256,128]{2,1,0:T(8,128)(2,1)S(1)} %get-tuple-element.44.refs_0_), channel_id=1, source_target_pairs={{0,2},{1,3},{2,0},{3,1},{4,6},{5,7},{6,4},{7,5},{8,10},{9,11},{10,... | collective-permute-start | bytes 1572872 | tf_op jit(solution)/shard_map/ppermute | solution.py:310
  37.2 11.2 %collective-permute-start.7 = (bf16[4,288,128]{2,1,0:T(8,128)(2,1)S(1)}, bf16[4,288,128]{2,1,0:T(8,128)(2,1)S(1)}, u32[]{:S(2)}, u32[]{:S(2)}) collective-permute-start(bf16[4,288,128]{2,1,0:T(8,128)(2,1)S(1)} %get-tuple-element.42), channel_id=1, source_target_pairs={{0,6},{1,7},{2,4},{3,5},{4,2},{5,3},{6,0},{7,1},{8,14},{9,15},{10,... | collective-permute-start | bytes 884744 | tf_op jit(solution)/shard_map/ppermute | solution.py:310
  39.4 13.3 %collective-permute-start.8 = (bf16[4,288,128]{2,1,0:T(8,128)(2,1)}, bf16[4,288,128]{2,1,0:T(8,128)(2,1)S(1)}, u32[]{:S(2)}, u32[]{:S(2)}) collective-permute-start(bf16[4,288,128]{2,1,0:T(8,128)(2,1)} %get-tuple-element.43), channel_id=1, source_target_pairs={{0,6},{1,7},{2,4},{3,5},{4,2},{5,3},{6,0},{7,1},{8,14},{9,15},{10,... | collective-permute-start | bytes 884744 | tf_op jit(solution)/shard_map/ppermute | solution.py:310
  40.6 15.2 %collective-permute-start.13 = (bf16[8,256,128]{2,1,0:T(8,128)(2,1)S(1)}, bf16[8,256,128]{2,1,0:T(8,128)(2,1)}, u32[]{:S(2)}, u32[]{:S(2)}) collective-permute-start(bf16[8,256,128]{2,1,0:T(8,128)(2,1)S(1)} %get-tuple-element.44.refs_0_), channel_id=1, source_target_pairs={{0,1},{1,0},{2,3},{3,2},{4,5},{5,4},{6,7},{7,6},{8,9},{9,8},{10,11... | collective-permute-start | bytes 1572872 | tf_op jit(solution)/shard_map/ppermute | solution.py:310
  48.4 8.0 %collective-permute-start.15 = (bf16[4,256,128]{2,1,0:T(8,128)(2,1)S(1)}, bf16[4,256,128]{2,1,0:T(8,128)(2,1)}, u32[]{:S(2)}, u32[]{:S(2)}) collective-permute-start(bf16[4,256,128]{2,1,0:T(8,128)(2,1)S(1)} %slice.8.refs_2_), channel_id=1, source_target_pairs={{0,1},{1,0},{2,3},{3,2},{4,5},{5,4},{6,7},{7,6},{8,9},{9,8},{10,11... | collective-permute-start | bytes 786440 | tf_op jit(solution)/shard_map/ppermute | solution.py:310
  48.5 9.3 %collective-permute-start.11 = (bf16[4,256,128]{2,1,0:T(8,128)(2,1)S(1)}, bf16[4,256,128]{2,1,0:T(8,128)(2,1)}, u32[]{:S(2)}, u32[]{:S(2)}) collective-permute-start(bf16[4,256,128]{2,1,0:T(8,128)(2,1)S(1)} %slice.8.refs_2_), channel_id=1, source_target_pairs={{0,2},{1,3},{2,0},{3,1},{4,6},{5,7},{6,4},{7,5},{8,10},{9,11},{10,... | collective-permute-start | bytes 786440 | tf_op jit(solution)/shard_map/ppermute | solution.py:310
  52.7 10.2 %collective-permute-start.12 = (bf16[4,256,128]{2,1,0:T(8,128)(2,1)S(1)}, bf16[4,256,128]{2,1,0:T(8,128)(2,1)}, u32[]{:S(2)}, u32[]{:S(2)}) collective-permute-start(bf16[4,256,128]{2,1,0:T(8,128)(2,1)S(1)} %slice.9.refs_3_), channel_id=1, source_target_pairs={{0,2},{1,3},{2,0},{3,1},{4,6},{5,7},{6,4},{7,5},{8,10},{9,11},{10,... | collective-permute-start | bytes 786440 | tf_op jit(solution)/shard_map/ppermute | solution.py:310
  53.4 11.3 %collective-permute-start.14 = (bf16[8,256,128]{2,1,0:T(8,128)(2,1)}, bf16[8,256,128]{2,1,0:T(8,128)(2,1)}, u32[]{:S(2)}, u32[]{:S(2)}) collective-permute-start(bf16[8,256,128]{2,1,0:T(8,128)(2,1)} %collective-permute-done.10.refs_1_), channel_id=1, source_target_pairs={{0,1},{1,0},{2,3},{3,2},{4,5},{5,4},{6,7},{7,6},{8,9},{9,8},{10,11... | collective-permute-start | bytes 1572872 | tf_op jit(solution)/shard_map/ppermute | solution.py:310
  54.2 0.9 copy-start.2
  55.7 8.4 %collective-permute-start.16 = (bf16[4,256,128]{2,1,0:T(8,128)(2,1)S(1)}, bf16[4,256,128]{2,1,0:T(8,128)(2,1)S(1)}, u32[]{:S(2)}, u32[]{:S(2)}) collective-permute-start(bf16[4,256,128]{2,1,0:T(8,128)(2,1)S(1)} %slice.9.refs_3_), channel_id=1, source_target_pairs={{0,1},{1,0},{2,3},{3,2},{4,5},{5,4},{6,7},{7,6},{8,9},{9,8},{10,11... | collective-permute-start | bytes 786440 | tf_op jit(solution)/shard_map/ppermute | solution.py:310
  56.3 13.3 %collective-permute-start.9 = (bf16[512,128]{1,0:T(8,128)(2,1)S(1)}, bf16[512,128]{1,0:T(8,128)(2,1)S(1)}, u32[]{:S(2)}, u32[]{:S(2)}) collective-permute-start(bf16[512,128]{1,0:T(8,128)(2,1)S(1)} %shard_map.67.x_ref), channel_id=1, source_target_pairs={{64,0},{128,192},{65,1},{129,193},{66,2},{130,194},{67,3},{131,195... | collective-permute-start | bytes 393224 | tf_op jit(solution)/shard_map/ppermute | solution.py:357
  57.8 6.3 %collective-permute-start.17 = (bf16[4,256,128]{2,1,0:T(8,128)(2,1)}, bf16[4,256,128]{2,1,0:T(8,128)(2,1)S(1)}, u32[]{:S(2)}, u32[]{:S(2)}) collective-permute-start(bf16[4,256,128]{2,1,0:T(8,128)(2,1)} %collective-permute-done.11.refs_4_), channel_id=1, source_target_pairs={{0,1},{1,0},{2,3},{3,2},{4,5},{5,4},{6,7},{7,6},{8,9},{9,8},{10,11... | collective-permute-start | bytes 786440 | tf_op jit(solution)/shard_map/ppermute | solution.py:310
  62.9 1.7 %collective-permute-start.18 = (bf16[4,256,128]{2,1,0:T(8,128)(2,1)}, bf16[4,256,128]{2,1,0:T(8,128)(2,1)S(1)}, u32[]{:S(2)}, u32[]{:S(2)}) collective-permute-start(bf16[4,256,128]{2,1,0:T(8,128)(2,1)} %collective-permute-done.12.refs_5_), channel_id=1, source_target_pairs={{0,1},{1,0},{2,3},{3,2},{4,5},{5,4},{6,7},{7,6},{8,9},{9,8},{10,11... | collective-permute-start | bytes 786440 | tf_op jit(solution)/shard_map/ppermute | solution.py:310
  67.1 5.6 %collective-permute-start.20 = (bf16[512,128]{1,0:T(8,128)(2,1)S(1)}, bf16[512,128]{1,0:T(8,128)(2,1)S(1)}, u32[]{:S(2)}, u32[]{:S(2)}) collective-permute-start(bf16[512,128]{1,0:T(8,128)(2,1)S(1)} %get-tuple-element.47), channel_id=1, source_target_pairs={{0,64},{64,128},{128,192},{192,0},{1,65},{65,129},{129,193},{193,1... | collective-permute-start | bytes 393224 | tf_op jit(solution)/shard_map/ppermute | solution.py:400
  70.3 5.3 %collective-permute-start.19 = (bf16[512,128]{1,0:T(8,128)(2,1)S(1)}, bf16[512,128]{1,0:T(8,128)(2,1)S(1)}, u32[]{:S(2)}, u32[]{:S(2)}) collective-permute-start(bf16[512,128]{1,0:T(8,128)(2,1)S(1)} %get-tuple-element.46), channel_id=1, source_target_pairs={{0,64},{64,128},{128,192},{192,0},{1,65},{65,129},{129,193},{193,1... | collective-permute-start | bytes 393224 | tf_op jit(solution)/shard_map/ppermute | solution.py:400
  73.4 7.1 %collective-permute-start.22 = (bf16[512,128]{1,0:T(8,128)(2,1)S(1)}, bf16[512,128]{1,0:T(8,128)(2,1)S(1)}, u32[]{:S(2)}, u32[]{:S(2)}) collective-permute-start(bf16[512,128]{1,0:T(8,128)(2,1)S(1)} %get-tuple-element.51), channel_id=1, source_target_pairs={{0,64},{64,128},{128,192},{1,65},{65,129},{129,193},{2,66},{66,130... | collective-permute-start | bytes 393224 | tf_op jit(solution)/shard_map/ppermute | solution.py:400
  76.4 6.9 %collective-permute-start.21 = (bf16[512,128]{1,0:T(8,128)(2,1)S(1)}, bf16[512,128]{1,0:T(8,128)(2,1)S(1)}, u32[]{:S(2)}, u32[]{:S(2)}) collective-permute-start(bf16[512,128]{1,0:T(8,128)(2,1)S(1)} %get-tuple-element.50), channel_id=1, source_target_pairs={{0,64},{64,128},{128,192},{1,65},{65,129},{129,193},{2,66},{66,130... | collective-permute-start | bytes 393224 | tf_op jit(solution)/shard_map/ppermute | solution.py:400
  81.4 8.9 %collective-permute-start.24 = (bf16[512,128]{1,0:T(8,128)(2,1)S(1)}, bf16[512,128]{1,0:T(8,128)(2,1)S(1)}, u32[]{:S(2)}, u32[]{:S(2)}) collective-permute-start(bf16[512,128]{1,0:T(8,128)(2,1)S(1)} %get-tuple-element.55), channel_id=1, source_target_pairs={{0,64},{64,128},{128,192},{1,65},{65,129},{129,193},{2,66},{66,130... | collective-permute-start | bytes 393224 | tf_op jit(solution)/shard_map/ppermute | solution.py:400
  83.9 11.0 %collective-permute-start.23 = (bf16[512,128]{1,0:T(8,128)(2,1)S(1)}, bf16[512,128]{1,0:T(8,128)(2,1)S(1)}, u32[]{:S(2)}, u32[]{:S(2)}) collective-permute-start(bf16[512,128]{1,0:T(8,128)(2,1)S(1)} %get-tuple-element.54), channel_id=1, source_target_pairs={{0,64},{64,128},{128,192},{1,65},{65,129},{129,193},{2,66},{66,130... | collective-permute-start | bytes 393224 | tf_op jit(solution)/shard_map/ppermute | solution.py:400
  93.0 6.9 %collective-permute-start.26 = (bf16[512,128]{1,0:T(8,128)(2,1)S(1)}, bf16[512,128]{1,0:T(8,128)(2,1)S(1)}, u32[]{:S(2)}, u32[]{:S(2)}) collective-permute-start(bf16[512,128]{1,0:T(8,128)(2,1)S(1)} %get-tuple-element.59), channel_id=1, source_target_pairs={{0,64},{64,128},{128,192},{1,65},{65,129},{129,193},{2,66},{66,130... | collective-permute-start | bytes 393224 | tf_op jit(solution)/shard_map/ppermute | solution.py:400
  97.6 6.9 %collective-permute-start.25 = (bf16[512,128]{1,0:T(8,128)(2,1)S(1)}, bf16[512,128]{1,0:T(8,128)(2,1)S(1)}, u32[]{:S(2)}, u32[]{:S(2)}) collective-permute-start(bf16[512,128]{1,0:T(8,128)(2,1)S(1)} %get-tuple-element.58), channel_id=1, source_target_pairs={{0,64},{64,128},{128,192},{1,65},{65,129},{129,193},{2,66},{66,130... | collective-permute-start | bytes 393224 | tf_op jit(solution)/shard_map/ppermute | solution.py:400
